TPU v7x, 256 devices: a whole 4x4x8 slice. The times are simulated.
256 devices in a mesh: vocab: 32 (over y, z), rows: 8 (over x, core).
Axes of the slice: x: 4, y: 4, z: 8, core: 2. Of those that a mesh axis runs over, the one named last changes fastest.
Arguments:
- hidden_states: bfloat16 [512, 5120], P(('vocab', 'rows')), may hold values from -1000 to 1000
- head_weight: bfloat16 [151552, 5120], P(('vocab', 'rows')), may hold values from -2 to 2
- teacher_ids: int32 [512, 64], P(('vocab', 'rows')), may hold values from 0 to 151551
- teacher_probs: float32 [512, 64], P(('vocab', 'rows')), may hold values from 0.001 to 0.015
- row_weight: float32 [512], P(('vocab', 'rows')), may hold values from 16 to 160
Outputs:
- grad_hidden: bfloat16 [512, 5120], P(('vocab', 'rows'))
- grad_weight: bfloat16 [151552, 5120], P(('vocab', 'rows'))
All inputs are finite; a program needn't handle non-finite values.
Results may differ from a plain program's by a relative error of at most 0.012.
Values may be sent and summed in bfloat16 or wider, within the bound.
No kernel may reach another device: no remote copies, remote signals or barrier semaphores. Data moves between devices by JAX's collectives and lax.ppermute only.
A program may use at most 128 MiB of HBM per device.

v0:
```python
import math

import jax
import jax.numpy as jnp
from jax import lax
from jax.sharding import PartitionSpec as P


def dense_target(local_column, probs_all, entries):
    all_rows = local_column.shape[0]
    width = local_column.shape[1]
    block = math.gcd(all_rows, 64)
    columns = jnp.arange(entries, dtype=jnp.int32)
    id_blocks = local_column.reshape(all_rows // block, block, width)
    prob_blocks = probs_all.reshape(all_rows // block, block, width)

    def one_block(pair):
        id_block, prob_block = pair
        matches = id_block[:, :, None] == columns[None, None, :]
        return jnp.sum(jnp.where(matches, prob_block[:, :, None], jnp.float32(0.0)), axis=1)

    stacked = lax.map(one_block, (id_blocks, prob_blocks))
    return stacked.reshape(all_rows, entries)


def per_device(hidden_states, head_weight, teacher_ids, teacher_probs, row_weight):
    gathered = lax.all_gather(hidden_states, ("vocab", "rows"), axis=0, tiled=True)
    ids_all = lax.all_gather(teacher_ids, ("vocab", "rows"), axis=0, tiled=True)
    probs_all, weight_all = (
        lax.all_gather(teacher_probs, ("vocab", "rows"), axis=0, tiled=True),
        lax.all_gather(row_weight, ("vocab", "rows"), axis=0, tiled=True),
    )
    logits = jnp.einsum("rd,vd->rv", gathered, head_weight, preferred_element_type=jnp.float32)
    local_top = jnp.max(logits, axis=1)
    row_top = lax.pmax(local_top, ("vocab", "rows"))
    exponent = jnp.exp(logits - row_top[:, None])
    row_total = lax.psum(jnp.sum(exponent, axis=1), ("vocab", "rows"))
    entries = head_weight.shape[0]
    first_entry = lax.axis_index(("vocab", "rows")) * entries
    local_column = ids_all - first_entry
    target = dense_target(local_column, probs_all, entries)
    teacher_mass = jnp.sum(probs_all, axis=1, keepdims=True)
    grad_logits = (
        weight_all[:, None] * (teacher_mass * exponent / row_total[:, None] - target)
    ).astype(jnp.bfloat16)
    grad_weight = jnp.einsum(
        "rv,rd->vd", grad_logits, gathered, preferred_element_type=jnp.float32
    ).astype(jnp.bfloat16)
    summed = lax.psum_scatter(
        jnp.dot(grad_logits, head_weight, preferred_element_type=jnp.float32),
        ("vocab", "rows"),
        scatter_dimension=0,
        tiled=True,
    )
    return (summed.astype(jnp.bfloat16), grad_weight)


def solution(mesh):
    in_specs = (
        P(("vocab", "rows"), None),
        P(("vocab", "rows"), None),
        P(("vocab", "rows"), None),
        P(("vocab", "rows"), None),
        P(("vocab", "rows")),
    )
    out_specs = (P(("vocab", "rows"), None), P(("vocab", "rows"), None))
    return jax.shard_map(
        per_device, mesh=mesh, in_specs=in_specs, out_specs=out_specs, check_vma=False
    )
```

profile of v0, /device:TPU:24, one launch (start us, length us, event | category | flops | bytes accessed | tf_op | source)
XLA Modules:
  0.0 489.4 jit_solution(9331202431830911476)
XLA Ops:
  7.2 0.7 all-gather.5.cloned.1.call-update
  7.9 64.9 %all-gather.2 = s32[256,2,64]{2,1,0:T(2,128)S(1)} all-gather(s32[1,2,64]{2,1,0:T(2,128)} %bitcast.34), channel_id=1, replica_groups=mesh['vocab'=32,'rows'=8] {'vocab','rows'}, dimensions={0}, use_global_device_ids=true | all-gather | bytes 131584 | tf_op jit(solution)/shard_map/all_gather | solution.py:28
  72.8 59.5 %all-gather = f32[256,2,64]{2,1,0:T(2,128)S(1)} all-gather(f32[1,2,64]{2,1,0:T(2,128)} %bitcast.35), channel_id=1, replica_groups=mesh['vocab'=32,'rows'=8] {'vocab','rows'}, dimensions={0}, use_global_device_ids=true | all-gather | bytes 131584 | tf_op jit(solution)/shard_map/all_gather | solution.py:30
  132.3 19.7 %while.11 = (s32[]{:T(128)}, f32[8,64,592]{2,1,0:T(8,128)S(1)}, s32[8,64,64]{2,1,0:T(8,128)S(1)}, f32[8,64,64]{2,1,0:T(8,128)S(1)}, s32[]{:T(128)}) while((s32[]{:T(128)}, f32[8,64,592]{2,1,0:T(8,128)S(1)}, s32[8,64,64]{2,1,0:T(8,128)S(1)}, f32[8,64,64]{2,1,0:T(8,128)S(1)}, s32[]{:T(128)}) %tuple.32), condition=%wide.region_7.8_spmd.clone, body=%wide.region_5.7_spmd.clone.sunk | while | flops 7236610 | bytes 577617 | solution.py:22
  132.4 2.4 select_reduce_fusion.2
  134.9 2.4 select_reduce_fusion.2
  137.3 2.4 select_reduce_fusion.2
  139.8 2.4 select_reduce_fusion.2
  142.3 2.4 select_reduce_fusion.2
  144.7 2.4 select_reduce_fusion.2
  147.2 2.4 select_reduce_fusion.2
  149.7 2.4 select_reduce_fusion.2
  152.1 0.4 copy.10
  152.5 0.3 reduce
  153.0 0.2 dynamic-update-slice
  153.2 11.4 %reshape.30 = bf16[512,5120]{1,0:T(8,128)(2,1)} reshape(bf16[256,2,5120]{2,1,0:T(2,128)(2,1)} %all-gather.5.cloned.1.call-done) | data formatting | bytes 10485760
  164.6 7.0 %fusion.3 = (f32[512]{0:T(512)S(1)}, f32[512,592]{0,1:T(8,128)S(1)}) fusion(bf16[512,5120]{1,0:T(8,128)(2,1)} %reshape.30, bf16[592,5120]{1,0:T(8,128)(2,1)} %param.8), kind=kOutput, calls=%fused_computation.12 | convolution fusion | flops 3104087552 | bytes 12519424 | tf_op jit(solution)/shard_map/rd,vd->rv/dot_general | solution.py:33
  171.6 74.0 %pmax.7 = f32[512]{0:T(512)S(1)} all-reduce(f32[512]{0:T(512)S(1)} %get-tuple-element.50), channel_id=1, replica_groups=mesh['vocab'=32,'rows'=8] {'vocab','rows'}, use_global_device_ids=true, to_apply=%region_2.0 | all-reduce | flops 512 | bytes 4096 | tf_op jit(solution)/shard_map/pmax | solution.py:35
  245.8 74.1 %all-reduce.2 = (f32[512]{0:T(512)S(1)}, f32[512]{0:T(512)S(1)}) all-reduce(f32[512]{0:T(512)S(1)} %fusion.2, f32[512]{0:T(512)S(1)} %dynamic-update-slice), channel_id=1, replica_groups=mesh['vocab'=32,'rows'=8] {'vocab','rows'}, use_global_device_ids=true, to_apply=%region_4.5 | all-reduce | flops 1024 | bytes 8192 | tf_op jit(solution)/shard_map/psum | solution.py:37
  319.9 0.3 multiply_convert_fusion
  320.3 9.8 %fusion.4 = f32[512,5120]{1,0:T(8,128)} fusion(bf16[512,592]{0,1:T(8,128)(2,1)S(1)} %multiply_convert_fusion, bf16[592,5120]{1,0:T(8,128)(2,1)} %param.8), kind=kOutput, calls=%fused_computation.13 | convolution fusion | flops 3103784960 | bytes 17154048 | tf_op jit(solution)/shard_map/dot_general | solution.py:50
  330.0 5.1 %convolution_convert_fusion = bf16[592,5120]{1,0:T(8,128)(2,1)} fusion(bf16[512,592]{0,1:T(8,128)(2,1)S(1)} %multiply_convert_fusion, bf16[512,5120]{1,0:T(8,128)(2,1)S(1)} %bitcast.27), kind=kOutput, calls=%fused_computation.6 | convolution fusion | flops 3106816000 | bytes 11911168 | tf_op jit(solution)/shard_map/rv,rd->vd/dot_general | solution.py:46
  335.2 145.8 %all-reduce.4 = bf16[512,5120]{1,0:T(8,128)(2,1)} all-reduce(f32[512,5120]{1,0:T(8,128)} %fusion.4), channel_id=2, replica_groups=mesh['vocab'=32,'rows'=8] {'vocab','rows'}, use_global_device_ids=true, to_apply=%region_8.9.clone | all-reduce | flops 2621440 | bytes 15728640
  481.0 1.5 dynamic-slice_convert_fusion
  (38 shorter events, 0.7 us)
Async XLA Ops:
  7.2 145.8 %copy-start = (f32[2]{0:T(128)S(1)}, f32[2]{0:T(128)}, u32[]{:S(2)}) copy-start(f32[2]{0:T(128)} %param.11) | copy-start | bytes 28
  7.2 146.1 %all-gather.5.cloned.1.call-start = ((), (), s32[]{:S(2)}) async-start(), calls=%async_computation | async-start | bytes 5263360 | tf_op jit(solution)/shard_map/all_gather | solution.py:27
  319.9 10.1 %slice-start = ((s8[5242880]{0:T(1024)(128)(4,1)}), s8[4194304]{0:T(1024)(128)(4,1)S(1)}, s32[]{:S(2)}) async-start(s8[5242880]{0:T(1024)(128)(4,1)} %bitcast.26), calls=%async_computation.1 | async-start | bytes 8388608
  320.2 9.8 %slice-start.1 = ((s8[5242880]{0:T(1024)(128)(4,1)}), s8[1048576]{0:T(1024)(128)(4,1)S(1)}, s32[]{:S(2)}) async-start(s8[5242880]{0:T(1024)(128)(4,1)} %bitcast.26), calls=%async_computation.2 | async-start | bytes 2097152
Sparse Core Ops, SparseCore 0:
  11.6 118.3 all-gather.4
where the time goes:
time: 492 us; the launch traced here: 489 us
  blocking collectives  418 us (85%)
  matrix products  21.9 us (4%)
  other arithmetic  20 us (4%)
  between operations  14.1 us (3%)
  local copies, waits for them, and re-layouts  14 us (3%)
    unnamed x1, blocking collectives  146 us
    psum x1, blocking collectives, per_device(): row_total = lax.psum(jnp.sum(exponent, axis=1), ('vocab', 'rows'))  74.1 us
    pmax x1, blocking collectives, per_device(): row_top = lax.pmax(local_top, ('vocab', 'rows'))  74 us
    all_gather x1, blocking collectives, per_device(): ids_all = lax.all_gather(teacher_ids, ('vocab', 'rows'), axis=0, tiled=True)  64.9 us
    all_gather x1, blocking collectives, per_device(): lax.all_gather(teacher_probs, ('vocab', 'rows'), axis=0, tiled=True)  59.5 us
    reduce_sum x8, other arithmetic, one_block(): jnp.sum(jnp.where(matches, prob_block[:, :, None], jnp.float32(0.0)), axi...  19 us
    unnamed x9, local copies, waits for them, and re-layouts  11.6 us
  transfers between devices with their start and end apart: 1, of which 0 were waited for; matrix products, arithmetic and copies ran while one was open for 4% of the time, Pallas kernels for 0%

commit v1 on v0

v1 whole, which is shorter than its diff:
```python
import jax
import jax.numpy as jnp
from jax import lax
from jax.sharding import Mesh, PartitionSpec as P

AXES = ("y", "z", "x", "core")
SWAP = [(0, 1), (1, 0)]
DIGIT = 512
HALF = 256
ID_SHIFT = 148


def split_bf16(value, pieces):
    parts = []
    for _ in range(pieces):
        part = value.astype(jnp.bfloat16)
        parts.append(part)
        value = value - part.astype(jnp.float32)
    return parts


def spread(block, axes, count):
    copies = jnp.broadcast_to(block[None], (count,) + block.shape)
    return lax.all_to_all(copies, axes, 0, 0, tiled=True)


def dense_target(local_ids, weighted_probs, entries):
    columns = jnp.arange(entries, dtype=jnp.int32)
    matches = local_ids.T[:, None, :] == columns[None, :, None]
    return jnp.sum(jnp.where(matches, weighted_probs.T[:, None, :], jnp.float32(0.0)), axis=0)


def per_device(sizes, hidden_states, head_weight, teacher_ids, teacher_probs, row_weight):
    size_y, size_z, size_x, _ = sizes
    own_rows, width = hidden_states.shape
    entries = head_weight.shape[0]
    kept = teacher_ids.shape[1]
    other_weight = lax.ppermute(head_weight, "core", SWAP)

    with jax.named_scope("pack"):
        mass = row_weight * jnp.sum(teacher_probs, axis=1)
        weighted = row_weight[:, None] * teacher_probs
        high = teacher_ids // DIGIT - ID_SHIFT
        low = teacher_ids % DIGIT - HALF
        extra = [high.astype(jnp.bfloat16), low.astype(jnp.bfloat16)]
        extra += split_bf16(weighted, 2)
        extra += split_bf16(mass[:, None], 3)
        used = sum(piece.shape[1] for piece in extra)
        padding = -used % 128
        extra.append(jnp.zeros((own_rows, padding), jnp.bfloat16))
        packed = jnp.concatenate([hidden_states] + extra, axis=1)

    with jax.named_scope("gather"):
        across_z = spread(packed, "z", size_z).reshape(size_z * own_rows, -1)
        gathered = spread(across_z, ("y", "x"), size_y * size_x)
        rows = size_y * size_x * size_z * own_rows
        gathered = gathered.reshape(rows, -1)

    hidden = gathered[:, :width]
    with jax.named_scope("unpack"):
        tail = gathered[:, width:].astype(jnp.float32)
        high = tail[:, :kept].astype(jnp.int32) + ID_SHIFT
        low = tail[:, kept : 2 * kept].astype(jnp.int32) + HALF
        ids = high * DIGIT + low
        weighted = tail[:, 2 * kept : 3 * kept] + tail[:, 3 * kept : 4 * kept]
        mass = tail[:, 4 * kept] + tail[:, 4 * kept + 1] + tail[:, 4 * kept + 2]

    device = lax.axis_index(AXES)
    core = lax.axis_index("core")
    first = device * entries
    other_first = (device + 1 - 2 * core) * entries
    with jax.named_scope("target"):
        target = dense_target(ids - first, weighted, entries)
        other_target = dense_target(ids - other_first, weighted, entries)

    with jax.named_scope("logits"):
        logits = jnp.einsum("vd,rd->vr", head_weight, hidden, preferred_element_type=jnp.float32)
        other_logits = jnp.einsum(
            "vd,rd->vr", other_weight, hidden, preferred_element_type=jnp.float32
        )
        top = jnp.maximum(jnp.max(logits, axis=0), jnp.max(other_logits, axis=0))
        exponent = jnp.exp(logits - top[None])
        other_exponent = jnp.exp(other_logits - top[None])
        total = jnp.sum(exponent, axis=0) + jnp.sum(other_exponent, axis=0)

    with jax.named_scope("stats"):
        stats = spread(jnp.stack([top, total]), ("y", "z", "x"), size_y * size_z * size_x)
        stats = stats.reshape(-1, 2, rows)
        row_top = jnp.max(stats[:, 0], axis=0)
        row_total = jnp.sum(stats[:, 1] * jnp.exp(stats[:, 0] - row_top[None]), axis=0)
        scale = mass * jnp.exp(top - row_top) / row_total

    with jax.named_scope("grads"):
        grad = (exponent * scale[None] - target).astype(jnp.bfloat16)
        other_grad = (other_exponent * scale[None] - other_target).astype(jnp.bfloat16)
        other_part = jnp.dot(other_grad, hidden, preferred_element_type=jnp.float32)
        returned = lax.ppermute(other_part.astype(jnp.bfloat16), "core", SWAP)
        partial = jnp.einsum(
            "vr,vd->rd", grad, head_weight, preferred_element_type=jnp.float32
        ) + jnp.einsum("vr,vd->rd", other_grad, other_weight, preferred_element_type=jnp.float32)
        partial = partial.astype(jnp.bfloat16)

    with jax.named_scope("scatter"):
        pieces = partial.reshape(size_y * size_x, size_z * own_rows, width)
        pieces = lax.all_to_all(pieces, ("y", "x"), 0, 0, tiled=True)
        summed = jnp.sum(pieces.astype(jnp.float32), axis=0).astype(jnp.bfloat16)
        pieces = summed.reshape(size_z, own_rows, width)
        pieces = lax.all_to_all(pieces, "z", 0, 0, tiled=True)
        grad_hidden = jnp.sum(pieces.astype(jnp.float32), axis=0).astype(jnp.bfloat16)

    with jax.named_scope("grad_weight"):
        own_part = jnp.dot(grad, hidden, preferred_element_type=jnp.float32)
        grad_weight = (own_part + returned.astype(jnp.float32)).astype(jnp.bfloat16)
    return grad_hidden, grad_weight


def solution(mesh):
    sizes = (4, 8, 4, 2)
    grid = Mesh(mesh.devices.reshape(sizes), AXES)
    in_specs = (P(AXES, None), P(AXES, None), P(AXES, None), P(AXES, None), P(AXES))
    out_specs = (P(AXES, None), P(AXES, None))

    def body(*args):
        return per_device(sizes, *args)

    return jax.shard_map(
        body, mesh=grid, in_specs=in_specs, out_specs=out_specs, check_vma=False
    )
```

time: 492 us -> 188 us (0.38)
  blocking collectives: 418 us -> 74.4 us
  waiting for transfers between devices: 0.68 us -> 39.2 us
  starting transfers between devices: 0.04 us -> 14.9 us
  between operations: 14.1 us -> 0.82 us
  local copies, waits for them, and re-layouts: 14 us -> 6.01 us
  matrix products: 21.9 us -> 27.9 us
    unnamed x1 -> x0, blocking collectives: 146 us -> none
    all_gather x2 -> x0, blocking collectives: 124 us -> none  [the longest x1 64.9 us: per_device(): ids_all = lax.all_gather(teacher_ids, ('vocab', 'rows'), axis=0, tiled=True)]
    all_to_all x0 -> x3, blocking collectives: none -> 74.4 us  [the longest x1 39.5 us: per_device(): pieces = lax.all_to_all(pieces, ('y', 'x'), 0, 0, tiled=True)]
    psum x1 -> x0, blocking collectives: 74.1 us -> none  [per_device(): row_total = lax.psum(jnp.sum(exponent, axis=1), ('vocab', 'rows'))]
    pmax x1 -> x0, blocking collectives: 74 us -> none  [per_device(): row_top = lax.pmax(local_top, ('vocab', 'rows'))]
    all_to_all x0 -> x2, waiting for transfers between devices: none -> 39.2 us  [spread(): return lax.all_to_all(copies, axes, 0, 0, tiled=True)]
    all_to_all x0 -> x2, starting transfers between devices: none -> 14.8 us  [spread(): return lax.all_to_all(copies, axes, 0, 0, tiled=True)]
    unnamed x9 -> x8, local copies, waits for them, and re-layouts: 11.6 us -> 0.63 us
  transfers between devices with their start and end apart: 1 -> 4, of which waited for: 0 -> 1; matrix products, arithmetic and copies ran while one was open for 4% -> 20% of each run, Pallas kernels for 0% -> 0%
where the time goes in v1:
time: 188 us; the launch traced here: 186 us
  blocking collectives  74.4 us (40%)
  waiting for transfers between devices  39.2 us (21%)
  matrix products  27.9 us (15%)
  other arithmetic  22.8 us (12%)
  starting transfers between devices  14.9 us (8%)
  local copies, waits for them, and re-layouts  6.01 us (3%)
    all_to_all x1, blocking collectives, per_device(): pieces = lax.all_to_all(pieces, ('y', 'x'), 0, 0, tiled=True)  39.5 us
    all_to_all x2, waiting for transfers between devices, spread(): return lax.all_to_all(copies, axes, 0, 0, tiled=True)  39.2 us
    all_to_all x1, blocking collectives, spread(): return lax.all_to_all(copies, axes, 0, 0, tiled=True)  19 us
    all_to_all x1, blocking collectives, per_device(): pieces = lax.all_to_all(pieces, 'z', 0, 0, tiled=True)  16 us
    all_to_all x2, starting transfers between devices, spread(): return lax.all_to_all(copies, axes, 0, 0, tiled=True)  14.8 us
    reduce_sum x1, other arithmetic, dense_target(): jnp.sum(jnp.where(matches, weighted_probs.T[:, None, :], jnp.float32(0.0)...  14.7 us
    dot_general x1, matrix products, per_device(): own_part = jnp.dot(grad, hidden, preferred_element_type=jnp.float32)  7.09 us
    dot_general x1, matrix products, per_device(): jnp.einsum('vr,vd->rd', other_grad, other_weight, preferred_element_type=...  4.96 us
  transfers between devices with their start and end apart: 4, of which 1 were waited for; matrix products, arithmetic and copies ran while one was open for 20% of the time, Pallas kernels for 0%

profile of v1, /device:TPU:24, one launch (start us, length us, event | category | flops | bytes accessed | tf_op | source)
XLA Modules:
  0.0 186.1 jit_solution(5937069788703784208)
XLA Ops:
  0.7 0.9 subtract_convert_fusion
  1.6 0.7 convert_bitcast_fusion
  2.6 0.7 fusion.25
  3.3 0.8 concatenate.3
  4.2 19.0 %all_to_all.25 = bf16[8,2,5504]{2,1,0:T(2,128)(2,1)S(1)} all-to-all(bf16[8,2,5504]{2,1,0:T(2,128)(2,1)S(1)} %broadcast_in_dim.27), channel_id=1, replica_groups=mesh['y'=4,'z'=8,'x'=4,'core'=2] {'z'}, dimensions={0} | all-to-all | bytes 352256 | tf_op jit(solution)/shard_map/gather/all_to_all | solution.py:24
  23.2 1.7 broadcast_in_dim.29
  25.0 7.2 %all-to-all-start.1 = ((bf16[16,16,5504]{2,1,0:T(8,128)(2,1)}), bf16[16,16,5504]{2,1,0:T(8,128)(2,1)S(1)}, u32[]{:S(2)}, u32[]{:S(2)}) async-start(bf16[16,16,5504]{2,1,0:T(8,128)(2,1)} %broadcast_in_dim.29), calls=%async_computation.1 | async-start | bytes 5636096 | tf_op jit(solution)/shard_map/gather/all_to_all | solution.py:24
  32.2 39.2 %all-to-all-done.1 = bf16[16,16,5504]{2,1,0:T(8,128)(2,1)S(1)} async-done(((bf16[16,16,5504]{2,1,0:T(8,128)(2,1)}), bf16[16,16,5504]{2,1,0:T(8,128)(2,1)S(1)}, u32[]{:S(2)}, u32[]{:S(2)}) %all-to-all-start.1) | async-done | bytes 2818080 | tf_op jit(solution)/shard_map/gather/all_to_all | solution.py:24
  71.7 0.7 copy.43
  72.4 0.7 copy.45
  73.1 4.5 %fusion.26 = (f32[256]{0:T(256)S(1)}, f32[256,592]{0,1:T(8,128)S(1)}) fusion(bf16[592,5120]{1,0:T(8,128)(2,1)} %param.6, bf16[256,5504]{1,0:T(8,128)(2,1)S(1)} %bitcast.45), kind=kOutput, calls=%fused_computation.61 | convolution fusion | flops 1552043776 | bytes 9290752 | tf_op jit(solution)/shard_map/logits/vd,rd->vr/dot_general | solution.py:77
  77.7 4.7 %fusion.27 = (f32[256]{0:T(256)S(1)}, f32[256,592]{0,1:T(8,128)S(1)}) fusion(bf16[592,5120]{1,0:T(8,128)(2,1)} %collective-permute-done, bf16[256,5504]{1,0:T(8,128)(2,1)S(1)} %bitcast.46), kind=kOutput, calls=%fused_computation.62 | convolution fusion | flops 1552043776 | bytes 9290752 | tf_op jit(solution)/shard_map/logits/vd,rd->vr/dot_general | solution.py:78
  83.2 0.8 broadcast_in_dim.30
  84.0 7.7 %all-to-all-start.2 = ((f32[128,2,256]{2,1,0:T(2,128)}), f32[128,2,256]{2,1,0:T(2,128)S(1)}, u32[]{:S(2)}, u32[]{:S(2)}) async-start(f32[128,2,256]{2,1,0:T(2,128)} %broadcast_in_dim.30), calls=%async_computation.2 | async-start | bytes 524288 | tf_op jit(solution)/shard_map/stats/all_to_all | solution.py:24
  91.7 14.7 %select_reduce_fusion = (f32[592,256]{1,0:T(8,128)}, f32[592,256]{1,0:T(8,128)}) fusion(s32[64,256]{1,0:T(8,128)} %copy.45, f32[64,256]{1,0:T(8,128)S(1)} %copy.44, s32[64,256]{1,0:T(8,128)} %copy.43), kind=kLoop, calls=%fused_computation | loop fusion | flops 57892864 | bytes 1409024 | tf_op jit(solution)/shard_map/target/reduce_sum | solution.py:30
  106.9 2.0 %fusion.10 = (bf16[592,256]{1,0:T(8,128)(2,1)S(1)}, bf16[592,256]{1,0:T(8,128)(2,1)S(1)}) fusion(f32[592,256]{1,0:T(8,128)} %get-tuple-element.2, f32[256,592]{0,1:T(8,128)} %copy-done.1, f32[256]{0:T(256)S(1)} %multiply_divide_fusion, f32[256]{0:T(256)S(1)} %max.17, f32[592,256]{1,0:T(8,128)} %get-tuple-element.3, f32[256,592]{0,1:T(8,128)} %copy-done), kind=kLoop, calls=%fused_computation.16 | loop fusion | flops 1212416 | bytes 3033088 | tf_op jit(solution)/shard_map/grads/convert_element_type | solution.py:95
  109.0 4.4 %convolution_convert_fusion = bf16[592,5120]{1,0:T(8,128)(2,1)} fusion(bf16[592,256]{1,0:T(8,128)(2,1)S(1)} %get-tuple-element.11, bf16[256,5504]{1,0:T(8,128)(2,1)S(1)} %bitcast.47), kind=kOutput, calls=%fused_computation.5 | convolution fusion | flops 1554923520 | bytes 8986624 | tf_op jit(solution)/shard_map/grads/dot_general | solution.py:96
  113.4 2.2 %fusion.28 = f32[256,5120]{1,0:T(8,128)S(1)} fusion(bf16[592,256]{1,0:T(8,128)(2,1)S(1)} %get-tuple-element.12, bf16[592,5120]{1,0:T(8,128)(2,1)S(1)} %bitcast.51), kind=kOutput, calls=%fused_computation.63 | convolution fusion | flops 1551892480 | bytes 11608064 | tf_op jit(solution)/shard_map/grads/vr,vd->rd/dot_general | solution.py:98
  115.6 5.0 %fusion = bf16[256,5120]{1,0:T(8,128)(2,1)S(1)} fusion(f32[256,5120]{1,0:T(8,128)S(1)} %fusion.28, bf16[592,256]{1,0:T(8,128)(2,1)S(1)} %get-tuple-element.11, bf16[592,5120]{1,0:T(8,128)(2,1)} %collective-permute-done), kind=kOutput, calls=%fused_computation.7 | convolution fusion | flops 1554513920 | bytes 14229504 | tf_op jit(solution)/shard_map/grads/vr,vd->rd/dot_general | solution.py:100
  120.6 39.5 %all_to_all.26 = bf16[16,16,5120]{2,1,0:T(8,128)(2,1)} all-to-all(bf16[16,16,5120]{2,1,0:T(8,128)(2,1)S(1)} %bitcast.49), channel_id=1, replica_groups=mesh['y'=4,'z'=8,'x'=4,'core'=2] {'y','x'}, dimensions={0} | all-to-all | bytes 5242880 | tf_op jit(solution)/shard_map/scatter/all_to_all | solution.py:105
  160.1 2.1 %reduce_sum.84 = bf16[16,5120]{1,0:T(8,128)(2,1)S(1)} reduce(bf16[16,16,5120]{2,1,0:T(8,128)(2,1)} %all_to_all.26, bf16[]{:T(256)} %constant.60.clone.1), dimensions={0}, to_apply=%region_9.10 | reduce | flops 1228800 | bytes 2785282 | tf_op jit(solution)/shard_map/scatter/reduce_sum | solution.py:106
  162.3 16.0 %all_to_all.27 = bf16[8,2,5120]{2,1,0:T(2,128)(2,1)S(1)} all-to-all(bf16[8,2,5120]{2,1,0:T(2,128)(2,1)S(1)} %reshape.83), channel_id=1, replica_groups=mesh['y'=4,'z'=8,'x'=4,'core'=2] {'z'}, dimensions={0} | all-to-all | bytes 327680 | tf_op jit(solution)/shard_map/scatter/all_to_all | solution.py:108
  178.3 0.7 reduce_sum.85
  179.0 7.1 %add_convert_fusion = bf16[592,5120]{1,0:T(8,128)(2,1)} fusion(bf16[592,5120]{1,0:T(8,128)(2,1)} %collective-permute-done.1, bf16[592,256]{1,0:T(8,128)(2,1)S(1)} %get-tuple-element.12, bf16[256,5504]{1,0:T(8,128)(2,1)S(1)} %bitcast.48), kind=kOutput, calls=%fused_computation.4 | convolution fusion | flops 1560985600 | bytes 15048704 | tf_op jit(solution)/shard_map/grad_weight/dot_general | solution.py:112
  (33 shorter events, 2.4 us)
Async XLA Ops:
  0.6 77.0 %collective-permute-start = (bf16[592,5120]{1,0:T(8,128)(2,1)}, bf16[592,5120]{1,0:T(8,128)(2,1)}, u32[]{:S(2)}, u32[]{:S(2)}) collective-permute-start(bf16[592,5120]{1,0:T(8,128)(2,1)} %param.6), channel_id=1, source_target_pairs={{0,1},{1,0},{2,3},{3,2},{4,5},{5,4},{6,7},{7,6},{8,9},{9,8},{10,11... | collective-permute-start | bytes 18186248 | tf_op jit(solution)/shard_map/ppermute | solution.py:38
  25.0 46.4 %all-to-all-start.1 = ((bf16[16,16,5504]{2,1,0:T(8,128)(2,1)}), bf16[16,16,5504]{2,1,0:T(8,128)(2,1)S(1)}, u32[]{:S(2)}, u32[]{:S(2)}) async-start(bf16[16,16,5504]{2,1,0:T(8,128)(2,1)} %broadcast_in_dim.29), calls=%async_computation.1 | async-start | bytes 5636096 | tf_op jit(solution)/shard_map/gather/all_to_all | solution.py:24
  77.6 4.9 %copy-start = (f32[256,592]{0,1:T(8,128)}, f32[256,592]{0,1:T(8,128)S(1)}, u32[]{:S(2)}) copy-start(f32[256,592]{0,1:T(8,128)S(1)} %get-tuple-element.22) | copy-start | bytes 1818628
  82.4 0.8 copy-start.1
  84.0 22.6 %all-to-all-start.2 = ((f32[128,2,256]{2,1,0:T(2,128)}), f32[128,2,256]{2,1,0:T(2,128)S(1)}, u32[]{:S(2)}, u32[]{:S(2)}) async-start(f32[128,2,256]{2,1,0:T(2,128)} %broadcast_in_dim.30), calls=%async_computation.2 | async-start | bytes 524288 | tf_op jit(solution)/shard_map/stats/all_to_all | solution.py:24
  106.9 6.4 %slice-start = ((s8[6062080]{0:T(1024)(128)(4,1)}), s8[4194304]{0:T(1024)(128)(4,1)S(1)}, s32[]{:S(2)}) async-start(s8[6062080]{0:T(1024)(128)(4,1)} %bitcast.50), calls=%async_computation.5 | async-start | bytes 8388608
  108.9 4.4 %slice-start.1 = ((s8[6062080]{0:T(1024)(128)(4,1)}), s8[1867776]{0:T(1024)(128)(4,1)S(1)}, s32[]{:S(2)}) async-start(s8[6062080]{0:T(1024)(128)(4,1)} %bitcast.50), calls=%async_computation.6 | async-start | bytes 3735552
  113.4 65.6 %collective-permute-start.1 = (bf16[592,5120]{1,0:T(8,128)(2,1)}, bf16[592,5120]{1,0:T(8,128)(2,1)}, u32[]{:S(2)}, u32[]{:S(2)}) collective-permute-start(bf16[592,5120]{1,0:T(8,128)(2,1)} %convolution_convert_fusion), channel_id=1, source_target_pairs={{0,1},{1,0},{2,3},{3,2},{4,5},{5,4},{6,7},{7,6},{8,9},{9,8},{10,11... | collective-permute-start | bytes 18186248 | tf_op jit(solution)/shard_map/grads/ppermute | solution.py:97

commit v2 on v1

--- a/solution.py
+++ b/solution.py
@@ -1,10 +1,12 @@
 import jax
 import jax.numpy as jnp
+import numpy as np
 from jax import lax
 from jax.sharding import Mesh, PartitionSpec as P
 
 AXES = ("y", "z", "x", "core")
 SWAP = [(0, 1), (1, 0)]
+SIDE = 4
 DIGIT = 512
 HALF = 256
 ID_SHIFT = 148
@@ -24,6 +26,41 @@
     return lax.all_to_all(copies, axes, 0, 0, tiled=True)
 
 
+def partner(block, sizes, leg, step):
+    pairs = []
+    for source, (y, z, x, core) in enumerate(np.ndindex(*sizes)):
+        if (core + leg) % 2 == 0:
+            x = x ^ step
+        else:
+            y = y ^ step
+        pairs.append((source, int(np.ravel_multi_index((y, z, x, core), sizes))))
+    return lax.ppermute(block, AXES, pairs)
+
+
+def gather_blocks(block, sizes, leg, place):
+    result = jnp.zeros((SIDE,) + block.shape, block.dtype)
+    for step in range(SIDE):
+        piece = partner(block, sizes, leg, step) if step else block
+        result = lax.dynamic_update_index_in_dim(result, piece, place ^ step, 0)
+    return result.reshape((-1,) + block.shape[1:])
+
+
+def scatter_blocks(values, sizes, leg, place):
+    values = values.reshape((SIDE, -1) + values.shape[1:])
+    pieces = []
+    for step in range(SIDE):
+        piece = lax.dynamic_index_in_dim(values, place ^ step, 0, keepdims=False)
+        pieces.append(partner(piece, sizes, leg, step) if step else piece)
+    return pieces
+
+
+def total(pieces):
+    result = pieces[0].astype(jnp.float32)
+    for piece in pieces[1:]:
+        result = result + piece.astype(jnp.float32)
+    return result.astype(jnp.bfloat16)
+
+
 def dense_target(local_ids, weighted_probs, entries):
     columns = jnp.arange(entries, dtype=jnp.int32)
     matches = local_ids.T[:, None, :] == columns[None, :, None]
@@ -35,6 +72,12 @@
     own_rows, width = hidden_states.shape
     entries = head_weight.shape[0]
     kept = teacher_ids.shape[1]
+    group = size_z * own_rows
+    rows = size_y * size_x * group
+    core = lax.axis_index("core")
+    place_x, place_y = lax.axis_index("x"), lax.axis_index("y")
+    first_place = jnp.where(core == 0, place_x, place_y)
+    second_place = jnp.where(core == 0, place_y, place_x)
     other_weight = lax.ppermute(head_weight, "core", SWAP)
 
     with jax.named_scope("pack"):
@@ -46,19 +89,18 @@
         extra += split_bf16(weighted, 2)
         extra += split_bf16(mass[:, None], 3)
         used = sum(piece.shape[1] for piece in extra)
-        padding = -used % 128
-        extra.append(jnp.zeros((own_rows, padding), jnp.bfloat16))
-        packed = jnp.concatenate([hidden_states] + extra, axis=1)
+        tail_width = used + -used % 128
+        extra.append(jnp.zeros((own_rows, tail_width - used), jnp.bfloat16))
+        packed = jnp.concatenate(extra + [hidden_states], axis=1)
 
     with jax.named_scope("gather"):
-        across_z = spread(packed, "z", size_z).reshape(size_z * own_rows, -1)
-        gathered = spread(across_z, ("y", "x"), size_y * size_x)
-        rows = size_y * size_x * size_z * own_rows
-        gathered = gathered.reshape(rows, -1)
+        across_z = spread(packed, "z", size_z).reshape(group, -1)
+        gathered = gather_blocks(across_z, sizes, 0, first_place)
+        gathered = gather_blocks(gathered, sizes, 1, second_place)
+        hidden = gathered[:, tail_width:]
 
-    hidden = gathered[:, :width]
     with jax.named_scope("unpack"):
-        tail = gathered[:, width:].astype(jnp.float32)
+        tail = gathered[:, :tail_width].astype(jnp.float32)
         high = tail[:, :kept].astype(jnp.int32) + ID_SHIFT
         low = tail[:, kept : 2 * kept].astype(jnp.int32) + HALF
         ids = high * DIGIT + low
@@ -66,7 +108,6 @@
         mass = tail[:, 4 * kept] + tail[:, 4 * kept + 1] + tail[:, 4 * kept + 2]
 
     device = lax.axis_index(AXES)
-    core = lax.axis_index("core")
     first = device * entries
     other_first = (device + 1 - 2 * core) * entries
     with jax.named_scope("target"):
@@ -81,10 +122,10 @@
         top = jnp.maximum(jnp.max(logits, axis=0), jnp.max(other_logits, axis=0))
         exponent = jnp.exp(logits - top[None])
         other_exponent = jnp.exp(other_logits - top[None])
-        total = jnp.sum(exponent, axis=0) + jnp.sum(other_exponent, axis=0)
+        row_sum = jnp.sum(exponent, axis=0) + jnp.sum(other_exponent, axis=0)
 
     with jax.named_scope("stats"):
-        stats = spread(jnp.stack([top, total]), ("y", "z", "x"), size_y * size_z * size_x)
+        stats = spread(jnp.stack([top, row_sum]), ("y", "z", "x"), size_y * size_z * size_x)
         stats = stats.reshape(-1, 2, rows)
         row_top = jnp.max(stats[:, 0], axis=0)
         row_total = jnp.sum(stats[:, 1] * jnp.exp(stats[:, 0] - row_top[None]), axis=0)
@@ -93,24 +134,35 @@
     with jax.named_scope("grads"):
         grad = (exponent * scale[None] - target).astype(jnp.bfloat16)
         other_grad = (other_exponent * scale[None] - other_target).astype(jnp.bfloat16)
-        other_part = jnp.dot(other_grad, hidden, preferred_element_type=jnp.float32)
-        returned = lax.ppermute(other_part.astype(jnp.bfloat16), "core", SWAP)
         partial = jnp.einsum(
             "vr,vd->rd", grad, head_weight, preferred_element_type=jnp.float32
         ) + jnp.einsum("vr,vd->rd", other_grad, other_weight, preferred_element_type=jnp.float32)
         partial = partial.astype(jnp.bfloat16)
 
     with jax.named_scope("scatter"):
-        pieces = partial.reshape(size_y * size_x, size_z * own_rows, width)
-        pieces = lax.all_to_all(pieces, ("y", "x"), 0, 0, tiled=True)
-        summed = jnp.sum(pieces.astype(jnp.float32), axis=0).astype(jnp.bfloat16)
-        pieces = summed.reshape(size_z, own_rows, width)
-        pieces = lax.all_to_all(pieces, "z", 0, 0, tiled=True)
-        grad_hidden = jnp.sum(pieces.astype(jnp.float32), axis=0).astype(jnp.bfloat16)
+        partial, other_grad = lax.optimization_barrier((partial, other_grad))
+        pieces = scatter_blocks(partial, sizes, 1, second_place)
+
+    with jax.named_scope("grad_weight"):
+        other_part = jnp.dot(other_grad, hidden, preferred_element_type=jnp.float32)
+        other_part = other_part.astype(jnp.bfloat16)
+        returned = lax.ppermute(other_part, "core", SWAP)
+
+    with jax.named_scope("scatter"):
+        pieces[0], other_part = lax.optimization_barrier((pieces[0], other_part))
+        summed = total(pieces)
+        summed, grad = lax.optimization_barrier((summed, grad))
+        pieces = scatter_blocks(summed, sizes, 0, first_place)
 
     with jax.named_scope("grad_weight"):
         own_part = jnp.dot(grad, hidden, preferred_element_type=jnp.float32)
         grad_weight = (own_part + returned.astype(jnp.float32)).astype(jnp.bfloat16)
+
+    with jax.named_scope("scatter"):
+        pieces[0], grad_weight = lax.optimization_barrier((pieces[0], grad_weight))
+        summed = total(pieces).reshape(size_z, own_rows, width)
+        pieces = lax.all_to_all(summed, "z", 0, 0, tiled=True)
+        grad_hidden = jnp.sum(pieces.astype(jnp.float32), axis=0).astype(jnp.bfloat16)
     return grad_hidden, grad_weight
 
 

time: 188 us -> 165 us (0.88)
  blocking collectives: 74.4 us -> 16 us
  starting transfers between devices: 14.9 us -> 34.3 us
  waiting for transfers between devices: 39.2 us -> 47.2 us
  other arithmetic: 22.8 us -> 30.7 us
  matrix products: 27.9 us -> 25.6 us
    all_to_all x3 -> x1, blocking collectives: 74.4 us -> 16 us  [per_device(): pieces = lax.all_to_all(summed, 'z', 0, 0, tiled=True)]
    ppermute x1 -> x13, waiting for transfers between devices: 0.01 us -> 37.2 us  [the longest x12 37.2 us: partner(): return lax.ppermute(block, AXES, pairs)]
    all_to_all x2, waiting for transfers between devices: 39.2 us -> 10 us  [spread(): return lax.all_to_all(copies, axes, 0, 0, tiled=True)]
    ppermute x1 -> x13, starting transfers between devices: 0.01 us -> 16.8 us  [the longest x12 16.7 us: partner(): return lax.ppermute(block, AXES, pairs)]
    reduce_sum x1, other arithmetic: 14.7 us -> 24.5 us  [dense_target(): jnp.sum(jnp.where(matches, weighted_probs.T[:, None, :], jnp.float32(0.0)...]
    dot_general x1, matrix products: 2.23 us -> 5.02 us  [per_device(): jnp.einsum('vr,vd->rd', grad, head_weight, preferred_element_type=jnp.flo...]
    dot_general x1, matrix products: 7.09 us -> 4.45 us  [per_device(): own_part = jnp.dot(grad, hidden, preferred_element_type=jnp.float32)]
    all_to_all x2, starting transfers between devices: 14.8 us -> 17.5 us  [spread(): return lax.all_to_all(copies, axes, 0, 0, tiled=True)]
  transfers between devices with their start and end apart: 4 -> 16, of which waited for: 1 -> 8; matrix products, arithmetic and copies ran while one was open for 20% -> 23% of each run, Pallas kernels for 0% -> 0%
where the time goes in v2:
time: 165 us; the launch traced here: 162 us
  waiting for transfers between devices  47.2 us (29%)
  starting transfers between devices  34.3 us (21%)
  other arithmetic  30.7 us (19%)
  matrix products  25.6 us (16%)
  blocking collectives  16 us (10%)
  local copies, waits for them, and re-layouts  6.97 us (4%)
    ppermute x12, waiting for transfers between devices, partner(): return lax.ppermute(block, AXES, pairs)  37.2 us
    reduce_sum x1, other arithmetic, dense_target(): jnp.sum(jnp.where(matches, weighted_probs.T[:, None, :], jnp.float32(0.0)...  24.5 us
    all_to_all x2, starting transfers between devices, spread(): return lax.all_to_all(copies, axes, 0, 0, tiled=True)  17.5 us
    ppermute x12, starting transfers between devices, partner(): return lax.ppermute(block, AXES, pairs)  16.7 us
    all_to_all x1, blocking collectives, per_device(): pieces = lax.all_to_all(summed, 'z', 0, 0, tiled=True)  16 us
    all_to_all x2, waiting for transfers between devices, spread(): return lax.all_to_all(copies, axes, 0, 0, tiled=True)  10 us
    dot_general x1, matrix products, per_device(): jnp.einsum('vr,vd->rd', other_grad, other_weight, preferred_element_type=...  5.12 us
    dot_general x1, matrix products, per_device(): jnp.einsum('vr,vd->rd', grad, head_weight, preferred_element_type=jnp.flo...  5.02 us
  transfers between devices with their start and end apart: 16, of which 8 were waited for; matrix products, arithmetic and copies ran while one was open for 23% of the time, Pallas kernels for 0%

profile of v2, /device:TPU:24, one launch (start us, length us, event | category | flops | bytes accessed | tf_op | source)
XLA Modules:
  0.0 161.8 jit_solution(244862044419830403)
XLA Ops:
  4.8 8.5 %all-to-all-start = ((bf16[8,2,5504]{2,1,0:T(2,128)(2,1)}), bf16[8,2,5504]{2,1,0:T(2,128)(2,1)S(1)}, u32[]{:S(2)}, u32[]{:S(2)}) async-start(bf16[8,2,5504]{2,1,0:T(2,128)(2,1)} %broadcast_in_dim.79), calls=%async_computation | async-start | bytes 352256 | tf_op jit(solution)/shard_map/gather/all_to_all | solution.py:26
  13.2 10.0 %all-to-all-done = bf16[8,2,5504]{2,1,0:T(2,128)(2,1)S(1)} async-done(((bf16[8,2,5504]{2,1,0:T(2,128)(2,1)}), bf16[8,2,5504]{2,1,0:T(2,128)(2,1)S(1)}, u32[]{:S(2)}, u32[]{:S(2)}) %all-to-all-start) | async-done | bytes 176160 | tf_op jit(solution)/shard_map/gather/all_to_all | solution.py:26
  23.3 2.8 %collective-permute-start.2 = (bf16[16,5504]{1,0:T(8,128)(2,1)S(1)}, bf16[16,5504]{1,0:T(8,128)(2,1)S(1)}, u32[]{:S(2)}, u32[]{:S(2)}) collective-permute-start(bf16[16,5504]{1,0:T(8,128)(2,1)S(1)} %reshape.90), channel_id=1, source_target_pairs={{0,6},{1,193},{2,4},{3,195},{4,2},{5,197},{6,0},{7,199},{8,14},{9,... | collective-permute-start | bytes 528392 | tf_op jit(solution)/shard_map/gather/ppermute | solution.py:37
  27.7 5.6 %collective-permute-done = bf16[16,5504]{1,0:T(8,128)(2,1)S(1)} collective-permute-done((bf16[16,5504]{1,0:T(8,128)(2,1)S(1)}, bf16[16,5504]{1,0:T(8,128)(2,1)S(1)}, u32[]{:S(2)}, u32[]{:S(2)}) %collective-permute-start) | collective-permute-done | bytes 176160 | tf_op jit(solution)/shard_map/gather/ppermute | solution.py:37
  34.2 1.0 collective-permute-start.5
  35.2 2.3 %collective-permute-start.4 = (bf16[64,5504]{1,0:T(8,128)(2,1)S(1)}, bf16[64,5504]{1,0:T(8,128)(2,1)S(1)}, u32[]{:S(2)}, u32[]{:S(2)}) collective-permute-start(bf16[64,5504]{1,0:T(8,128)(2,1)S(1)} %bitcast.85), channel_id=1, source_target_pairs={{0,128},{1,5},{2,130},{3,7},{4,132},{5,1},{6,134},{7,3},{8,136},{9... | collective-permute-start | bytes 2113544 | tf_op jit(solution)/shard_map/gather/ppermute | solution.py:37
  37.8 6.8 %collective-permute-done.3 = bf16[64,5504]{1,0:T(8,128)(2,1)} collective-permute-done((bf16[64,5504]{1,0:T(8,128)(2,1)S(1)}, bf16[64,5504]{1,0:T(8,128)(2,1)}, u32[]{:S(2)}, u32[]{:S(2)}) %collective-permute-start.3) | collective-permute-done | bytes 704544 | tf_op jit(solution)/shard_map/gather/ppermute | solution.py:37
  44.7 1.2 bitcast_dynamic-update-slice_fusion.2
  45.8 5.9 %collective-permute-done.4 = bf16[64,5504]{1,0:T(8,128)(2,1)S(1)} collective-permute-done((bf16[64,5504]{1,0:T(8,128)(2,1)S(1)}, bf16[64,5504]{1,0:T(8,128)(2,1)S(1)}, u32[]{:S(2)}, u32[]{:S(2)}) %collective-permute-start.4) | collective-permute-done | bytes 704544 | tf_op jit(solution)/shard_map/gather/ppermute | solution.py:37
  51.8 2.3 %collective-permute-done.5 = bf16[64,5504]{1,0:T(8,128)(2,1)S(1)} collective-permute-done((bf16[64,5504]{1,0:T(8,128)(2,1)S(1)}, bf16[64,5504]{1,0:T(8,128)(2,1)S(1)}, u32[]{:S(2)}, u32[]{:S(2)}) %collective-permute-start.5) | collective-permute-done | bytes 704544 | tf_op jit(solution)/shard_map/gather/ppermute | solution.py:37
  55.9 4.5 %fusion.23 = (f32[256]{0:T(256)S(1)}, f32[256,592]{0,1:T(8,128)S(1)}) fusion(bf16[592,5120]{1,0:T(8,128)(2,1)} %param.6, bf16[256,5504]{1,0:T(8,128)(2,1)S(1)} %bitcast.78), kind=kOutput, calls=%fused_computation.78 | convolution fusion | flops 1552043776 | bytes 9290752 | tf_op jit(solution)/shard_map/logits/vd,rd->vr/dot_general | solution.py:118
  60.4 4.7 %fusion.24 = (f32[256]{0:T(256)S(1)}, f32[256,592]{0,1:T(8,128)S(1)}) fusion(bf16[592,5120]{1,0:T(8,128)(2,1)} %collective-permute-done.6, bf16[256,5504]{1,0:T(8,128)(2,1)S(1)} %bitcast.79), kind=kOutput, calls=%fused_computation.79 | convolution fusion | flops 1552043776 | bytes 9290752 | tf_op jit(solution)/shard_map/logits/vd,rd->vr/dot_general | solution.py:119
  66.7 9.0 %all-to-all-start.1 = ((f32[128,2,256]{2,1,0:T(2,128)}), f32[128,2,256]{2,1,0:T(2,128)S(1)}, u32[]{:S(2)}, u32[]{:S(2)}) async-start(f32[128,2,256]{2,1,0:T(2,128)} %broadcast_in_dim.88), calls=%async_computation.1 | async-start | bytes 524288 | tf_op jit(solution)/shard_map/stats/all_to_all | solution.py:26
  75.8 24.5 %select_reduce_fusion = (f32[592,256]{1,0:T(8,128)}, f32[592,256]{1,0:T(8,128)}) fusion(s32[64,256]{1,0:T(8,128)} %copy.42, f32[64,256]{1,0:T(8,128)S(1)} %copy.41, s32[64,256]{1,0:T(8,128)} %copy.40), kind=kLoop, calls=%fused_computation | loop fusion | flops 57892864 | bytes 1409024 | tf_op jit(solution)/shard_map/target/reduce_sum | solution.py:67
  100.8 1.9 %fusion.7 = (bf16[592,256]{1,0:T(8,128)(2,1)S(1)}, bf16[592,256]{1,0:T(8,128)(2,1)S(1)}) fusion(f32[592,256]{1,0:T(8,128)} %get-tuple-element.16, f32[256,592]{0,1:T(8,128)} %copy-done.1, f32[256]{0:T(256)S(1)} %multiply_divide_fusion, f32[256]{0:T(256)S(1)} %max.17, f32[592,256]{1,0:T(8,128)} %get-tuple-element.17, f32[256,592]{0,1:T(8,128)} %copy-done), kind=kLoop, calls=%fused_computation.24 | loop fusion | flops 1212416 | bytes 3033088 | tf_op jit(solution)/shard_map/grads/convert_element_type | solution.py:136
  102.7 5.0 %fusion.25 = f32[256,5120]{1,0:T(8,128)S(1)} fusion(bf16[592,256]{1,0:T(8,128)(2,1)S(1)} %get-tuple-element.13, bf16[592,5120]{1,0:T(8,128)(2,1)} %param.6), kind=kOutput, calls=%fused_computation.80 | convolution fusion | flops 1551892480 | bytes 11608064 | tf_op jit(solution)/shard_map/grads/vr,vd->rd/dot_general | solution.py:137
  107.7 5.1 %fusion = bf16[256,5120]{1,0:T(8,128)(2,1)S(1)} fusion(f32[256,5120]{1,0:T(8,128)S(1)} %fusion.25, bf16[592,256]{1,0:T(8,128)(2,1)S(1)} %get-tuple-element.10, bf16[592,5120]{1,0:T(8,128)(2,1)} %collective-permute-done.6), kind=kOutput, calls=%fused_computation.7 | convolution fusion | flops 1554513920 | bytes 14229504 | tf_op jit(solution)/shard_map/grads/vr,vd->rd/dot_general | solution.py:139
  112.8 1.8 %convolution_convert_fusion = bf16[592,5120]{1,0:T(8,128)(2,1)S(1)} fusion(bf16[592,256]{1,0:T(8,128)(2,1)S(1)} %get-tuple-element.10, bf16[256,5504]{1,0:T(8,128)(2,1)S(1)} %bitcast.80), kind=kOutput, calls=%fused_computation.5 | convolution fusion | flops 1554923520 | bytes 8986624 | tf_op jit(solution)/shard_map/grad_weight/dot_general | solution.py:147
  115.3 2.4 %collective-permute-start.8 = (bf16[64,5120]{1,0:T(8,128)(2,1)S(1)}, bf16[64,5120]{1,0:T(8,128)(2,1)S(1)}, u32[]{:S(2)}, u32[]{:S(2)}) collective-permute-start(bf16[64,5120]{1,0:T(8,128)(2,1)S(1)} %get-tuple-element.22), channel_id=1, source_target_pairs={{0,128},{1,5},{2,130},{3,7},{4,132},{5,1},{6,134},{7,3},{8,136},{9... | collective-permute-start | bytes 1966088 | tf_op jit(solution)/shard_map/scatter/ppermute | solution.py:37
  117.7 1.4 collective-permute-start.7
  119.1 14.7 %collective-permute-done.9 = bf16[64,5120]{1,0:T(8,128)(2,1)S(1)} collective-permute-done((bf16[64,5120]{1,0:T(8,128)(2,1)S(1)}, bf16[64,5120]{1,0:T(8,128)(2,1)S(1)}, u32[]{:S(2)}, u32[]{:S(2)}) %collective-permute-start.9) | collective-permute-done | bytes 655392 | tf_op jit(solution)/shard_map/scatter/ppermute | solution.py:37
  135.1 2.8 %collective-permute-start.13 = (bf16[16,5120]{1,0:T(8,128)(2,1)S(1)}, bf16[16,5120]{1,0:T(8,128)(2,1)S(1)}, u32[]{:S(2)}, u32[]{:S(2)}) collective-permute-start(bf16[16,5120]{1,0:T(8,128)(2,1)S(1)} %get-tuple-element.25), channel_id=1, source_target_pairs={{0,6},{1,193},{2,4},{3,195},{4,2},{5,197},{6,0},{7,199},{8,14},{9,... | collective-permute-start | bytes 491528 | tf_op jit(solution)/shard_map/scatter/ppermute | solution.py:37
  139.3 4.5 %add_convert_fusion = bf16[592,5120]{1,0:T(8,128)(2,1)} fusion(bf16[592,5120]{1,0:T(8,128)(2,1)S(1)} %collective-permute-done.10, bf16[592,256]{1,0:T(8,128)(2,1)S(1)} %get-tuple-element.13, bf16[256,5504]{1,0:T(8,128)(2,1)S(1)} %bitcast.81), kind=kOutput, calls=%fused_computation.4 | convolution fusion | flops 1560985600 | bytes 15048704 | tf_op jit(solution)/shard_map/grad_weight/dot_general | solution.py:158
  144.9 16.0 %all_to_all.15 = bf16[8,2,5120]{2,1,0:T(2,128)(2,1)S(1)} all-to-all(bf16[8,2,5120]{2,1,0:T(2,128)(2,1)S(1)} %reshape.95), channel_id=1, replica_groups=mesh['y'=4,'z'=8,'x'=4,'core'=2] {'z'}, dimensions={0} | all-to-all | bytes 327680 | tf_op jit(solution)/shard_map/scatter/all_to_all | solution.py:164
  (63 shorter events, 16.1 us)
Async XLA Ops:
  4.8 18.5 %all-to-all-start = ((bf16[8,2,5504]{2,1,0:T(2,128)(2,1)}), bf16[8,2,5504]{2,1,0:T(2,128)(2,1)S(1)}, u32[]{:S(2)}, u32[]{:S(2)}) async-start(bf16[8,2,5504]{2,1,0:T(2,128)(2,1)} %broadcast_in_dim.79), calls=%async_computation | async-start | bytes 352256 | tf_op jit(solution)/shard_map/gather/all_to_all | solution.py:26
  23.3 10.0 %collective-permute-start.2 = (bf16[16,5504]{1,0:T(8,128)(2,1)S(1)}, bf16[16,5504]{1,0:T(8,128)(2,1)S(1)}, u32[]{:S(2)}, u32[]{:S(2)}) collective-permute-start(bf16[16,5504]{1,0:T(8,128)(2,1)S(1)} %reshape.90), channel_id=1, source_target_pairs={{0,6},{1,193},{2,4},{3,195},{4,2},{5,197},{6,0},{7,199},{8,14},{9,... | collective-permute-start | bytes 528392 | tf_op jit(solution)/shard_map/gather/ppermute | solution.py:37
  26.2 7.1 %collective-permute-start.1 = (bf16[16,5504]{1,0:T(8,128)(2,1)S(1)}, bf16[16,5504]{1,0:T(8,128)(2,1)S(1)}, u32[]{:S(2)}, u32[]{:S(2)}) collective-permute-start(bf16[16,5504]{1,0:T(8,128)(2,1)S(1)} %reshape.90), channel_id=1, source_target_pairs={{0,4},{1,129},{2,6},{3,131},{4,0},{5,133},{6,2},{7,135},{8,12},{9,... | collective-permute-start | bytes 528392 | tf_op jit(solution)/shard_map/gather/ppermute | solution.py:37
  27.0 6.3 %collective-permute-start = (bf16[16,5504]{1,0:T(8,128)(2,1)S(1)}, bf16[16,5504]{1,0:T(8,128)(2,1)S(1)}, u32[]{:S(2)}, u32[]{:S(2)}) collective-permute-start(bf16[16,5504]{1,0:T(8,128)(2,1)S(1)} %reshape.90), channel_id=1, source_target_pairs={{0,2},{1,65},{2,0},{3,67},{4,6},{5,69},{6,4},{7,71},{8,10},{9,73},... | collective-permute-start | bytes 528392 | tf_op jit(solution)/shard_map/gather/ppermute | solution.py:37
  33.4 11.3 %collective-permute-start.3 = (bf16[64,5504]{1,0:T(8,128)(2,1)S(1)}, bf16[64,5504]{1,0:T(8,128)(2,1)}, u32[]{:S(2)}, u32[]{:S(2)}) collective-permute-start(bf16[64,5504]{1,0:T(8,128)(2,1)S(1)} %bitcast.83), channel_id=1, source_target_pairs={{0,64},{1,3},{2,66},{3,1},{4,68},{5,7},{6,70},{7,5},{8,72},{9,11},... | collective-permute-start | bytes 2113544 | tf_op jit(solution)/shard_map/gather/ppermute | solution.py:37
  34.2 26.2 %collective-permute-start.6 = (bf16[592,5120]{1,0:T(8,128)(2,1)}, bf16[592,5120]{1,0:T(8,128)(2,1)}, u32[]{:S(2)}, u32[]{:S(2)}) collective-permute-start(bf16[592,5120]{1,0:T(8,128)(2,1)} %param.6), channel_id=1, source_target_pairs={{0,1},{1,0},{2,3},{3,2},{4,5},{5,4},{6,7},{7,6},{8,9},{9,8},{10,11... | collective-permute-start | bytes 18186248 | tf_op jit(solution)/shard_map/ppermute | solution.py:81
  34.2 19.9 %collective-permute-start.5 = (bf16[64,5504]{1,0:T(8,128)(2,1)S(1)}, bf16[64,5504]{1,0:T(8,128)(2,1)S(1)}, u32[]{:S(2)}, u32[]{:S(2)}) collective-permute-start(bf16[64,5504]{1,0:T(8,128)(2,1)S(1)} %bitcast.84), channel_id=1, source_target_pairs={{0,192},{1,7},{2,194},{3,5},{4,196},{5,3},{6,198},{7,1},{8,200},{9... | collective-permute-start | bytes 2113544 | tf_op jit(solution)/shard_map/gather/ppermute | solution.py:37
  35.2 16.5 %collective-permute-start.4 = (bf16[64,5504]{1,0:T(8,128)(2,1)S(1)}, bf16[64,5504]{1,0:T(8,128)(2,1)S(1)}, u32[]{:S(2)}, u32[]{:S(2)}) collective-permute-start(bf16[64,5504]{1,0:T(8,128)(2,1)S(1)} %bitcast.85), channel_id=1, source_target_pairs={{0,128},{1,5},{2,130},{3,7},{4,132},{5,1},{6,134},{7,3},{8,136},{9... | collective-permute-start | bytes 2113544 | tf_op jit(solution)/shard_map/gather/ppermute | solution.py:37
  60.4 4.8 %copy-start = (f32[256,592]{0,1:T(8,128)}, f32[256,592]{0,1:T(8,128)S(1)}, u32[]{:S(2)}) copy-start(f32[256,592]{0,1:T(8,128)S(1)} %get-tuple-element.44) | copy-start | bytes 1818628
  65.1 0.8 copy-start.1
  66.7 33.7 %all-to-all-start.1 = ((f32[128,2,256]{2,1,0:T(2,128)}), f32[128,2,256]{2,1,0:T(2,128)S(1)}, u32[]{:S(2)}, u32[]{:S(2)}) async-start(f32[128,2,256]{2,1,0:T(2,128)} %broadcast_in_dim.88), calls=%async_computation.1 | async-start | bytes 524288 | tf_op jit(solution)/shard_map/stats/all_to_all | solution.py:26
  114.6 24.7 %collective-permute-start.10 = (bf16[592,5120]{1,0:T(8,128)(2,1)S(1)}, bf16[592,5120]{1,0:T(8,128)(2,1)S(1)}, u32[]{:S(2)}, u32[]{:S(2)}) collective-permute-start(bf16[592,5120]{1,0:T(8,128)(2,1)S(1)} %convolution_convert_fusion), channel_id=1, source_target_pairs={{0,1},{1,0},{2,3},{3,2},{4,5},{5,4},{6,7},{7,6},{8,9},{9,8},{10,11... | collective-permute-start | bytes 18186248 | tf_op jit(solution)/shard_map/grad_weight/ppermute | solution.py:149
  114.9 18.9 %collective-permute-start.9 = (bf16[64,5120]{1,0:T(8,128)(2,1)S(1)}, bf16[64,5120]{1,0:T(8,128)(2,1)S(1)}, u32[]{:S(2)}, u32[]{:S(2)}) collective-permute-start(bf16[64,5120]{1,0:T(8,128)(2,1)S(1)} %get-tuple-element.21), channel_id=1, source_target_pairs={{0,192},{1,7},{2,194},{3,5},{4,196},{5,3},{6,198},{7,1},{8,200},{9... | collective-permute-start | bytes 1966088 | tf_op jit(solution)/shard_map/scatter/ppermute | solution.py:37
  115.3 18.5 %collective-permute-start.8 = (bf16[64,5120]{1,0:T(8,128)(2,1)S(1)}, bf16[64,5120]{1,0:T(8,128)(2,1)S(1)}, u32[]{:S(2)}, u32[]{:S(2)}) collective-permute-start(bf16[64,5120]{1,0:T(8,128)(2,1)S(1)} %get-tuple-element.22), channel_id=1, source_target_pairs={{0,128},{1,5},{2,130},{3,7},{4,132},{5,1},{6,134},{7,3},{8,136},{9... | collective-permute-start | bytes 1966088 | tf_op jit(solution)/shard_map/scatter/ppermute | solution.py:37
  117.7 17.0 %collective-permute-start.7 = (bf16[64,5120]{1,0:T(8,128)(2,1)S(1)}, bf16[64,5120]{1,0:T(8,128)(2,1)S(1)}, u32[]{:S(2)}, u32[]{:S(2)}) collective-permute-start(bf16[64,5120]{1,0:T(8,128)(2,1)S(1)} %get-tuple-element.23), channel_id=1, source_target_pairs={{0,64},{1,3},{2,66},{3,1},{4,68},{5,7},{6,70},{7,5},{8,72},{9,11},... | collective-permute-start | bytes 1966088 | tf_op jit(solution)/shard_map/scatter/ppermute | solution.py:37
  135.1 8.6 %collective-permute-start.13 = (bf16[16,5120]{1,0:T(8,128)(2,1)S(1)}, bf16[16,5120]{1,0:T(8,128)(2,1)S(1)}, u32[]{:S(2)}, u32[]{:S(2)}) collective-permute-start(bf16[16,5120]{1,0:T(8,128)(2,1)S(1)} %get-tuple-element.25), channel_id=1, source_target_pairs={{0,6},{1,193},{2,4},{3,195},{4,2},{5,197},{6,0},{7,199},{8,14},{9,... | collective-permute-start | bytes 491528 | tf_op jit(solution)/shard_map/scatter/ppermute | solution.py:37
  137.9 6.8 %collective-permute-start.12 = (bf16[16,5120]{1,0:T(8,128)(2,1)S(1)}, bf16[16,5120]{1,0:T(8,128)(2,1)S(1)}, u32[]{:S(2)}, u32[]{:S(2)}) collective-permute-start(bf16[16,5120]{1,0:T(8,128)(2,1)S(1)} %get-tuple-element.26), channel_id=1, source_target_pairs={{0,4},{1,129},{2,6},{3,131},{4,0},{5,133},{6,2},{7,135},{8,12},{9,... | collective-permute-start | bytes 491528 | tf_op jit(solution)/shard_map/scatter/ppermute | solution.py:37
  138.7 6.0 %collective-permute-start.11 = (bf16[16,5120]{1,0:T(8,128)(2,1)S(1)}, bf16[16,5120]{1,0:T(8,128)(2,1)S(1)}, u32[]{:S(2)}, u32[]{:S(2)}) collective-permute-start(bf16[16,5120]{1,0:T(8,128)(2,1)S(1)} %get-tuple-element.27), channel_id=1, source_target_pairs={{0,2},{1,65},{2,0},{3,67},{4,6},{5,69},{6,4},{7,71},{8,10},{9,73},... | collective-permute-start | bytes 491528 | tf_op jit(solution)/shard_map/scatter/ppermute | solution.py:37

commit v3 on v2

v3 whole, which is shorter than its diff:
```python
import jax
import jax.numpy as jnp
import numpy as np
from jax import lax
from jax.experimental import pallas as pl
from jax.experimental.pallas import tpu as pltpu
from jax.sharding import Mesh, PartitionSpec as P

AXES = ("y", "z", "x", "core")
SWAP = [(0, 1), (1, 0)]
SIDE = 4
DIGIT = 512
HALF = 256
ID_SHIFT = 148


def spread(block, axes, count):
    copies = jnp.broadcast_to(block[None], (count,) + block.shape)
    return lax.all_to_all(copies, axes, 0, 0, tiled=True)


def partner(block, sizes, leg, step):
    pairs = []
    for source, (y, z, x, core) in enumerate(np.ndindex(*sizes)):
        if (core + leg) % 2 == 0:
            x = x ^ step
        else:
            y = y ^ step
        pairs.append((source, int(np.ravel_multi_index((y, z, x, core), sizes))))
    return lax.ppermute(block, AXES, pairs)


def gather_blocks(block, sizes, leg, spots):
    result = jnp.zeros((SIDE,) + block.shape, block.dtype)
    for step in range(SIDE):
        piece = partner(block, sizes, leg, step) if step else block
        result = lax.dynamic_update_slice(
            result, piece[None], (spots[step],) + (jnp.uint32(0),) * block.ndim
        )
    return result.reshape((-1,) + block.shape[1:])


def scatter_blocks(values, sizes, leg, spots):
    values = values.reshape((SIDE, -1) + values.shape[1:])
    pieces = []
    for step in range(SIDE):
        start = (spots[step],) + (jnp.uint32(0),) * (values.ndim - 1)
        piece = lax.dynamic_slice(values, start, (1,) + values.shape[1:])[0]
        pieces.append(partner(piece, sizes, leg, step) if step else piece)
    return pieces


def total(pieces):
    result = pieces[0].astype(jnp.float32)
    for piece in pieces[1:]:
        result = result + piece.astype(jnp.float32)
    return result.astype(jnp.bfloat16)


def rounded(value):
    return value.astype(jnp.bfloat16).astype(jnp.float32)


def pack_kernel(weight_ref, hidden_ref, ids_ref, probs_ref, out_ref):
    probs = probs_ref[...]
    own_rows, kept = probs.shape
    width = hidden_ref.shape[1]
    row = lax.broadcasted_iota(jnp.int32, (own_rows, 1), 0)
    weight = jnp.zeros((own_rows, 1), jnp.float32)
    for i in range(own_rows):
        weight = jnp.where(row == i, weight_ref[i], weight)
    ids = ids_ref[...]
    high = ((ids >> 9) - ID_SHIFT).astype(jnp.float32)
    low = ((ids & (DIGIT - 1)) - HALF).astype(jnp.float32)
    weighted = probs * weight
    weighted_high = rounded(weighted)
    mass = jnp.sum(probs, axis=1, keepdims=True) * weight
    column = lax.broadcasted_iota(jnp.int32, (own_rows, 2 * kept), 1)
    pieces = jnp.zeros((own_rows, 2 * kept), jnp.float32)
    for i in range(3):
        part = rounded(mass)
        pieces = jnp.where(column == i, part, pieces)
        mass = mass - part
    tail = jnp.concatenate(
        [
            jnp.concatenate([high, low], axis=1),
            jnp.concatenate([weighted_high, rounded(weighted - weighted_high)], axis=1),
            pieces,
        ],
        axis=1,
    ).astype(jnp.bfloat16)
    hidden = hidden_ref[...]
    for i in range(out_ref.shape[0]):
        out_ref[i, :, :width] = hidden
        out_ref[i, :, width:] = tail


def pack(hidden, ids, probs, weight, copies):
    own_rows, width = hidden.shape
    kept = ids.shape[1]
    vmem = pl.BlockSpec(memory_space=pltpu.VMEM)
    return pl.pallas_call(
        pack_kernel,
        out_shape=jax.ShapeDtypeStruct((copies, own_rows, width + 6 * kept), jnp.bfloat16),
        in_specs=[pl.BlockSpec(memory_space=pltpu.SMEM), vmem, vmem, vmem],
        out_specs=vmem,
        name="pack",
    )(weight, hidden, ids, probs)


def target_kernel(first_ref, digits_ref, probs_ref, out_ref, place_ref):
    entries = out_ref.shape[0] // 2
    kept = place_ref.shape[0]
    digits = digits_ref[...].astype(jnp.float32).T.astype(jnp.int32)
    probs = probs_ref[...].astype(jnp.float32).T
    probs = probs[:kept] + probs[kept:]
    ids = (digits[:kept] + ID_SHIFT) * DIGIT + digits[kept:] + HALF
    own = ids - first_ref[0]
    other = ids - first_ref[1]
    none = jnp.int32(4 * entries)
    place = jnp.where((other >= 0) & (other < entries), other + entries, none)
    place = jnp.where((own >= 0) & (own < entries), own, place)
    place_ref[...] = place
    out_ref[...] = jnp.zeros_like(out_ref)
    rows = out_ref.shape[1]
    step = 16
    index = lax.broadcasted_iota(jnp.int32, (step, rows), 0)

    def body(lowest):
        place = place_ref[...]
        chosen = jnp.min(place, axis=0, keepdims=True)
        hit = place == chosen
        amount = jnp.sum(jnp.where(hit, probs, 0.0), axis=0, keepdims=True)
        rest = jnp.where(hit, none, place)
        place_ref[...] = rest

        def one(i, carry):
            at = pl.ds(pl.multiple_of(i * step, step), step)
            out_ref[at] = jnp.where(index + i * step == chosen, amount, out_ref[at])
            return carry

        lax.fori_loop(0, 2 * entries // step, one, 0, unroll=2)
        return jnp.min(rest)

    lax.while_loop(lambda lowest: lowest < none, body, jnp.min(place))


def dense_target(gathered, firsts, width, kept, entries):
    rows = gathered.shape[0]
    at = width // (2 * kept)
    return pl.pallas_call(
        target_kernel,
        out_shape=jax.ShapeDtypeStruct((2 * entries, rows), jnp.float32),
        grid=(1,),
        in_specs=[
            pl.BlockSpec(memory_space=pltpu.SMEM),
            pl.BlockSpec((rows, 2 * kept), lambda i: (0, at)),
            pl.BlockSpec((rows, 2 * kept), lambda i: (0, at + 1)),
        ],
        out_specs=pl.BlockSpec((2 * entries, rows), lambda i: (0, 0)),
        scratch_shapes=[pltpu.VMEM((kept, rows), jnp.int32)],
        cost_estimate=pl.CostEstimate(flops=10000000, bytes_accessed=4000000, transcendentals=0),
        compiler_params=pltpu.CompilerParams(vmem_limit_bytes=8 * 1024 * 1024),
        name="target",
    )(firsts, gathered, gathered)


def logits_kernel(gathered_ref, own_ref, other_ref, exp_ref, stats_ref):
    entries, width = own_ref.shape
    tile = 1024
    dims = (((1,), (1,)), ((), ()))
    for start in range(0, width, tile):
        at = slice(start, start + tile)
        hidden = gathered_ref[:, at]
        for i, ref in enumerate((own_ref, other_ref)):
            part = lax.dot_general(ref[:, at], hidden, dims, preferred_element_type=jnp.float32)
            rows = slice(i * entries, (i + 1) * entries)
            exp_ref[rows] = part if start == 0 else exp_ref[rows] + part
    logits = exp_ref[...]
    top = jnp.max(logits, axis=0, keepdims=True)
    exponent = jnp.exp(logits - top)
    exp_ref[...] = exponent
    stats_ref[0:1] = top
    stats_ref[1:2] = jnp.sum(exponent, axis=0, keepdims=True)


def exponents(gathered, own_weight, other_weight):
    rows = gathered.shape[0]
    entries, width = own_weight.shape
    vmem = pl.BlockSpec(memory_space=pltpu.VMEM)
    return pl.pallas_call(
        logits_kernel,
        out_shape=(
            jax.ShapeDtypeStruct((2 * entries, rows), jnp.float32),
            jax.ShapeDtypeStruct((2, rows), jnp.float32),
        ),
        in_specs=[vmem] * 3,
        out_specs=(vmem, vmem),
        compiler_params=pltpu.CompilerParams(vmem_limit_bytes=24 * 1024 * 1024),
        cost_estimate=pl.CostEstimate(
            flops=4 * entries * rows * width,
            bytes_accessed=4 * entries * width,
            transcendentals=2 * entries * rows,
        ),
        name="exponents",
    )(gathered, own_weight, other_weight)


def grad_kernel(
    stats_ref, local_ref, gathered_ref, exp_ref, target_ref, own_ref, other_ref,
    out_ref, own_grad_ref, other_grad_ref,
):
    entries, width = own_ref.shape
    tile = 512
    tops = stats_ref[:, 0, :]
    top = jnp.max(tops, axis=0, keepdims=True)
    total = jnp.sum(stats_ref[:, 1, :] * jnp.exp(tops - top), axis=0, keepdims=True)
    tail = gathered_ref[:, gathered_ref.shape[1] - 128 :]
    mass = jnp.sum(tail.astype(jnp.float32).T, axis=0, keepdims=True)
    scale = mass * jnp.exp(local_ref[0:1] - top) / total
    grad = (exp_ref[...] * scale - target_ref[...]).astype(jnp.bfloat16)
    own_grad_ref[...] = grad[:entries]
    other_grad_ref[...] = grad[entries:]
    own_turned = grad[:entries].T
    other_turned = grad[entries:].T
    for start in range(0, width, tile):
        at = slice(start, start + tile)
        out = jnp.dot(own_turned, own_ref[:, at], preferred_element_type=jnp.float32)
        out += jnp.dot(other_turned, other_ref[:, at], preferred_element_type=jnp.float32)
        out_ref[:, at] = out.astype(jnp.bfloat16)


def gradients(stats, local, gathered, exponent, target, own_weight, other_weight, kept):
    entries, width = own_weight.shape
    rows = gathered.shape[0]
    vmem = pl.BlockSpec(memory_space=pltpu.VMEM)
    return pl.pallas_call(
        grad_kernel,
        out_shape=(
            jax.ShapeDtypeStruct((rows, width), jnp.bfloat16),
            jax.ShapeDtypeStruct((entries, rows), jnp.bfloat16),
            jax.ShapeDtypeStruct((entries, rows), jnp.bfloat16),
        ),
        in_specs=[vmem] * 7,
        out_specs=(vmem,) * 3,
        compiler_params=pltpu.CompilerParams(vmem_limit_bytes=28 * 1024 * 1024),
        cost_estimate=pl.CostEstimate(
            flops=4 * entries * rows * width,
            bytes_accessed=4 * entries * width,
            transcendentals=0,
        ),
        name="gradients",
    )(stats, local, gathered, exponent, target, own_weight, other_weight)


def per_device(sizes, hidden_states, head_weight, teacher_ids, teacher_probs, row_weight):
    size_y, size_z, size_x, _ = sizes
    own_rows, width = hidden_states.shape
    entries = head_weight.shape[0]
    kept = teacher_ids.shape[1]
    group = size_z * own_rows
    rows = size_y * size_x * group
    core = lax.axis_index("core")
    device = lax.axis_index(AXES)
    place_x, place_y = lax.axis_index("x"), lax.axis_index("y")
    first_place = jnp.where(core == 0, place_x, place_y).astype(jnp.uint32)
    second_place = jnp.where(core == 0, place_y, place_x).astype(jnp.uint32)
    first_spots = [first_place ^ step for step in range(SIDE)]
    second_spots = [second_place ^ step for step in range(SIDE)]
    firsts = jnp.stack([device * entries, (device + 1 - 2 * core) * entries])
    other_weight = lax.ppermute(head_weight, "core", SWAP)

    with jax.named_scope("pack"):
        hidden_states, first_spots, second_spots, firsts = lax.optimization_barrier(
            (hidden_states, first_spots, second_spots, firsts)
        )
        packed = pack(hidden_states, teacher_ids, teacher_probs, row_weight, size_z)

    with jax.named_scope("gather"):
        across_z = lax.all_to_all(packed, "z", 0, 0, tiled=True).reshape(group, -1)
        gathered = gather_blocks(across_z, sizes, 0, first_spots)
        gathered = gather_blocks(gathered, sizes, 1, second_spots)
        hidden = gathered[:, :width]

    with jax.named_scope("target"):
        target = dense_target(gathered, firsts, width, kept, entries)

    with jax.named_scope("logits"):
        exponent, local = exponents(gathered, head_weight, other_weight)

    with jax.named_scope("stats"):
        local, target = lax.optimization_barrier((local, target))
        stats = spread(local, ("y", "z", "x"), size_y * size_z * size_x)
        stats = stats.reshape(-1, 2, rows)

    with jax.named_scope("grads"):
        partial, grad, other_grad = gradients(
            stats, local, gathered, exponent, target, head_weight, other_weight, kept
        )

    with jax.named_scope("scatter"):
        partial, other_grad = lax.optimization_barrier((partial, other_grad))
        pieces = scatter_blocks(partial, sizes, 1, second_spots)

    with jax.named_scope("grad_weight"):
        other_part = jnp.dot(other_grad, hidden, preferred_element_type=jnp.float32)
        other_part = other_part.astype(jnp.bfloat16)
        returned = lax.ppermute(other_part, "core", SWAP)

    with jax.named_scope("scatter"):
        pieces[0], other_part = lax.optimization_barrier((pieces[0], other_part))
        summed = total(pieces)
        summed, grad = lax.optimization_barrier((summed, grad))
        pieces = scatter_blocks(summed, sizes, 0, first_spots)

    with jax.named_scope("grad_weight"):
        own_part = jnp.dot(grad, hidden, preferred_element_type=jnp.float32)
        grad_weight = (own_part + returned.astype(jnp.float32)).astype(jnp.bfloat16)

    with jax.named_scope("scatter"):
        pieces[0], grad_weight = lax.optimization_barrier((pieces[0], grad_weight))
        summed = total(pieces).reshape(size_z, own_rows, width)
        pieces = lax.all_to_all(summed, "z", 0, 0, tiled=True)
        grad_hidden = jnp.sum(pieces.astype(jnp.float32), axis=0).astype(jnp.bfloat16)
    return grad_hidden, grad_weight


def solution(mesh):
    sizes = (4, 8, 4, 2)
    grid = Mesh(mesh.devices.reshape(sizes), AXES)
    in_specs = (P(AXES, None), P(AXES, None), P(AXES, None), P(AXES, None), P(AXES))
    out_specs = (P(AXES, None), P(AXES, None))

    def body(*args):
        return per_device(sizes, *args)

    return jax.shard_map(
        body, mesh=grid, in_specs=in_specs, out_specs=out_specs, check_vma=False
    )
```

time: 165 us -> 134 us (0.81)
  other arithmetic: 30.7 us -> 1.23 us
  matrix products: 25.6 us -> 6.22 us
  Pallas kernels: 0 us -> 17.8 us
  blocking collectives: 16 us -> 31.7 us
  starting transfers between devices: 34.3 us -> 25.3 us
  local copies, waits for them, and re-layouts: 6.97 us -> 1.14 us
    reduce_sum x3 -> x0, other arithmetic: 24.7 us -> none  [the longest x1 24.5 us: dense_target(): jnp.sum(jnp.where(matches, weighted_probs.T[:, None, :], jnp.float32(0.0)...]
    dot_general x4 -> x0, matrix products: 19.3 us -> none  [the longest x1 5.12 us: per_device(): jnp.einsum('vr,vd->rd', other_grad, other_weight, preferred_element_type=...]
    all_to_all x0 -> x1, blocking collectives: none -> 19.2 us  [spread(): return lax.all_to_all(copies, axes, 0, 0, tiled=True)]
    pallas_call x0 -> x4, Pallas kernels: none -> 17.8 us  [the longest x1 7.26 us: gradients(): pl.pallas_call(grad_kernel, out_shape=(jax.ShapeDtypeStruct((rows, width)...]
    all_to_all x2 -> x1, starting transfers between devices: 17.5 us -> 8.47 us  [per_device(): across_z = lax.all_to_all(packed, 'z', 0, 0, tiled=True).reshape(group, -1)]
    convert_element_type x5 -> x0, other arithmetic: 4.1 us -> none  [the longest x1 1.85 us: per_device(): (other_exponent * scale[None] - other_target).astype(jnp.bfloat16)]
    all_to_all x1, blocking collectives: 16 us -> 12.5 us  [per_device(): pieces = lax.all_to_all(summed, 'z', 0, 0, tiled=True)]
    all_to_all x2 -> x1, waiting for transfers between devices: 10 us -> 10 us  [per_device(): across_z = lax.all_to_all(packed, 'z', 0, 0, tiled=True).reshape(group, -1)]
  transfers between devices with their start and end apart: 16 -> 15, of which waited for: 8 -> 8; matrix products, arithmetic and copies ran while one was open for 23% -> 4% of each run, Pallas kernels for 0% -> 2%
where the time goes in v3:
time: 134 us; the launch traced here: 132 us
  waiting for transfers between devices  47.9 us (36%)
  blocking collectives  31.7 us (24%)
  starting transfers between devices  25.3 us (19%)
  Pallas kernels  17.8 us (13%)
  matrix products  6.22 us (5%)
    ppermute x12, waiting for transfers between devices, partner(): return lax.ppermute(block, AXES, pairs)  37.9 us
    all_to_all x1, blocking collectives, spread(): return lax.all_to_all(copies, axes, 0, 0, tiled=True)  19.2 us
    ppermute x12, starting transfers between devices, partner(): return lax.ppermute(block, AXES, pairs)  16.7 us
    all_to_all x1, blocking collectives, per_device(): pieces = lax.all_to_all(summed, 'z', 0, 0, tiled=True)  12.5 us
    all_to_all x1, waiting for transfers between devices, per_device(): across_z = lax.all_to_all(packed, 'z', 0, 0, tiled=True).reshape(group, -1)  10 us
    all_to_all x1, starting transfers between devices, per_device(): across_z = lax.all_to_all(packed, 'z', 0, 0, tiled=True).reshape(group, -1)  8.47 us
    pallas_call x1, Pallas kernels, gradients(): pl.pallas_call(grad_kernel, out_shape=(jax.ShapeDtypeStruct((rows, width)...  7.26 us
    pallas_call x1, Pallas kernels, exponents(): pl.pallas_call(logits_kernel, out_shape=(jax.ShapeDtypeStruct((2 * entrie...  6.37 us
  transfers between devices with their start and end apart: 15, of which 8 were waited for; matrix products, arithmetic and copies ran while one was open for 4% of the time, Pallas kernels for 2%

profile of v3, /device:TPU:24, one launch (start us, length us, event | category | flops | bytes accessed | tf_op | source)
XLA Modules:
  0.0 132.1 jit_solution(4461884455897761404)
XLA Ops:
  0.7 1.6 %pack.1 = bf16[8,2,5504]{2,1,0:T(2,128)(2,1)} custom-call(f32[2]{0:T(128)} %weight_ref.1, bf16[2,5120]{1,0:T(2,128)(2,1)} %hidden_ref, s32[2,64]{1,0:T(2,128)} %ids_ref.1, f32[2,64]{1,0:T(2,128)} %probs_ref.1), custom_call_target="tpu_custom_call" | custom-call | tf_op jit(solution)/shard_map/pack/pack/pallas_call | solution.py:102
  2.3 8.5 %all-to-all-start = ((bf16[8,2,5504]{2,1,0:T(2,128)(2,1)}), bf16[8,2,5504]{2,1,0:T(2,128)(2,1)S(1)}, u32[]{:S(2)}, u32[]{:S(2)}) async-start(bf16[8,2,5504]{2,1,0:T(2,128)(2,1)} %pack.1), calls=%async_computation | async-start | bytes 352256 | tf_op jit(solution)/shard_map/gather/all_to_all | solution.py:280
  10.8 10.0 %all-to-all-done = bf16[8,2,5504]{2,1,0:T(2,128)(2,1)S(1)} async-done(((bf16[8,2,5504]{2,1,0:T(2,128)(2,1)}), bf16[8,2,5504]{2,1,0:T(2,128)(2,1)S(1)}, u32[]{:S(2)}, u32[]{:S(2)}) %all-to-all-start) | async-done | bytes 176160 | tf_op jit(solution)/shard_map/gather/all_to_all | solution.py:280
  20.9 2.8 %collective-permute-start.2 = (bf16[16,5504]{1,0:T(8,128)(2,1)S(1)}, bf16[16,5504]{1,0:T(8,128)(2,1)S(1)}, u32[]{:S(2)}, u32[]{:S(2)}) collective-permute-start(bf16[16,5504]{1,0:T(8,128)(2,1)S(1)} %reshape.30), channel_id=1, source_target_pairs={{0,6},{1,193},{2,4},{3,195},{4,2},{5,197},{6,0},{7,199},{8,14},{9,... | collective-permute-start | bytes 528392 | tf_op jit(solution)/shard_map/gather/ppermute | solution.py:30
  25.2 5.6 %collective-permute-done = bf16[16,5504]{1,0:T(8,128)(2,1)S(1)} collective-permute-done((bf16[16,5504]{1,0:T(8,128)(2,1)S(1)}, bf16[16,5504]{1,0:T(8,128)(2,1)S(1)}, u32[]{:S(2)}, u32[]{:S(2)}) %collective-permute-start) | collective-permute-done | bytes 176160 | tf_op jit(solution)/shard_map/gather/ppermute | solution.py:30
  31.7 1.0 collective-permute-start.5
  32.7 2.3 %collective-permute-start.4 = (bf16[64,5504]{1,0:T(8,128)(2,1)S(1)}, bf16[64,5504]{1,0:T(8,128)(2,1)S(1)}, u32[]{:S(2)}, u32[]{:S(2)}) collective-permute-start(bf16[64,5504]{1,0:T(8,128)(2,1)S(1)} %bitcast.50), channel_id=1, source_target_pairs={{0,128},{1,5},{2,130},{3,7},{4,132},{5,1},{6,134},{7,3},{8,136},{9... | collective-permute-start | bytes 2113544 | tf_op jit(solution)/shard_map/gather/ppermute | solution.py:30
  35.3 6.7 %collective-permute-done.3 = bf16[64,5504]{1,0:T(8,128)(2,1)S(1)} collective-permute-done((bf16[64,5504]{1,0:T(8,128)(2,1)S(1)}, bf16[64,5504]{1,0:T(8,128)(2,1)S(1)}, u32[]{:S(2)}, u32[]{:S(2)}) %collective-permute-start.3) | collective-permute-done | bytes 704544 | tf_op jit(solution)/shard_map/gather/ppermute | solution.py:30
  42.1 7.1 %collective-permute-done.4 = bf16[64,5504]{1,0:T(8,128)(2,1)S(1)} collective-permute-done((bf16[64,5504]{1,0:T(8,128)(2,1)S(1)}, bf16[64,5504]{1,0:T(8,128)(2,1)S(1)}, u32[]{:S(2)}, u32[]{:S(2)}) %collective-permute-start.4) | collective-permute-done | bytes 704544 | tf_op jit(solution)/shard_map/gather/ppermute | solution.py:30
  49.3 2.3 %collective-permute-done.5 = bf16[64,5504]{1,0:T(8,128)(2,1)S(1)} collective-permute-done((bf16[64,5504]{1,0:T(8,128)(2,1)S(1)}, bf16[64,5504]{1,0:T(8,128)(2,1)S(1)}, u32[]{:S(2)}, u32[]{:S(2)}) %collective-permute-start.5) | collective-permute-done | bytes 704544 | tf_op jit(solution)/shard_map/gather/ppermute | solution.py:30
  51.7 2.6 %target.1.target_ref = f32[1184,256]{1,0:T(8,128)S(1)} custom-call(s32[2]{0:T(128)S(1)} %pad_add_fusion.first_ref, bf16[256,5504]{1,0:T(8,128)(2,1)S(1)} %bitcast.39, bf16[256,5504]{1,0:T(8,128)(2,1)S(1)} %bitcast.40), custom_call_target="tpu_custom_call" | custom-call | flops 10000000 | bytes 4000000 | tf_op jit(solution)/shard_map/target/target/pallas_call | solution.py:151
  54.3 6.4 %exponents.1 = (f32[1184,256]{1,0:T(8,128)S(1)}, f32[2,256]{1,0:T(2,128)S(1)}) custom-call(bf16[256,5504]{1,0:T(8,128)(2,1)S(1)} %bitcast.41, bf16[592,5120]{1,0:T(8,128)(2,1)S(1)} %bitcast.46, bf16[592,5120]{1,0:T(8,128)(2,1)} %collective-permute-done.6.other_ref), custom_call_target="tpu_custom_call" | custom-call | flops 3103784960 | bytes 12124160 | tf_op jit(solution)/shard_map/logits/exponents/pallas_call | solution.py:191
  60.8 19.2 %all_to_all.15.stats_ref = f32[128,2,256]{2,1,0:T(2,128)S(1)} all-to-all(f32[128,2,256]{2,1,0:T(2,128)S(1)} %broadcast_in_dim.38), channel_id=1, replica_groups=mesh['y'=4,'z'=8,'x'=4,'core'=2] {'y','z','x'}, dimensions={0} | all-to-all | bytes 524288 | tf_op jit(solution)/shard_map/stats/all_to_all | solution.py:19
  80.0 7.3 %gradients.1 = (bf16[256,5120]{1,0:T(8,128)(2,1)S(1)}, bf16[592,256]{1,0:T(8,128)(2,1)S(1)}, bf16[592,256]{1,0:T(8,128)(2,1)S(1)}) custom-call(f32[128,2,256]{2,1,0:T(2,128)S(1)} %all_to_all.15.stats_ref, f32[2,256]{1,0:T(2,128)S(1)} %get-tuple-element.37.local_ref, bf16[256,5504]{1,0:T(8,128)(2,1)S(1)} %bitcast.42, ...), custom_call_target="tpu_custom_call" | custom-call | flops 3103784960 | bytes 12124160 | tf_op jit(solution)/shard_map/grads/gradients/pallas_call | solution.py:237
  87.3 1.8 %convolution_convert_fusion = bf16[592,5120]{1,0:T(8,128)(2,1)S(1)} fusion(bf16[592,256]{1,0:T(8,128)(2,1)S(1)} %get-tuple-element.43, bf16[256,5504]{1,0:T(8,128)(2,1)S(1)} %bitcast.43), kind=kOutput, calls=%fused_computation.1 | convolution fusion | flops 1554923520 | bytes 8986624 | tf_op jit(solution)/shard_map/grad_weight/dot_general | solution.py:306
  89.3 2.7 %collective-permute-start.9 = (bf16[64,5120]{1,0:T(8,128)(2,1)S(1)}, bf16[64,5120]{1,0:T(8,128)(2,1)S(1)}, u32[]{:S(2)}, u32[]{:S(2)}) collective-permute-start(bf16[64,5120]{1,0:T(8,128)(2,1)S(1)} %get-tuple-element.51), channel_id=1, source_target_pairs={{0,192},{1,7},{2,194},{3,5},{4,196},{5,3},{6,198},{7,1},{8,200},{9... | collective-permute-start | bytes 1966088 | tf_op jit(solution)/shard_map/scatter/ppermute | solution.py:30
  92.0 1.2 collective-permute-start.8
  93.5 14.7 %collective-permute-done.9 = bf16[64,5120]{1,0:T(8,128)(2,1)S(1)} collective-permute-done((bf16[64,5120]{1,0:T(8,128)(2,1)S(1)}, bf16[64,5120]{1,0:T(8,128)(2,1)S(1)}, u32[]{:S(2)}, u32[]{:S(2)}) %collective-permute-start.9) | collective-permute-done | bytes 655392 | tf_op jit(solution)/shard_map/scatter/ppermute | solution.py:30
  108.2 0.9 collective-permute-done.7
  109.5 1.4 %collective-permute-start.13 = (bf16[16,5120]{1,0:T(8,128)(2,1)S(1)}, bf16[16,5120]{1,0:T(8,128)(2,1)S(1)}, u32[]{:S(2)}, u32[]{:S(2)}) collective-permute-start(bf16[16,5120]{1,0:T(8,128)(2,1)S(1)} %get-tuple-element.55), channel_id=1, source_target_pairs={{0,6},{1,193},{2,4},{3,195},{4,2},{5,197},{6,0},{7,199},{8,14},{9,... | collective-permute-start | bytes 491528 | tf_op jit(solution)/shard_map/scatter/ppermute | solution.py:30
  111.0 1.4 %collective-permute-start.12 = (bf16[16,5120]{1,0:T(8,128)(2,1)S(1)}, bf16[16,5120]{1,0:T(8,128)(2,1)S(1)}, u32[]{:S(2)}, u32[]{:S(2)}) collective-permute-start(bf16[16,5120]{1,0:T(8,128)(2,1)S(1)} %get-tuple-element.56), channel_id=1, source_target_pairs={{0,4},{1,129},{2,6},{3,131},{4,0},{5,133},{6,2},{7,135},{8,12},{9,... | collective-permute-start | bytes 491528 | tf_op jit(solution)/shard_map/scatter/ppermute | solution.py:30
  112.4 1.3 collective-permute-start.11
  113.7 4.5 %add_convert_fusion = bf16[592,5120]{1,0:T(8,128)(2,1)} fusion(bf16[592,5120]{1,0:T(8,128)(2,1)S(1)} %collective-permute-done.10, bf16[592,256]{1,0:T(8,128)(2,1)S(1)} %get-tuple-element.47, bf16[256,5504]{1,0:T(8,128)(2,1)S(1)} %bitcast.44), kind=kOutput, calls=%fused_computation | convolution fusion | flops 1560985600 | bytes 15048704 | tf_op jit(solution)/shard_map/grad_weight/dot_general | solution.py:317
  118.9 12.5 %all_to_all.16 = bf16[8,2,5120]{2,1,0:T(2,128)(2,1)S(1)} all-to-all(bf16[8,2,5120]{2,1,0:T(2,128)(2,1)S(1)} %reshape.36), channel_id=1, replica_groups=mesh['y'=4,'z'=8,'x'=4,'core'=2] {'z'}, dimensions={0} | all-to-all | bytes 327680 | tf_op jit(solution)/shard_map/scatter/all_to_all | solution.py:323
  (39 shorter events, 5.6 us)
Async XLA Ops:
  2.3 18.5 %all-to-all-start = ((bf16[8,2,5504]{2,1,0:T(2,128)(2,1)}), bf16[8,2,5504]{2,1,0:T(2,128)(2,1)S(1)}, u32[]{:S(2)}, u32[]{:S(2)}) async-start(bf16[8,2,5504]{2,1,0:T(2,128)(2,1)} %pack.1), calls=%async_computation | async-start | bytes 352256 | tf_op jit(solution)/shard_map/gather/all_to_all | solution.py:280
  10.8 43.5 %collective-permute-start.6 = (bf16[592,5120]{1,0:T(8,128)(2,1)}, bf16[592,5120]{1,0:T(8,128)(2,1)}, u32[]{:S(2)}, u32[]{:S(2)}) collective-permute-start(bf16[592,5120]{1,0:T(8,128)(2,1)} %own_ref.3), channel_id=1, source_target_pairs={{0,1},{1,0},{2,3},{3,2},{4,5},{5,4},{6,7},{7,6},{8,9},{9,8},{10,11... | collective-permute-start | bytes 18186248 | tf_op jit(solution)/shard_map/ppermute | solution.py:271
  20.9 10.0 %collective-permute-start.2 = (bf16[16,5504]{1,0:T(8,128)(2,1)S(1)}, bf16[16,5504]{1,0:T(8,128)(2,1)S(1)}, u32[]{:S(2)}, u32[]{:S(2)}) collective-permute-start(bf16[16,5504]{1,0:T(8,128)(2,1)S(1)} %reshape.30), channel_id=1, source_target_pairs={{0,6},{1,193},{2,4},{3,195},{4,2},{5,197},{6,0},{7,199},{8,14},{9,... | collective-permute-start | bytes 528392 | tf_op jit(solution)/shard_map/gather/ppermute | solution.py:30
  23.7 7.1 %collective-permute-start.1 = (bf16[16,5504]{1,0:T(8,128)(2,1)S(1)}, bf16[16,5504]{1,0:T(8,128)(2,1)S(1)}, u32[]{:S(2)}, u32[]{:S(2)}) collective-permute-start(bf16[16,5504]{1,0:T(8,128)(2,1)S(1)} %reshape.30), channel_id=1, source_target_pairs={{0,4},{1,129},{2,6},{3,131},{4,0},{5,133},{6,2},{7,135},{8,12},{9,... | collective-permute-start | bytes 528392 | tf_op jit(solution)/shard_map/gather/ppermute | solution.py:30
  24.5 6.3 %collective-permute-start = (bf16[16,5504]{1,0:T(8,128)(2,1)S(1)}, bf16[16,5504]{1,0:T(8,128)(2,1)S(1)}, u32[]{:S(2)}, u32[]{:S(2)}) collective-permute-start(bf16[16,5504]{1,0:T(8,128)(2,1)S(1)} %reshape.30), channel_id=1, source_target_pairs={{0,2},{1,65},{2,0},{3,67},{4,6},{5,69},{6,4},{7,71},{8,10},{9,73},... | collective-permute-start | bytes 528392 | tf_op jit(solution)/shard_map/gather/ppermute | solution.py:30
  30.9 11.2 %collective-permute-start.3 = (bf16[64,5504]{1,0:T(8,128)(2,1)S(1)}, bf16[64,5504]{1,0:T(8,128)(2,1)S(1)}, u32[]{:S(2)}, u32[]{:S(2)}) collective-permute-start(bf16[64,5504]{1,0:T(8,128)(2,1)S(1)} %bitcast.48), channel_id=1, source_target_pairs={{0,64},{1,3},{2,66},{3,1},{4,68},{5,7},{6,70},{7,5},{8,72},{9,11},... | collective-permute-start | bytes 2113544 | tf_op jit(solution)/shard_map/gather/ppermute | solution.py:30
  31.7 19.9 %collective-permute-start.5 = (bf16[64,5504]{1,0:T(8,128)(2,1)S(1)}, bf16[64,5504]{1,0:T(8,128)(2,1)S(1)}, u32[]{:S(2)}, u32[]{:S(2)}) collective-permute-start(bf16[64,5504]{1,0:T(8,128)(2,1)S(1)} %bitcast.49), channel_id=1, source_target_pairs={{0,192},{1,7},{2,194},{3,5},{4,196},{5,3},{6,198},{7,1},{8,200},{9... | collective-permute-start | bytes 2113544 | tf_op jit(solution)/shard_map/gather/ppermute | solution.py:30
  32.7 16.5 %collective-permute-start.4 = (bf16[64,5504]{1,0:T(8,128)(2,1)S(1)}, bf16[64,5504]{1,0:T(8,128)(2,1)S(1)}, u32[]{:S(2)}, u32[]{:S(2)}) collective-permute-start(bf16[64,5504]{1,0:T(8,128)(2,1)S(1)} %bitcast.50), channel_id=1, source_target_pairs={{0,128},{1,5},{2,130},{3,7},{4,132},{5,1},{6,134},{7,3},{8,136},{9... | collective-permute-start | bytes 2113544 | tf_op jit(solution)/shard_map/gather/ppermute | solution.py:30
  35.1 19.2 %slice-start = ((s8[6062080]{0:T(1024)(128)(4,1)}), s8[4194304]{0:T(1024)(128)(4,1)S(1)}, s32[]{:S(2)}) async-start(s8[6062080]{0:T(1024)(128)(4,1)} %bitcast.45), calls=%async_computation.3 | async-start | bytes 8388608
  49.3 5.0 %slice-start.1 = ((s8[6062080]{0:T(1024)(128)(4,1)}), s8[1867776]{0:T(1024)(128)(4,1)S(1)}, s32[]{:S(2)}) async-start(s8[6062080]{0:T(1024)(128)(4,1)} %bitcast.45), calls=%async_computation.4 | async-start | bytes 3735552
  89.0 24.7 %collective-permute-start.10 = (bf16[592,5120]{1,0:T(8,128)(2,1)S(1)}, bf16[592,5120]{1,0:T(8,128)(2,1)S(1)}, u32[]{:S(2)}, u32[]{:S(2)}) collective-permute-start(bf16[592,5120]{1,0:T(8,128)(2,1)S(1)} %convolution_convert_fusion), channel_id=1, source_target_pairs={{0,1},{1,0},{2,3},{3,2},{4,5},{5,4},{6,7},{7,6},{8,9},{9,8},{10,11... | collective-permute-start | bytes 18186248 | tf_op jit(solution)/shard_map/grad_weight/ppermute | solution.py:308
  89.3 18.9 %collective-permute-start.9 = (bf16[64,5120]{1,0:T(8,128)(2,1)S(1)}, bf16[64,5120]{1,0:T(8,128)(2,1)S(1)}, u32[]{:S(2)}, u32[]{:S(2)}) collective-permute-start(bf16[64,5120]{1,0:T(8,128)(2,1)S(1)} %get-tuple-element.51), channel_id=1, source_target_pairs={{0,192},{1,7},{2,194},{3,5},{4,196},{5,3},{6,198},{7,1},{8,200},{9... | collective-permute-start | bytes 1966088 | tf_op jit(solution)/shard_map/scatter/ppermute | solution.py:30
  92.0 16.2 %collective-permute-start.8 = (bf16[64,5120]{1,0:T(8,128)(2,1)S(1)}, bf16[64,5120]{1,0:T(8,128)(2,1)S(1)}, u32[]{:S(2)}, u32[]{:S(2)}) collective-permute-start(bf16[64,5120]{1,0:T(8,128)(2,1)S(1)} %get-tuple-element.52), channel_id=1, source_target_pairs={{0,128},{1,5},{2,130},{3,7},{4,132},{5,1},{6,134},{7,3},{8,136},{9... | collective-permute-start | bytes 1966088 | tf_op jit(solution)/shard_map/scatter/ppermute | solution.py:30
  93.2 15.9 %collective-permute-start.7 = (bf16[64,5120]{1,0:T(8,128)(2,1)S(1)}, bf16[64,5120]{1,0:T(8,128)(2,1)S(1)}, u32[]{:S(2)}, u32[]{:S(2)}) collective-permute-start(bf16[64,5120]{1,0:T(8,128)(2,1)S(1)} %get-tuple-element.53), channel_id=1, source_target_pairs={{0,64},{1,3},{2,66},{3,1},{4,68},{5,7},{6,70},{7,5},{8,72},{9,11},... | collective-permute-start | bytes 1966088 | tf_op jit(solution)/shard_map/scatter/ppermute | solution.py:30
  109.5 8.6 %collective-permute-start.13 = (bf16[16,5120]{1,0:T(8,128)(2,1)S(1)}, bf16[16,5120]{1,0:T(8,128)(2,1)S(1)}, u32[]{:S(2)}, u32[]{:S(2)}) collective-permute-start(bf16[16,5120]{1,0:T(8,128)(2,1)S(1)} %get-tuple-element.55), channel_id=1, source_target_pairs={{0,6},{1,193},{2,4},{3,195},{4,2},{5,197},{6,0},{7,199},{8,14},{9,... | collective-permute-start | bytes 491528 | tf_op jit(solution)/shard_map/scatter/ppermute | solution.py:30
  111.0 7.2 %collective-permute-start.12 = (bf16[16,5120]{1,0:T(8,128)(2,1)S(1)}, bf16[16,5120]{1,0:T(8,128)(2,1)S(1)}, u32[]{:S(2)}, u32[]{:S(2)}) collective-permute-start(bf16[16,5120]{1,0:T(8,128)(2,1)S(1)} %get-tuple-element.56), channel_id=1, source_target_pairs={{0,4},{1,129},{2,6},{3,131},{4,0},{5,133},{6,2},{7,135},{8,12},{9,... | collective-permute-start | bytes 491528 | tf_op jit(solution)/shard_map/scatter/ppermute | solution.py:30
  112.4 6.3 %collective-permute-start.11 = (bf16[16,5120]{1,0:T(8,128)(2,1)S(1)}, bf16[16,5120]{1,0:T(8,128)(2,1)S(1)}, u32[]{:S(2)}, u32[]{:S(2)}) collective-permute-start(bf16[16,5120]{1,0:T(8,128)(2,1)S(1)} %get-tuple-element.57), channel_id=1, source_target_pairs={{0,2},{1,65},{2,0},{3,67},{4,6},{5,69},{6,4},{7,71},{8,10},{9,73},... | collective-permute-start | bytes 491528 | tf_op jit(solution)/shard_map/scatter/ppermute | solution.py:30

commit v4 on v3

--- a/solution.py
+++ b/solution.py
@@ -9,6 +9,7 @@
 AXES = ("y", "z", "x", "core")
 SWAP = [(0, 1), (1, 0)]
 SIDE = 4
+STEPS = (0, 2, 1, 3)
 DIGIT = 512
 HALF = 256
 ID_SHIFT = 148
@@ -30,20 +31,24 @@
     return lax.ppermute(block, AXES, pairs)
 
 
-def gather_blocks(block, sizes, leg, spots):
+def gather_blocks(block, sizes, leg, spots, beside=None):
+    own = block
+    if beside is not None:
+        own, beside = lax.optimization_barrier((own, beside))
     result = jnp.zeros((SIDE,) + block.shape, block.dtype)
-    for step in range(SIDE):
-        piece = partner(block, sizes, leg, step) if step else block
+    pieces = {step: partner(block, sizes, leg, step) for step in STEPS[1:]}
+    pieces[0] = own
+    for step in STEPS:
         result = lax.dynamic_update_slice(
-            result, piece[None], (spots[step],) + (jnp.uint32(0),) * block.ndim
+            result, pieces[step][None], (spots[step],) + (jnp.uint32(0),) * block.ndim
         )
-    return result.reshape((-1,) + block.shape[1:])
+    return result.reshape((-1,) + block.shape[1:]), beside
 
 
 def scatter_blocks(values, sizes, leg, spots):
     values = values.reshape((SIDE, -1) + values.shape[1:])
     pieces = []
-    for step in range(SIDE):
+    for step in STEPS:
         start = (spots[step],) + (jnp.uint32(0),) * (values.ndim - 1)
         piece = lax.dynamic_slice(values, start, (1,) + values.shape[1:])[0]
         pieces.append(partner(piece, sizes, leg, step) if step else piece)
@@ -120,29 +125,35 @@
     none = jnp.int32(4 * entries)
     place = jnp.where((other >= 0) & (other < entries), other + entries, none)
     place = jnp.where((own >= 0) & (own < entries), own, place)
-    place_ref[...] = place
-    out_ref[...] = jnp.zeros_like(out_ref)
     rows = out_ref.shape[1]
     step = 16
     index = lax.broadcasted_iota(jnp.int32, (step, rows), 0)
 
-    def body(lowest):
-        place = place_ref[...]
+    def take(place):
         chosen = jnp.min(place, axis=0, keepdims=True)
         hit = place == chosen
         amount = jnp.sum(jnp.where(hit, probs, 0.0), axis=0, keepdims=True)
-        rest = jnp.where(hit, none, place)
-        place_ref[...] = rest
+        return chosen, amount, jnp.where(hit, none, place)
+
+    def put(place, fresh):
+        chosen, amount, place = take(place)
+        second, second_amount, place = take(place)
+        place_ref[...] = place
 
         def one(i, carry):
             at = pl.ds(pl.multiple_of(i * step, step), step)
-            out_ref[at] = jnp.where(index + i * step == chosen, amount, out_ref[at])
+            here = index + i * step
+            value = jnp.zeros((step, rows), jnp.float32) if fresh else out_ref[at]
+            value = jnp.where(here == chosen, amount, value)
+            out_ref[at] = jnp.where(here == second, second_amount, value)
             return carry
 
         lax.fori_loop(0, 2 * entries // step, one, 0, unroll=2)
-        return jnp.min(rest)
-
-    lax.while_loop(lambda lowest: lowest < none, body, jnp.min(place))
+        return jnp.min(place)
+
+    lax.while_loop(
+        lambda lowest: lowest < none, lambda lowest: put(place_ref[...], False), put(place, True)
+    )
 
 
 def dense_target(gathered, firsts, width, kept, entries):
@@ -165,17 +176,16 @@
     )(firsts, gathered, gathered)
 
 
-def logits_kernel(gathered_ref, own_ref, other_ref, exp_ref, stats_ref):
-    entries, width = own_ref.shape
+def logits_kernel(gathered_ref, weights_ref, exp_ref, stats_ref):
+    width = weights_ref.shape[1]
     tile = 1024
     dims = (((1,), (1,)), ((), ()))
     for start in range(0, width, tile):
         at = slice(start, start + tile)
-        hidden = gathered_ref[:, at]
-        for i, ref in enumerate((own_ref, other_ref)):
-            part = lax.dot_general(ref[:, at], hidden, dims, preferred_element_type=jnp.float32)
-            rows = slice(i * entries, (i + 1) * entries)
-            exp_ref[rows] = part if start == 0 else exp_ref[rows] + part
+        part = lax.dot_general(
+            weights_ref[:, at], gathered_ref[:, at], dims, preferred_element_type=jnp.float32
+        )
+        exp_ref[...] = part if start == 0 else exp_ref[...] + part
     logits = exp_ref[...]
     top = jnp.max(logits, axis=0, keepdims=True)
     exponent = jnp.exp(logits - top)
@@ -184,33 +194,33 @@
     stats_ref[1:2] = jnp.sum(exponent, axis=0, keepdims=True)
 
 
-def exponents(gathered, own_weight, other_weight):
+def exponents(gathered, weights):
     rows = gathered.shape[0]
-    entries, width = own_weight.shape
+    entries, width = weights.shape
     vmem = pl.BlockSpec(memory_space=pltpu.VMEM)
     return pl.pallas_call(
         logits_kernel,
         out_shape=(
-            jax.ShapeDtypeStruct((2 * entries, rows), jnp.float32),
+            jax.ShapeDtypeStruct((entries, rows), jnp.float32),
             jax.ShapeDtypeStruct((2, rows), jnp.float32),
         ),
-        in_specs=[vmem] * 3,
+        in_specs=[vmem] * 2,
         out_specs=(vmem, vmem),
         compiler_params=pltpu.CompilerParams(vmem_limit_bytes=24 * 1024 * 1024),
         cost_estimate=pl.CostEstimate(
-            flops=4 * entries * rows * width,
-            bytes_accessed=4 * entries * width,
-            transcendentals=2 * entries * rows,
+            flops=2 * entries * rows * width,
+            bytes_accessed=2 * entries * width,
+            transcendentals=entries * rows,
         ),
         name="exponents",
-    )(gathered, own_weight, other_weight)
+    )(gathered, weights)
 
 
 def grad_kernel(
-    stats_ref, local_ref, gathered_ref, exp_ref, target_ref, own_ref, other_ref,
+    stats_ref, local_ref, gathered_ref, exp_ref, target_ref, weights_ref,
     out_ref, own_grad_ref, other_grad_ref,
 ):
-    entries, width = own_ref.shape
+    entries, width = weights_ref.shape
     tile = 512
     tops = stats_ref[:, 0, :]
     top = jnp.max(tops, axis=0, keepdims=True)
@@ -219,38 +229,36 @@
     mass = jnp.sum(tail.astype(jnp.float32).T, axis=0, keepdims=True)
     scale = mass * jnp.exp(local_ref[0:1] - top) / total
     grad = (exp_ref[...] * scale - target_ref[...]).astype(jnp.bfloat16)
-    own_grad_ref[...] = grad[:entries]
-    other_grad_ref[...] = grad[entries:]
-    own_turned = grad[:entries].T
-    other_turned = grad[entries:].T
+    own_grad_ref[...] = grad[: entries // 2]
+    other_grad_ref[...] = grad[entries // 2 :]
+    turned = grad.T
     for start in range(0, width, tile):
         at = slice(start, start + tile)
-        out = jnp.dot(own_turned, own_ref[:, at], preferred_element_type=jnp.float32)
-        out += jnp.dot(other_turned, other_ref[:, at], preferred_element_type=jnp.float32)
+        out = jnp.dot(turned, weights_ref[:, at], preferred_element_type=jnp.float32)
         out_ref[:, at] = out.astype(jnp.bfloat16)
 
 
-def gradients(stats, local, gathered, exponent, target, own_weight, other_weight, kept):
-    entries, width = own_weight.shape
+def gradients(stats, local, gathered, exponent, target, weights):
+    entries, width = weights.shape
     rows = gathered.shape[0]
     vmem = pl.BlockSpec(memory_space=pltpu.VMEM)
     return pl.pallas_call(
         grad_kernel,
         out_shape=(
             jax.ShapeDtypeStruct((rows, width), jnp.bfloat16),
-            jax.ShapeDtypeStruct((entries, rows), jnp.bfloat16),
-            jax.ShapeDtypeStruct((entries, rows), jnp.bfloat16),
+            jax.ShapeDtypeStruct((entries // 2, rows), jnp.bfloat16),
+            jax.ShapeDtypeStruct((entries // 2, rows), jnp.bfloat16),
         ),
-        in_specs=[vmem] * 7,
+        in_specs=[vmem] * 6,
         out_specs=(vmem,) * 3,
         compiler_params=pltpu.CompilerParams(vmem_limit_bytes=28 * 1024 * 1024),
         cost_estimate=pl.CostEstimate(
-            flops=4 * entries * rows * width,
-            bytes_accessed=4 * entries * width,
+            flops=2 * entries * rows * width,
+            bytes_accessed=2 * entries * width,
             transcendentals=0,
         ),
         name="gradients",
-    )(stats, local, gathered, exponent, target, own_weight, other_weight)
+    )(stats, local, gathered, exponent, target, weights)
 
 
 def per_device(sizes, hidden_states, head_weight, teacher_ids, teacher_probs, row_weight):
@@ -278,15 +286,17 @@
 
     with jax.named_scope("gather"):
         across_z = lax.all_to_all(packed, "z", 0, 0, tiled=True).reshape(group, -1)
-        gathered = gather_blocks(across_z, sizes, 0, first_spots)
-        gathered = gather_blocks(gathered, sizes, 1, second_spots)
+        gathered, _ = gather_blocks(across_z, sizes, 0, first_spots)
+        gathered, other_weight = lax.optimization_barrier((gathered, other_weight))
+        weights = jnp.concatenate([head_weight, other_weight], axis=0)
+        gathered, weights = gather_blocks(gathered, sizes, 1, second_spots, weights)
         hidden = gathered[:, :width]
 
     with jax.named_scope("target"):
         target = dense_target(gathered, firsts, width, kept, entries)
 
     with jax.named_scope("logits"):
-        exponent, local = exponents(gathered, head_weight, other_weight)
+        exponent, local = exponents(gathered, weights)
 
     with jax.named_scope("stats"):
         local, target = lax.optimization_barrier((local, target))
@@ -295,7 +305,7 @@
 
     with jax.named_scope("grads"):
         partial, grad, other_grad = gradients(
-            stats, local, gathered, exponent, target, head_weight, other_weight, kept
+            stats, local, gathered, exponent, target, weights
         )
 
     with jax.named_scope("scatter"):

time: 134 us -> 126 us (0.940)
  blocking collectives: 31.7 us -> 50.4 us
  waiting for transfers between devices: 47.9 us -> 29.6 us
  starting transfers between devices: 25.3 us -> 17 us
  Pallas kernels: 17.8 us -> 10.3 us
  other arithmetic: 1.23 us -> 8.12 us
    all_to_all x0 -> x1, blocking collectives: none -> 19.1 us  [per_device(): across_z = lax.all_to_all(packed, 'z', 0, 0, tiled=True).reshape(group, -1)]
    all_to_all x1 -> x0, waiting for transfers between devices: 10 us -> none  [per_device(): across_z = lax.all_to_all(packed, 'z', 0, 0, tiled=True).reshape(group, -1)]
    all_to_all x1 -> x0, starting transfers between devices: 8.47 us -> none  [per_device(): across_z = lax.all_to_all(packed, 'z', 0, 0, tiled=True).reshape(group, -1)]
    ppermute x12, waiting for transfers between devices: 37.9 us -> 29.6 us  [partner(): return lax.ppermute(block, AXES, pairs)]
    concatenate x0 -> x1, other arithmetic: none -> 6.88 us  [per_device(): weights = jnp.concatenate([head_weight, other_weight], axis=0)]
    pallas_call x1, Pallas kernels: 7.26 us -> 3.9 us  [gradients(): pl.pallas_call(grad_kernel, out_shape=(jax.ShapeDtypeStruct((rows, width)...]
    pallas_call x1, Pallas kernels: 6.37 us -> 3.69 us  [exponents(): pl.pallas_call(logits_kernel, out_shape=(jax.ShapeDtypeStruct((entries, r...]
    pallas_call x1, Pallas kernels: 2.61 us -> 1.19 us  [dense_target(): pl.pallas_call(target_kernel, out_shape=jax.ShapeDtypeStruct((2 * entries...]
  transfers between devices with their start and end apart: 15 -> 14, of which waited for: 8 -> 8; matrix products, arithmetic and copies ran while one was open for 4% -> 10% of each run, Pallas kernels for 2% -> 1%
where the time goes in v4:
time: 126 us; the launch traced here: 124 us
  blocking collectives  50.4 us (40%)
  waiting for transfers between devices  29.6 us (23%)
  starting transfers between devices  17 us (13%)
  Pallas kernels  10.3 us (8%)
  other arithmetic  8.12 us (6%)
  matrix products  6.21 us (5%)
    ppermute x12, waiting for transfers between devices, partner(): return lax.ppermute(block, AXES, pairs)  29.6 us
    all_to_all x1, blocking collectives, per_device(): across_z = lax.all_to_all(packed, 'z', 0, 0, tiled=True).reshape(group, -1)  19.1 us
    all_to_all x1, blocking collectives, spread(): return lax.all_to_all(copies, axes, 0, 0, tiled=True)  19 us
    ppermute x12, starting transfers between devices, partner(): return lax.ppermute(block, AXES, pairs)  16.9 us
    all_to_all x1, blocking collectives, per_device(): pieces = lax.all_to_all(summed, 'z', 0, 0, tiled=True)  12.2 us
    concatenate x1, other arithmetic, per_device(): weights = jnp.concatenate([head_weight, other_weight], axis=0)  6.88 us
    dot_general x1, matrix products, per_device(): own_part = jnp.dot(grad, hidden, preferred_element_type=jnp.float32)  4.46 us
    pallas_call x1, Pallas kernels, gradients(): pl.pallas_call(grad_kernel, out_shape=(jax.ShapeDtypeStruct((rows, width)...  3.9 us
  transfers between devices with their start and end apart: 14, of which 8 were waited for; matrix products, arithmetic and copies ran while one was open for 10% of the time, Pallas kernels for 1%

profile of v4, /device:TPU:24, one launch (start us, length us, event | category | flops | bytes accessed | tf_op | source)
XLA Modules:
  0.0 123.7 jit_solution(9953159433776830299)
XLA Ops:
  0.8 1.6 %pack.1 = bf16[8,2,5504]{2,1,0:T(2,128)(2,1)} custom-call(f32[2]{0:T(128)} %weight_ref.1, bf16[2,5120]{1,0:T(2,128)(2,1)} %hidden_ref, s32[2,64]{1,0:T(2,128)} %ids_ref.1, f32[2,64]{1,0:T(2,128)} %probs_ref.1), custom_call_target="tpu_custom_call" | custom-call | tf_op jit(solution)/shard_map/pack/pack/pallas_call | solution.py:107
  2.4 19.1 %all_to_all.15 = bf16[8,2,5504]{2,1,0:T(2,128)(2,1)S(1)} all-to-all(bf16[8,2,5504]{2,1,0:T(2,128)(2,1)} %pack.1), channel_id=1, replica_groups=mesh['y'=4,'z'=8,'x'=4,'core'=2] {'z'}, dimensions={0} | all-to-all | bytes 352256 | tf_op jit(solution)/shard_map/gather/all_to_all | solution.py:288
  21.6 3.1 %collective-permute-start = (bf16[16,5504]{1,0:T(8,128)(2,1)S(1)}, bf16[16,5504]{1,0:T(8,128)(2,1)S(1)}, u32[]{:S(2)}, u32[]{:S(2)}) collective-permute-start(bf16[16,5504]{1,0:T(8,128)(2,1)S(1)} %reshape.27), channel_id=1, source_target_pairs={{0,4},{1,129},{2,6},{3,131},{4,0},{5,133},{6,2},{7,135},{8,12},{9,... | collective-permute-start | bytes 528392 | tf_op jit(solution)/shard_map/gather/ppermute | solution.py:31
  26.0 2.6 %collective-permute-done = bf16[16,5504]{1,0:T(8,128)(2,1)S(1)} collective-permute-done((bf16[16,5504]{1,0:T(8,128)(2,1)S(1)}, bf16[16,5504]{1,0:T(8,128)(2,1)S(1)}, u32[]{:S(2)}, u32[]{:S(2)}) %collective-permute-start) | collective-permute-done | bytes 176160 | tf_op jit(solution)/shard_map/gather/ppermute | solution.py:31
  28.7 2.0 %collective-permute-done.1 = bf16[16,5504]{1,0:T(8,128)(2,1)S(1)} collective-permute-done((bf16[16,5504]{1,0:T(8,128)(2,1)S(1)}, bf16[16,5504]{1,0:T(8,128)(2,1)S(1)}, u32[]{:S(2)}, u32[]{:S(2)}) %collective-permute-start.1) | collective-permute-done | bytes 176160 | tf_op jit(solution)/shard_map/gather/ppermute | solution.py:31
  30.6 1.3 %collective-permute-done.2 = bf16[16,5504]{1,0:T(8,128)(2,1)S(1)} collective-permute-done((bf16[16,5504]{1,0:T(8,128)(2,1)S(1)}, bf16[16,5504]{1,0:T(8,128)(2,1)S(1)}, u32[]{:S(2)}, u32[]{:S(2)}) %collective-permute-start.2) | collective-permute-done | bytes 176160 | tf_op jit(solution)/shard_map/gather/ppermute | solution.py:31
  32.0 1.3 %collective-permute-start.4 = (bf16[64,5504]{1,0:T(8,128)(2,1)S(1)}, bf16[64,5504]{1,0:T(8,128)(2,1)S(1)}, u32[]{:S(2)}, u32[]{:S(2)}) collective-permute-start(bf16[64,5504]{1,0:T(8,128)(2,1)S(1)} %bitcast.45), channel_id=1, source_target_pairs={{0,128},{1,5},{2,130},{3,7},{4,132},{5,1},{6,134},{7,3},{8,136},{9... | collective-permute-start | bytes 2113544 | tf_op jit(solution)/shard_map/gather/ppermute | solution.py:31
  33.3 2.9 %collective-permute-start.6 = (bf16[64,5504]{1,0:T(8,128)(2,1)S(1)}, bf16[64,5504]{1,0:T(8,128)(2,1)S(1)}, u32[]{:S(2)}, u32[]{:S(2)}) collective-permute-start(bf16[64,5504]{1,0:T(8,128)(2,1)S(1)} %bitcast.47), channel_id=1, source_target_pairs={{0,192},{1,7},{2,194},{3,5},{4,196},{5,3},{6,198},{7,1},{8,200},{9... | collective-permute-start | bytes 2113544 | tf_op jit(solution)/shard_map/gather/ppermute | solution.py:31
  36.2 6.9 %pad_maximum_fusion.weights_ref = bf16[1184,5120]{1,0:T(8,128)(2,1)S(1)} fusion(bf16[592,5120]{1,0:T(8,128)(2,1)} %collective-permute-done.3, bf16[592,5120]{1,0:T(8,128)(2,1)} %param.6), kind=kLoop, calls=%fused_computation | loop fusion | flops 24248320 | bytes 24248320 | tf_op jit(solution)/shard_map/gather/concatenate | solution.py:291
  43.3 1.5 %collective-permute-done.4 = bf16[64,5504]{1,0:T(8,128)(2,1)S(1)} collective-permute-done((bf16[64,5504]{1,0:T(8,128)(2,1)S(1)}, bf16[64,5504]{1,0:T(8,128)(2,1)S(1)}, u32[]{:S(2)}, u32[]{:S(2)}) %collective-permute-start.4) | collective-permute-done | bytes 704544 | tf_op jit(solution)/shard_map/gather/ppermute | solution.py:31
  44.9 5.0 %collective-permute-done.5 = bf16[64,5504]{1,0:T(8,128)(2,1)S(1)} collective-permute-done((bf16[64,5504]{1,0:T(8,128)(2,1)S(1)}, bf16[64,5504]{1,0:T(8,128)(2,1)S(1)}, u32[]{:S(2)}, u32[]{:S(2)}) %collective-permute-start.5) | collective-permute-done | bytes 704544 | tf_op jit(solution)/shard_map/gather/ppermute | solution.py:31
  49.9 2.3 %collective-permute-done.6 = bf16[64,5504]{1,0:T(8,128)(2,1)S(1)} collective-permute-done((bf16[64,5504]{1,0:T(8,128)(2,1)S(1)}, bf16[64,5504]{1,0:T(8,128)(2,1)S(1)}, u32[]{:S(2)}, u32[]{:S(2)}) %collective-permute-start.6) | collective-permute-done | bytes 704544 | tf_op jit(solution)/shard_map/gather/ppermute | solution.py:31
  53.5 3.7 %exponents.1 = (f32[1184,256]{1,0:T(8,128)S(1)}, f32[2,256]{1,0:T(2,128)S(1)}) custom-call(bf16[256,5504]{1,0:T(8,128)(2,1)S(1)} %bitcast.40, bf16[1184,5120]{1,0:T(8,128)(2,1)S(1)} %pad_maximum_fusion.weights_ref), custom_call_target="tpu_custom_call" | custom-call | flops 3103784960 | bytes 12124160 | tf_op jit(solution)/shard_map/logits/exponents/pallas_call | solution.py:201
  57.3 19.0 %all_to_all.16.stats_ref = f32[128,2,256]{2,1,0:T(2,128)S(1)} all-to-all(f32[128,2,256]{2,1,0:T(2,128)S(1)} %broadcast_in_dim.42), channel_id=1, replica_groups=mesh['y'=4,'z'=8,'x'=4,'core'=2] {'y','z','x'}, dimensions={0} | all-to-all | bytes 524288 | tf_op jit(solution)/shard_map/stats/all_to_all | solution.py:20
  76.3 3.9 %gradients.1 = (bf16[256,5120]{1,0:T(8,128)(2,1)S(1)}, bf16[592,256]{1,0:T(8,128)(2,1)S(1)}, bf16[592,256]{1,0:T(8,128)(2,1)S(1)}) custom-call(f32[128,2,256]{2,1,0:T(2,128)S(1)} %all_to_all.16.stats_ref, f32[2,256]{1,0:T(2,128)S(1)} %get-tuple-element.45.local_ref, bf16[256,5504]{1,0:T(8,128)(2,1)S(1)} %bitcast.41, ...), custom_call_target="tpu_custom_call" | custom-call | flops 3103784960 | bytes 12124160 | tf_op jit(solution)/shard_map/grads/gradients/pallas_call | solution.py:245
  80.2 1.7 %convolution_convert_fusion = bf16[592,5120]{1,0:T(8,128)(2,1)S(1)} fusion(bf16[592,256]{1,0:T(8,128)(2,1)S(1)} %get-tuple-element.51, bf16[256,5504]{1,0:T(8,128)(2,1)S(1)} %bitcast.42), kind=kOutput, calls=%fused_computation.2 | convolution fusion | flops 1554923520 | bytes 8986624 | tf_op jit(solution)/shard_map/grad_weight/dot_general | solution.py:316
  82.3 2.2 %collective-permute-start.7 = (bf16[64,5120]{1,0:T(8,128)(2,1)S(1)}, bf16[64,5120]{1,0:T(8,128)(2,1)S(1)}, u32[]{:S(2)}, u32[]{:S(2)}) collective-permute-start(bf16[64,5120]{1,0:T(8,128)(2,1)S(1)} %get-tuple-element.61), channel_id=1, source_target_pairs={{0,128},{1,5},{2,130},{3,7},{4,132},{5,1},{6,134},{7,3},{8,136},{9... | collective-permute-start | bytes 1966088 | tf_op jit(solution)/shard_map/scatter/ppermute | solution.py:31
  84.5 1.3 %collective-permute-start.8 = (bf16[64,5120]{1,0:T(8,128)(2,1)S(1)}, bf16[64,5120]{1,0:T(8,128)(2,1)S(1)}, u32[]{:S(2)}, u32[]{:S(2)}) collective-permute-start(bf16[64,5120]{1,0:T(8,128)(2,1)S(1)} %get-tuple-element.60), channel_id=1, source_target_pairs={{0,64},{1,3},{2,66},{3,1},{4,68},{5,7},{6,70},{7,5},{8,72},{9,11},... | collective-permute-start | bytes 1966088 | tf_op jit(solution)/shard_map/scatter/ppermute | solution.py:31
  86.5 8.0 %collective-permute-done.7 = bf16[64,5120]{1,0:T(8,128)(2,1)S(1)} collective-permute-done((bf16[64,5120]{1,0:T(8,128)(2,1)S(1)}, bf16[64,5120]{1,0:T(8,128)(2,1)S(1)}, u32[]{:S(2)}, u32[]{:S(2)}) %collective-permute-start.7) | collective-permute-done | bytes 655392 | tf_op jit(solution)/shard_map/scatter/ppermute | solution.py:31
  94.6 6.9 %collective-permute-done.8 = bf16[64,5120]{1,0:T(8,128)(2,1)S(1)} collective-permute-done((bf16[64,5120]{1,0:T(8,128)(2,1)S(1)}, bf16[64,5120]{1,0:T(8,128)(2,1)S(1)}, u32[]{:S(2)}, u32[]{:S(2)}) %collective-permute-start.8) | collective-permute-done | bytes 655392 | tf_op jit(solution)/shard_map/scatter/ppermute | solution.py:31
  101.9 1.4 %collective-permute-start.11 = (bf16[16,5120]{1,0:T(8,128)(2,1)S(1)}, bf16[16,5120]{1,0:T(8,128)(2,1)S(1)}, u32[]{:S(2)}, u32[]{:S(2)}) collective-permute-start(bf16[16,5120]{1,0:T(8,128)(2,1)S(1)} %get-tuple-element.65), channel_id=1, source_target_pairs={{0,4},{1,129},{2,6},{3,131},{4,0},{5,133},{6,2},{7,135},{8,12},{9,... | collective-permute-start | bytes 491528 | tf_op jit(solution)/shard_map/scatter/ppermute | solution.py:31
  103.9 2.2 %collective-permute-start.13 = (bf16[16,5120]{1,0:T(8,128)(2,1)S(1)}, bf16[16,5120]{1,0:T(8,128)(2,1)S(1)}, u32[]{:S(2)}, u32[]{:S(2)}) collective-permute-start(bf16[16,5120]{1,0:T(8,128)(2,1)S(1)} %get-tuple-element.63), channel_id=1, source_target_pairs={{0,6},{1,193},{2,4},{3,195},{4,2},{5,197},{6,0},{7,199},{8,14},{9,... | collective-permute-start | bytes 491528 | tf_op jit(solution)/shard_map/scatter/ppermute | solution.py:31
  106.1 4.5 %add_convert_fusion = bf16[592,5120]{1,0:T(8,128)(2,1)} fusion(bf16[592,5120]{1,0:T(8,128)(2,1)S(1)} %collective-permute-done.10, bf16[592,256]{1,0:T(8,128)(2,1)S(1)} %get-tuple-element.55, bf16[256,5504]{1,0:T(8,128)(2,1)S(1)} %bitcast.43), kind=kOutput, calls=%fused_computation.1 | convolution fusion | flops 1560985600 | bytes 15048704 | tf_op jit(solution)/shard_map/grad_weight/dot_general | solution.py:327
  110.7 12.2 %all_to_all.17 = bf16[8,2,5120]{2,1,0:T(2,128)(2,1)S(1)} all-to-all(bf16[8,2,5120]{2,1,0:T(2,128)(2,1)S(1)} %reshape.32), channel_id=1, replica_groups=mesh['y'=4,'z'=8,'x'=4,'core'=2] {'z'}, dimensions={0} | all-to-all | bytes 327680 | tf_op jit(solution)/shard_map/scatter/all_to_all | solution.py:333
  (34 shorter events, 6.3 us)
Async XLA Ops:
  0.6 31.4 %collective-permute-start.3 = (bf16[592,5120]{1,0:T(8,128)(2,1)}, bf16[592,5120]{1,0:T(8,128)(2,1)}, u32[]{:S(2)}, u32[]{:S(2)}) collective-permute-start(bf16[592,5120]{1,0:T(8,128)(2,1)} %param.6), channel_id=1, source_target_pairs={{0,1},{1,0},{2,3},{3,2},{4,5},{5,4},{6,7},{7,6},{8,9},{9,8},{10,11... | collective-permute-start | bytes 18186248 | tf_op jit(solution)/shard_map/ppermute | solution.py:279
  21.6 7.0 %collective-permute-start = (bf16[16,5504]{1,0:T(8,128)(2,1)S(1)}, bf16[16,5504]{1,0:T(8,128)(2,1)S(1)}, u32[]{:S(2)}, u32[]{:S(2)}) collective-permute-start(bf16[16,5504]{1,0:T(8,128)(2,1)S(1)} %reshape.27), channel_id=1, source_target_pairs={{0,4},{1,129},{2,6},{3,131},{4,0},{5,133},{6,2},{7,135},{8,12},{9,... | collective-permute-start | bytes 528392 | tf_op jit(solution)/shard_map/gather/ppermute | solution.py:31
  24.7 5.9 %collective-permute-start.1 = (bf16[16,5504]{1,0:T(8,128)(2,1)S(1)}, bf16[16,5504]{1,0:T(8,128)(2,1)S(1)}, u32[]{:S(2)}, u32[]{:S(2)}) collective-permute-start(bf16[16,5504]{1,0:T(8,128)(2,1)S(1)} %reshape.27), channel_id=1, source_target_pairs={{0,2},{1,65},{2,0},{3,67},{4,6},{5,69},{6,4},{7,71},{8,10},{9,73},... | collective-permute-start | bytes 528392 | tf_op jit(solution)/shard_map/gather/ppermute | solution.py:31
  25.3 6.7 %collective-permute-start.2 = (bf16[16,5504]{1,0:T(8,128)(2,1)S(1)}, bf16[16,5504]{1,0:T(8,128)(2,1)S(1)}, u32[]{:S(2)}, u32[]{:S(2)}) collective-permute-start(bf16[16,5504]{1,0:T(8,128)(2,1)S(1)} %reshape.27), channel_id=1, source_target_pairs={{0,6},{1,193},{2,4},{3,195},{4,2},{5,197},{6,0},{7,199},{8,14},{9,... | collective-permute-start | bytes 528392 | tf_op jit(solution)/shard_map/gather/ppermute | solution.py:31
  32.0 12.8 %collective-permute-start.4 = (bf16[64,5504]{1,0:T(8,128)(2,1)S(1)}, bf16[64,5504]{1,0:T(8,128)(2,1)S(1)}, u32[]{:S(2)}, u32[]{:S(2)}) collective-permute-start(bf16[64,5504]{1,0:T(8,128)(2,1)S(1)} %bitcast.45), channel_id=1, source_target_pairs={{0,128},{1,5},{2,130},{3,7},{4,132},{5,1},{6,134},{7,3},{8,136},{9... | collective-permute-start | bytes 2113544 | tf_op jit(solution)/shard_map/gather/ppermute | solution.py:31
  33.3 16.5 %collective-permute-start.5 = (bf16[64,5504]{1,0:T(8,128)(2,1)S(1)}, bf16[64,5504]{1,0:T(8,128)(2,1)S(1)}, u32[]{:S(2)}, u32[]{:S(2)}) collective-permute-start(bf16[64,5504]{1,0:T(8,128)(2,1)S(1)} %bitcast.46), channel_id=1, source_target_pairs={{0,64},{1,3},{2,66},{3,1},{4,68},{5,7},{6,70},{7,5},{8,72},{9,11},... | collective-permute-start | bytes 2113544 | tf_op jit(solution)/shard_map/gather/ppermute | solution.py:31
  33.3 18.9 %collective-permute-start.6 = (bf16[64,5504]{1,0:T(8,128)(2,1)S(1)}, bf16[64,5504]{1,0:T(8,128)(2,1)S(1)}, u32[]{:S(2)}, u32[]{:S(2)}) collective-permute-start(bf16[64,5504]{1,0:T(8,128)(2,1)S(1)} %bitcast.47), channel_id=1, source_target_pairs={{0,192},{1,7},{2,194},{3,5},{4,196},{5,3},{6,198},{7,1},{8,200},{9... | collective-permute-start | bytes 2113544 | tf_op jit(solution)/shard_map/gather/ppermute | solution.py:31
  82.0 24.1 %collective-permute-start.10 = (bf16[592,5120]{1,0:T(8,128)(2,1)S(1)}, bf16[592,5120]{1,0:T(8,128)(2,1)S(1)}, u32[]{:S(2)}, u32[]{:S(2)}) collective-permute-start(bf16[592,5120]{1,0:T(8,128)(2,1)S(1)} %convolution_convert_fusion), channel_id=1, source_target_pairs={{0,1},{1,0},{2,3},{3,2},{4,5},{5,4},{6,7},{7,6},{8,9},{9,8},{10,11... | collective-permute-start | bytes 18186248 | tf_op jit(solution)/shard_map/grad_weight/ppermute | solution.py:318
  82.3 12.3 %collective-permute-start.7 = (bf16[64,5120]{1,0:T(8,128)(2,1)S(1)}, bf16[64,5120]{1,0:T(8,128)(2,1)S(1)}, u32[]{:S(2)}, u32[]{:S(2)}) collective-permute-start(bf16[64,5120]{1,0:T(8,128)(2,1)S(1)} %get-tuple-element.61), channel_id=1, source_target_pairs={{0,128},{1,5},{2,130},{3,7},{4,132},{5,1},{6,134},{7,3},{8,136},{9... | collective-permute-start | bytes 1966088 | tf_op jit(solution)/shard_map/scatter/ppermute | solution.py:31
  84.5 16.9 %collective-permute-start.8 = (bf16[64,5120]{1,0:T(8,128)(2,1)S(1)}, bf16[64,5120]{1,0:T(8,128)(2,1)S(1)}, u32[]{:S(2)}, u32[]{:S(2)}) collective-permute-start(bf16[64,5120]{1,0:T(8,128)(2,1)S(1)} %get-tuple-element.60), channel_id=1, source_target_pairs={{0,64},{1,3},{2,66},{3,1},{4,68},{5,7},{6,70},{7,5},{8,72},{9,11},... | collective-permute-start | bytes 1966088 | tf_op jit(solution)/shard_map/scatter/ppermute | solution.py:31
  85.8 15.7 %collective-permute-start.9 = (bf16[64,5120]{1,0:T(8,128)(2,1)S(1)}, bf16[64,5120]{1,0:T(8,128)(2,1)S(1)}, u32[]{:S(2)}, u32[]{:S(2)}) collective-permute-start(bf16[64,5120]{1,0:T(8,128)(2,1)S(1)} %get-tuple-element.59), channel_id=1, source_target_pairs={{0,192},{1,7},{2,194},{3,5},{4,196},{5,3},{6,198},{7,1},{8,200},{9... | collective-permute-start | bytes 1966088 | tf_op jit(solution)/shard_map/scatter/ppermute | solution.py:31
  101.9 8.6 %collective-permute-start.11 = (bf16[16,5120]{1,0:T(8,128)(2,1)S(1)}, bf16[16,5120]{1,0:T(8,128)(2,1)S(1)}, u32[]{:S(2)}, u32[]{:S(2)}) collective-permute-start(bf16[16,5120]{1,0:T(8,128)(2,1)S(1)} %get-tuple-element.65), channel_id=1, source_target_pairs={{0,4},{1,129},{2,6},{3,131},{4,0},{5,133},{6,2},{7,135},{8,12},{9,... | collective-permute-start | bytes 491528 | tf_op jit(solution)/shard_map/scatter/ppermute | solution.py:31
  103.3 7.3 %collective-permute-start.12 = (bf16[16,5120]{1,0:T(8,128)(2,1)S(1)}, bf16[16,5120]{1,0:T(8,128)(2,1)S(1)}, u32[]{:S(2)}, u32[]{:S(2)}) collective-permute-start(bf16[16,5120]{1,0:T(8,128)(2,1)S(1)} %get-tuple-element.64), channel_id=1, source_target_pairs={{0,2},{1,65},{2,0},{3,67},{4,6},{5,69},{6,4},{7,71},{8,10},{9,73},... | collective-permute-start | bytes 491528 | tf_op jit(solution)/shard_map/scatter/ppermute | solution.py:31
  103.9 6.7 %collective-permute-start.13 = (bf16[16,5120]{1,0:T(8,128)(2,1)S(1)}, bf16[16,5120]{1,0:T(8,128)(2,1)S(1)}, u32[]{:S(2)}, u32[]{:S(2)}) collective-permute-start(bf16[16,5120]{1,0:T(8,128)(2,1)S(1)} %get-tuple-element.63), channel_id=1, source_target_pairs={{0,6},{1,193},{2,4},{3,195},{4,2},{5,197},{6,0},{7,199},{8,14},{9,... | collective-permute-start | bytes 491528 | tf_op jit(solution)/shard_map/scatter/ppermute | solution.py:31

commit v5 on v4

--- a/solution.py
+++ b/solution.py
@@ -58,7 +58,7 @@
 def total(pieces):
     result = pieces[0].astype(jnp.float32)
     for piece in pieces[1:]:
-        result = result + piece.astype(jnp.float32)
+        result = lax.optimization_barrier(result) + piece.astype(jnp.float32)
     return result.astype(jnp.bfloat16)
 
 
@@ -190,8 +190,13 @@
     top = jnp.max(logits, axis=0, keepdims=True)
     exponent = jnp.exp(logits - top)
     exp_ref[...] = exponent
-    stats_ref[0:1] = top
-    stats_ref[1:2] = jnp.sum(exponent, axis=0, keepdims=True)
+    total = jnp.sum(exponent, axis=0, keepdims=True)
+    lanes = stats_ref.shape[1]
+    half = stats_ref.shape[0] // 2
+    for i in range(half):
+        at = slice(i * lanes, (i + 1) * lanes)
+        stats_ref[i : i + 1] = top[:, at]
+        stats_ref[half + i : half + i + 1] = total[:, at]
 
 
 def exponents(gathered, weights):
@@ -202,7 +207,7 @@
         logits_kernel,
         out_shape=(
             jax.ShapeDtypeStruct((entries, rows), jnp.float32),
-            jax.ShapeDtypeStruct((2, rows), jnp.float32),
+            jax.ShapeDtypeStruct((2 * rows // 128, 128), jnp.float32),
         ),
         in_specs=[vmem] * 2,
         out_specs=(vmem, vmem),
@@ -222,12 +227,21 @@
 ):
     entries, width = weights_ref.shape
     tile = 512
-    tops = stats_ref[:, 0, :]
-    top = jnp.max(tops, axis=0, keepdims=True)
-    total = jnp.sum(stats_ref[:, 1, :] * jnp.exp(tops - top), axis=0, keepdims=True)
+    half = stats_ref.shape[1] // 2
+    tops, totals, locals_ = [], [], []
+    for i in range(half):
+        values = stats_ref[:, i, :]
+        top = jnp.max(values, axis=0, keepdims=True)
+        total = stats_ref[:, half + i, :] * jnp.exp(values - top)
+        tops.append(top)
+        totals.append(jnp.sum(total, axis=0, keepdims=True))
+        locals_.append(local_ref[i : i + 1])
+    top = jnp.concatenate(tops, axis=1)
+    total = jnp.concatenate(totals, axis=1)
+    local = jnp.concatenate(locals_, axis=1)
     tail = gathered_ref[:, gathered_ref.shape[1] - 128 :]
     mass = jnp.sum(tail.astype(jnp.float32).T, axis=0, keepdims=True)
-    scale = mass * jnp.exp(local_ref[0:1] - top) / total
+    scale = mass * jnp.exp(local - top) / total
     grad = (exp_ref[...] * scale - target_ref[...]).astype(jnp.bfloat16)
     own_grad_ref[...] = grad[: entries // 2]
     other_grad_ref[...] = grad[entries // 2 :]
@@ -259,6 +273,33 @@
         ),
         name="gradients",
     )(stats, local, gathered, exponent, target, weights)
+
+
+def product_kernel(own_grad_ref, other_grad_ref, own_ref, other_ref, out_ref):
+    out = jnp.dot(own_grad_ref[...], own_ref[...], preferred_element_type=jnp.float32)
+    out += jnp.dot(other_grad_ref[...], other_ref[...], preferred_element_type=jnp.float32)
+    out_ref[...] = out.astype(jnp.bfloat16)
+
+
+def product(own_grad, other_grad, own_hidden, other_hidden, width):
+    entries, rows = own_grad.shape
+    tile = 1024
+    grad_spec = pl.BlockSpec((entries, rows), lambda n: (0, 0))
+    hidden_spec = pl.BlockSpec((rows, tile), lambda n: (0, n))
+    return pl.pallas_call(
+        product_kernel,
+        out_shape=jax.ShapeDtypeStruct((entries, width), jnp.bfloat16),
+        grid=(width // tile,),
+        in_specs=[grad_spec, grad_spec, hidden_spec, hidden_spec],
+        out_specs=pl.BlockSpec((entries, tile), lambda n: (0, n)),
+        compiler_params=pltpu.CompilerParams(vmem_limit_bytes=16 * 1024 * 1024),
+        cost_estimate=pl.CostEstimate(
+            flops=4 * entries * rows * width,
+            bytes_accessed=2 * entries * width + 4 * rows * width,
+            transcendentals=0,
+        ),
+        name="product",
+    )(own_grad, other_grad, own_hidden, other_hidden)
 
 
 def per_device(sizes, hidden_states, head_weight, teacher_ids, teacher_probs, row_weight):
@@ -290,7 +331,6 @@
         gathered, other_weight = lax.optimization_barrier((gathered, other_weight))
         weights = jnp.concatenate([head_weight, other_weight], axis=0)
         gathered, weights = gather_blocks(gathered, sizes, 1, second_spots, weights)
-        hidden = gathered[:, :width]
 
     with jax.named_scope("target"):
         target = dense_target(gathered, firsts, width, kept, entries)
@@ -301,7 +341,9 @@
     with jax.named_scope("stats"):
         local, target = lax.optimization_barrier((local, target))
         stats = spread(local, ("y", "z", "x"), size_y * size_z * size_x)
-        stats = stats.reshape(-1, 2, rows)
+        stats = stats.reshape((-1,) + local.shape)
+        stats, sent = lax.optimization_barrier((stats, gathered))
+        other_gathered = lax.ppermute(sent, "core", SWAP)
 
     with jax.named_scope("grads"):
         partial, grad, other_grad = gradients(
@@ -309,29 +351,20 @@
         )
 
     with jax.named_scope("scatter"):
-        partial, other_grad = lax.optimization_barrier((partial, other_grad))
         pieces = scatter_blocks(partial, sizes, 1, second_spots)
 
     with jax.named_scope("grad_weight"):
-        other_part = jnp.dot(other_grad, hidden, preferred_element_type=jnp.float32)
-        other_part = other_part.astype(jnp.bfloat16)
-        returned = lax.ppermute(other_part, "core", SWAP)
-
-    with jax.named_scope("scatter"):
-        pieces[0], other_part = lax.optimization_barrier((pieces[0], other_part))
-        summed = total(pieces)
-        summed, grad = lax.optimization_barrier((summed, grad))
-        pieces = scatter_blocks(summed, sizes, 0, first_spots)
-
-    with jax.named_scope("grad_weight"):
-        own_part = jnp.dot(grad, hidden, preferred_element_type=jnp.float32)
-        grad_weight = (own_part + returned.astype(jnp.float32)).astype(jnp.bfloat16)
+        received = lax.ppermute(other_grad, "core", SWAP)
+        grad_weight = product(grad, received, gathered, other_gathered, width)
 
     with jax.named_scope("scatter"):
         pieces[0], grad_weight = lax.optimization_barrier((pieces[0], grad_weight))
+        summed = total(pieces)
+        pieces = scatter_blocks(summed, sizes, 0, first_spots)
         summed = total(pieces).reshape(size_z, own_rows, width)
         pieces = lax.all_to_all(summed, "z", 0, 0, tiled=True)
         grad_hidden = jnp.sum(pieces.astype(jnp.float32), axis=0).astype(jnp.bfloat16)
+
     return grad_hidden, grad_weight
 
 

time: 126 us -> 123 us (0.976)
  matrix products: 6.21 us -> 0 us
  Pallas kernels: 10.3 us -> 16.1 us
  waiting for transfers between devices: 29.6 us -> 27.8 us
    dot_general x2 -> x0, matrix products: 6.21 us -> none  [the longest x1 4.46 us: per_device(): own_part = jnp.dot(grad, hidden, preferred_element_type=jnp.float32)]
    pallas_call x0 -> x1, Pallas kernels: none -> 5.83 us  [product(): pl.pallas_call(product_kernel, out_shape=jax.ShapeDtypeStruct((entries, w...]
    ppermute x12, waiting for transfers between devices: 29.6 us -> 27.8 us  [partner(): return lax.ppermute(block, AXES, pairs)]
  transfers between devices with their start and end apart: 14 -> 15, of which waited for: 8 -> 10; matrix products, arithmetic and copies ran while one was open for 10% -> 7% of each run, Pallas kernels for 1% -> 9%
where the time goes in v5:
time: 123 us; the launch traced here: 121 us
  blocking collectives  50.3 us (41%)
  waiting for transfers between devices  27.8 us (23%)
  starting transfers between devices  17.1 us (14%)
  Pallas kernels  16.1 us (13%)
  other arithmetic  8.29 us (7%)
    ppermute x12, waiting for transfers between devices, partner(): return lax.ppermute(block, AXES, pairs)  27.8 us
    all_to_all x1, blocking collectives, per_device(): across_z = lax.all_to_all(packed, 'z', 0, 0, tiled=True).reshape(group, -1)  19.1 us
    all_to_all x1, blocking collectives, spread(): return lax.all_to_all(copies, axes, 0, 0, tiled=True)  19 us
    ppermute x12, starting transfers between devices, partner(): return lax.ppermute(block, AXES, pairs)  17 us
    all_to_all x1, blocking collectives, per_device(): pieces = lax.all_to_all(summed, 'z', 0, 0, tiled=True)  12.2 us
    concatenate x1, other arithmetic, per_device(): weights = jnp.concatenate([head_weight, other_weight], axis=0)  6.89 us
    pallas_call x1, Pallas kernels, product(): pl.pallas_call(product_kernel, out_shape=jax.ShapeDtypeStruct((entries, w...  5.83 us
    pallas_call x1, Pallas kernels, gradients(): pl.pallas_call(grad_kernel, out_shape=(jax.ShapeDtypeStruct((rows, width)...  3.9 us
  transfers between devices with their start and end apart: 15, of which 10 were waited for; matrix products, arithmetic and copies ran while one was open for 7% of the time, Pallas kernels for 9%

profile of v5, /device:TPU:24, one launch (start us, length us, event | category | flops | bytes accessed | tf_op | source)
XLA Modules:
  0.0 121.5 jit_solution(17482994721273569333)
XLA Ops:
  0.8 1.6 %pack.1 = bf16[8,2,5504]{2,1,0:T(2,128)(2,1)} custom-call(f32[2]{0:T(128)} %weight_ref.1, bf16[2,5120]{1,0:T(2,128)(2,1)} %hidden_ref, s32[2,64]{1,0:T(2,128)} %ids_ref.1, f32[2,64]{1,0:T(2,128)} %probs_ref.1), custom_call_target="tpu_custom_call" | custom-call | tf_op jit(solution)/shard_map/pack/pack/pallas_call | solution.py:107
  2.4 19.1 %all_to_all.15 = bf16[8,2,5504]{2,1,0:T(2,128)(2,1)S(1)} all-to-all(bf16[8,2,5504]{2,1,0:T(2,128)(2,1)} %pack.1), channel_id=1, replica_groups=mesh['y'=4,'z'=8,'x'=4,'core'=2] {'z'}, dimensions={0} | all-to-all | bytes 352256 | tf_op jit(solution)/shard_map/gather/all_to_all | solution.py:329
  21.6 3.1 %collective-permute-start = (bf16[16,5504]{1,0:T(8,128)(2,1)S(1)}, bf16[16,5504]{1,0:T(8,128)(2,1)S(1)}, u32[]{:S(2)}, u32[]{:S(2)}) collective-permute-start(bf16[16,5504]{1,0:T(8,128)(2,1)S(1)} %reshape.29), channel_id=1, source_target_pairs={{0,4},{1,129},{2,6},{3,131},{4,0},{5,133},{6,2},{7,135},{8,12},{9,... | collective-permute-start | bytes 528392 | tf_op jit(solution)/shard_map/gather/ppermute | solution.py:31
  26.0 2.6 %collective-permute-done = bf16[16,5504]{1,0:T(8,128)(2,1)S(1)} collective-permute-done((bf16[16,5504]{1,0:T(8,128)(2,1)S(1)}, bf16[16,5504]{1,0:T(8,128)(2,1)S(1)}, u32[]{:S(2)}, u32[]{:S(2)}) %collective-permute-start) | collective-permute-done | bytes 176160 | tf_op jit(solution)/shard_map/gather/ppermute | solution.py:31
  28.7 2.0 %collective-permute-done.1 = bf16[16,5504]{1,0:T(8,128)(2,1)S(1)} collective-permute-done((bf16[16,5504]{1,0:T(8,128)(2,1)S(1)}, bf16[16,5504]{1,0:T(8,128)(2,1)S(1)}, u32[]{:S(2)}, u32[]{:S(2)}) %collective-permute-start.1) | collective-permute-done | bytes 176160 | tf_op jit(solution)/shard_map/gather/ppermute | solution.py:31
  30.6 1.3 %collective-permute-done.2 = bf16[16,5504]{1,0:T(8,128)(2,1)S(1)} collective-permute-done((bf16[16,5504]{1,0:T(8,128)(2,1)S(1)}, bf16[16,5504]{1,0:T(8,128)(2,1)S(1)}, u32[]{:S(2)}, u32[]{:S(2)}) %collective-permute-start.2) | collective-permute-done | bytes 176160 | tf_op jit(solution)/shard_map/gather/ppermute | solution.py:31
  32.0 1.3 %collective-permute-start.4 = (bf16[64,5504]{1,0:T(8,128)(2,1)S(1)}, bf16[64,5504]{1,0:T(8,128)(2,1)S(1)}, u32[]{:S(2)}, u32[]{:S(2)}) collective-permute-start(bf16[64,5504]{1,0:T(8,128)(2,1)S(1)} %bitcast.44), channel_id=1, source_target_pairs={{0,128},{1,5},{2,130},{3,7},{4,132},{5,1},{6,134},{7,3},{8,136},{9... | collective-permute-start | bytes 2113544 | tf_op jit(solution)/shard_map/gather/ppermute | solution.py:31
  33.3 2.9 %collective-permute-start.6 = (bf16[64,5504]{1,0:T(8,128)(2,1)S(1)}, bf16[64,5504]{1,0:T(8,128)(2,1)S(1)}, u32[]{:S(2)}, u32[]{:S(2)}) collective-permute-start(bf16[64,5504]{1,0:T(8,128)(2,1)S(1)} %bitcast.46), channel_id=1, source_target_pairs={{0,192},{1,7},{2,194},{3,5},{4,196},{5,3},{6,198},{7,1},{8,200},{9... | collective-permute-start | bytes 2113544 | tf_op jit(solution)/shard_map/gather/ppermute | solution.py:31
  36.2 6.9 %pad_maximum_fusion.weights_ref = bf16[1184,5120]{1,0:T(8,128)(2,1)S(1)} fusion(bf16[592,5120]{1,0:T(8,128)(2,1)} %collective-permute-done.3, bf16[592,5120]{1,0:T(8,128)(2,1)} %param.6), kind=kLoop, calls=%fused_computation | loop fusion | flops 24248320 | bytes 24248320 | tf_op jit(solution)/shard_map/gather/concatenate | solution.py:332
  43.3 1.5 %collective-permute-done.4 = bf16[64,5504]{1,0:T(8,128)(2,1)S(1)} collective-permute-done((bf16[64,5504]{1,0:T(8,128)(2,1)S(1)}, bf16[64,5504]{1,0:T(8,128)(2,1)S(1)}, u32[]{:S(2)}, u32[]{:S(2)}) %collective-permute-start.4) | collective-permute-done | bytes 704544 | tf_op jit(solution)/shard_map/gather/ppermute | solution.py:31
  44.9 5.0 %collective-permute-done.5 = bf16[64,5504]{1,0:T(8,128)(2,1)S(1)} collective-permute-done((bf16[64,5504]{1,0:T(8,128)(2,1)S(1)}, bf16[64,5504]{1,0:T(8,128)(2,1)S(1)}, u32[]{:S(2)}, u32[]{:S(2)}) %collective-permute-start.5) | collective-permute-done | bytes 704544 | tf_op jit(solution)/shard_map/gather/ppermute | solution.py:31
  49.9 2.3 %collective-permute-done.6 = bf16[64,5504]{1,0:T(8,128)(2,1)S(1)} collective-permute-done((bf16[64,5504]{1,0:T(8,128)(2,1)S(1)}, bf16[64,5504]{1,0:T(8,128)(2,1)S(1)}, u32[]{:S(2)}, u32[]{:S(2)}) %collective-permute-start.6) | collective-permute-done | bytes 704544 | tf_op jit(solution)/shard_map/gather/ppermute | solution.py:31
  53.5 3.6 %exponents.1 = (f32[1184,256]{1,0:T(8,128)S(1)}, f32[4,128]{1,0:T(4,128)S(1)}) custom-call(bf16[256,5504]{1,0:T(8,128)(2,1)S(1)} %bitcast.39, bf16[1184,5120]{1,0:T(8,128)(2,1)S(1)} %pad_maximum_fusion.weights_ref), custom_call_target="tpu_custom_call" | custom-call | flops 3103784960 | bytes 12124160 | tf_op jit(solution)/shard_map/logits/exponents/pallas_call | solution.py:206
  57.2 19.0 %all_to_all.16.stats_ref = f32[128,4,128]{2,1,0:T(4,128)S(1)} all-to-all(f32[128,4,128]{2,1,0:T(4,128)S(1)} %broadcast_in_dim.42), channel_id=1, replica_groups=mesh['y'=4,'z'=8,'x'=4,'core'=2] {'y','z','x'}, dimensions={0} | all-to-all | bytes 524288 | tf_op jit(solution)/shard_map/stats/all_to_all | solution.py:20
  76.2 3.9 %gradients.1 = (bf16[256,5120]{1,0:T(8,128)(2,1)S(1)}, bf16[592,256]{1,0:T(8,128)(2,1)S(1)}, bf16[592,256]{1,0:T(8,128)(2,1)S(1)}) custom-call(f32[128,4,128]{2,1,0:T(4,128)S(1)} %all_to_all.16.stats_ref, f32[4,128]{1,0:T(4,128)S(1)} %get-tuple-element.42.local_ref, bf16[256,5504]{1,0:T(8,128)(2,1)S(1)} %bitcast.41, ...), custom_call_target="tpu_custom_call" | custom-call | flops 3103784960 | bytes 12124160 | tf_op jit(solution)/shard_map/grads/gradients/pallas_call | solution.py:259
  80.3 2.2 %collective-permute-start.9 = (bf16[64,5120]{1,0:T(8,128)(2,1)S(1)}, bf16[64,5120]{1,0:T(8,128)(2,1)S(1)}, u32[]{:S(2)}, u32[]{:S(2)}) collective-permute-start(bf16[64,5120]{1,0:T(8,128)(2,1)S(1)} %get-tuple-element.54), channel_id=1, source_target_pairs={{0,128},{1,5},{2,130},{3,7},{4,132},{5,1},{6,134},{7,3},{8,136},{9... | collective-permute-start | bytes 1966088 | tf_op jit(solution)/shard_map/scatter/ppermute | solution.py:31
  84.7 5.8 %product.1 = bf16[592,5120]{1,0:T(8,128)(2,1)} custom-call(bf16[592,256]{1,0:T(8,128)(2,1)S(1)} %get-tuple-element.47.own_grad_ref, bf16[592,256]{1,0:T(8,128)(2,1)S(1)} %collective-permute-done.7.other_grad_ref, bf16[256,5504]{1,0:T(8,128)(2,1)S(1)} %bitcast.42, bf16[256,5504]{1,0:T(8,128)(2,1)S(1)} %collective-permute-done.8.other_ref), custom_call_target="tpu_custom_call" | custom-call | flops 3103784960 | bytes 11304960 | tf_op jit(solution)/shard_map/grad_weight/product/pallas_call | solution.py:289
  90.6 1.9 %collective-permute-done.9 = bf16[64,5120]{1,0:T(8,128)(2,1)S(1)} collective-permute-done((bf16[64,5120]{1,0:T(8,128)(2,1)S(1)}, bf16[64,5120]{1,0:T(8,128)(2,1)S(1)}, u32[]{:S(2)}, u32[]{:S(2)}) %collective-permute-start.9) | collective-permute-done | bytes 655392 | tf_op jit(solution)/shard_map/scatter/ppermute | solution.py:31
  92.7 6.8 %collective-permute-done.10 = bf16[64,5120]{1,0:T(8,128)(2,1)S(1)} collective-permute-done((bf16[64,5120]{1,0:T(8,128)(2,1)S(1)}, bf16[64,5120]{1,0:T(8,128)(2,1)S(1)}, u32[]{:S(2)}, u32[]{:S(2)}) %collective-permute-start.10) | collective-permute-done | bytes 655392 | tf_op jit(solution)/shard_map/scatter/ppermute | solution.py:31
  99.8 1.4 %collective-permute-start.12 = (bf16[16,5120]{1,0:T(8,128)(2,1)S(1)}, bf16[16,5120]{1,0:T(8,128)(2,1)S(1)}, u32[]{:S(2)}, u32[]{:S(2)}) collective-permute-start(bf16[16,5120]{1,0:T(8,128)(2,1)S(1)} %get-tuple-element.58), channel_id=1, source_target_pairs={{0,4},{1,129},{2,6},{3,131},{4,0},{5,133},{6,2},{7,135},{8,12},{9,... | collective-permute-start | bytes 491528 | tf_op jit(solution)/shard_map/scatter/ppermute | solution.py:31
  101.7 2.3 %collective-permute-start.14 = (bf16[16,5120]{1,0:T(8,128)(2,1)S(1)}, bf16[16,5120]{1,0:T(8,128)(2,1)S(1)}, u32[]{:S(2)}, u32[]{:S(2)}) collective-permute-start(bf16[16,5120]{1,0:T(8,128)(2,1)S(1)} %get-tuple-element.56), channel_id=1, source_target_pairs={{0,6},{1,193},{2,4},{3,195},{4,2},{5,197},{6,0},{7,199},{8,14},{9,... | collective-permute-start | bytes 491528 | tf_op jit(solution)/shard_map/scatter/ppermute | solution.py:31
  104.0 2.8 %collective-permute-done.12 = bf16[16,5120]{1,0:T(8,128)(2,1)S(1)} collective-permute-done((bf16[16,5120]{1,0:T(8,128)(2,1)S(1)}, bf16[16,5120]{1,0:T(8,128)(2,1)S(1)}, u32[]{:S(2)}, u32[]{:S(2)}) %collective-permute-start.12) | collective-permute-done | bytes 163872 | tf_op jit(solution)/shard_map/scatter/ppermute | solution.py:31
  106.8 1.7 %collective-permute-done.14 = bf16[16,5120]{1,0:T(8,128)(2,1)S(1)} collective-permute-done((bf16[16,5120]{1,0:T(8,128)(2,1)S(1)}, bf16[16,5120]{1,0:T(8,128)(2,1)S(1)}, u32[]{:S(2)}, u32[]{:S(2)}) %collective-permute-start.14) | collective-permute-done | bytes 163872 | tf_op jit(solution)/shard_map/scatter/ppermute | solution.py:31
  108.5 12.2 %all_to_all.17 = bf16[8,2,5120]{2,1,0:T(2,128)(2,1)S(1)} all-to-all(bf16[8,2,5120]{2,1,0:T(2,128)(2,1)S(1)} %reshape.34), channel_id=1, replica_groups=mesh['y'=4,'z'=8,'x'=4,'core'=2] {'z'}, dimensions={0} | all-to-all | bytes 327680 | tf_op jit(solution)/shard_map/scatter/all_to_all | solution.py:365
  (40 shorter events, 7.5 us)
Async XLA Ops:
  0.6 31.4 %collective-permute-start.3 = (bf16[592,5120]{1,0:T(8,128)(2,1)}, bf16[592,5120]{1,0:T(8,128)(2,1)}, u32[]{:S(2)}, u32[]{:S(2)}) collective-permute-start(bf16[592,5120]{1,0:T(8,128)(2,1)} %param.6), channel_id=1, source_target_pairs={{0,1},{1,0},{2,3},{3,2},{4,5},{5,4},{6,7},{7,6},{8,9},{9,8},{10,11... | collective-permute-start | bytes 18186248 | tf_op jit(solution)/shard_map/ppermute | solution.py:320
  21.6 7.0 %collective-permute-start = (bf16[16,5504]{1,0:T(8,128)(2,1)S(1)}, bf16[16,5504]{1,0:T(8,128)(2,1)S(1)}, u32[]{:S(2)}, u32[]{:S(2)}) collective-permute-start(bf16[16,5504]{1,0:T(8,128)(2,1)S(1)} %reshape.29), channel_id=1, source_target_pairs={{0,4},{1,129},{2,6},{3,131},{4,0},{5,133},{6,2},{7,135},{8,12},{9,... | collective-permute-start | bytes 528392 | tf_op jit(solution)/shard_map/gather/ppermute | solution.py:31
  24.7 5.9 %collective-permute-start.1 = (bf16[16,5504]{1,0:T(8,128)(2,1)S(1)}, bf16[16,5504]{1,0:T(8,128)(2,1)S(1)}, u32[]{:S(2)}, u32[]{:S(2)}) collective-permute-start(bf16[16,5504]{1,0:T(8,128)(2,1)S(1)} %reshape.29), channel_id=1, source_target_pairs={{0,2},{1,65},{2,0},{3,67},{4,6},{5,69},{6,4},{7,71},{8,10},{9,73},... | collective-permute-start | bytes 528392 | tf_op jit(solution)/shard_map/gather/ppermute | solution.py:31
  25.3 6.7 %collective-permute-start.2 = (bf16[16,5504]{1,0:T(8,128)(2,1)S(1)}, bf16[16,5504]{1,0:T(8,128)(2,1)S(1)}, u32[]{:S(2)}, u32[]{:S(2)}) collective-permute-start(bf16[16,5504]{1,0:T(8,128)(2,1)S(1)} %reshape.29), channel_id=1, source_target_pairs={{0,6},{1,193},{2,4},{3,195},{4,2},{5,197},{6,0},{7,199},{8,14},{9,... | collective-permute-start | bytes 528392 | tf_op jit(solution)/shard_map/gather/ppermute | solution.py:31
  32.0 12.8 %collective-permute-start.4 = (bf16[64,5504]{1,0:T(8,128)(2,1)S(1)}, bf16[64,5504]{1,0:T(8,128)(2,1)S(1)}, u32[]{:S(2)}, u32[]{:S(2)}) collective-permute-start(bf16[64,5504]{1,0:T(8,128)(2,1)S(1)} %bitcast.44), channel_id=1, source_target_pairs={{0,128},{1,5},{2,130},{3,7},{4,132},{5,1},{6,134},{7,3},{8,136},{9... | collective-permute-start | bytes 2113544 | tf_op jit(solution)/shard_map/gather/ppermute | solution.py:31
  33.3 16.5 %collective-permute-start.5 = (bf16[64,5504]{1,0:T(8,128)(2,1)S(1)}, bf16[64,5504]{1,0:T(8,128)(2,1)S(1)}, u32[]{:S(2)}, u32[]{:S(2)}) collective-permute-start(bf16[64,5504]{1,0:T(8,128)(2,1)S(1)} %bitcast.45), channel_id=1, source_target_pairs={{0,64},{1,3},{2,66},{3,1},{4,68},{5,7},{6,70},{7,5},{8,72},{9,11},... | collective-permute-start | bytes 2113544 | tf_op jit(solution)/shard_map/gather/ppermute | solution.py:31
  33.3 18.9 %collective-permute-start.6 = (bf16[64,5504]{1,0:T(8,128)(2,1)S(1)}, bf16[64,5504]{1,0:T(8,128)(2,1)S(1)}, u32[]{:S(2)}, u32[]{:S(2)}) collective-permute-start(bf16[64,5504]{1,0:T(8,128)(2,1)S(1)} %bitcast.46), channel_id=1, source_target_pairs={{0,192},{1,7},{2,194},{3,5},{4,196},{5,3},{6,198},{7,1},{8,200},{9... | collective-permute-start | bytes 2113544 | tf_op jit(solution)/shard_map/gather/ppermute | solution.py:31
  76.2 8.5 %collective-permute-start.8 = (bf16[256,5504]{1,0:T(8,128)(2,1)S(1)}, bf16[256,5504]{1,0:T(8,128)(2,1)S(1)}, u32[]{:S(2)}, u32[]{:S(2)}) collective-permute-start(bf16[256,5504]{1,0:T(8,128)(2,1)S(1)} %bitcast.40), channel_id=1, source_target_pairs={{0,1},{1,0},{2,3},{3,2},{4,5},{5,4},{6,7},{7,6},{8,9},{9,8},{10,11... | collective-permute-start | bytes 8454152 | tf_op jit(solution)/shard_map/stats/ppermute | solution.py:346
  80.3 12.3 %collective-permute-start.9 = (bf16[64,5120]{1,0:T(8,128)(2,1)S(1)}, bf16[64,5120]{1,0:T(8,128)(2,1)S(1)}, u32[]{:S(2)}, u32[]{:S(2)}) collective-permute-start(bf16[64,5120]{1,0:T(8,128)(2,1)S(1)} %get-tuple-element.54), channel_id=1, source_target_pairs={{0,128},{1,5},{2,130},{3,7},{4,132},{5,1},{6,134},{7,3},{8,136},{9... | collective-permute-start | bytes 1966088 | tf_op jit(solution)/shard_map/scatter/ppermute | solution.py:31
  82.5 2.2 %collective-permute-start.7 = (bf16[592,256]{1,0:T(8,128)(2,1)S(1)}, bf16[592,256]{1,0:T(8,128)(2,1)S(1)}, u32[]{:S(2)}, u32[]{:S(2)}) collective-permute-start(bf16[592,256]{1,0:T(8,128)(2,1)S(1)} %get-tuple-element.48), channel_id=1, source_target_pairs={{0,1},{1,0},{2,3},{3,2},{4,5},{5,4},{6,7},{7,6},{8,9},{9,8},{10,11... | collective-permute-start | bytes 909320 | tf_op jit(solution)/shard_map/grad_weight/ppermute | solution.py:357
  82.5 16.9 %collective-permute-start.10 = (bf16[64,5120]{1,0:T(8,128)(2,1)S(1)}, bf16[64,5120]{1,0:T(8,128)(2,1)S(1)}, u32[]{:S(2)}, u32[]{:S(2)}) collective-permute-start(bf16[64,5120]{1,0:T(8,128)(2,1)S(1)} %get-tuple-element.53), channel_id=1, source_target_pairs={{0,64},{1,3},{2,66},{3,1},{4,68},{5,7},{6,70},{7,5},{8,72},{9,11},... | collective-permute-start | bytes 1966088 | tf_op jit(solution)/shard_map/scatter/ppermute | solution.py:31
  83.8 15.7 %collective-permute-start.11 = (bf16[64,5120]{1,0:T(8,128)(2,1)S(1)}, bf16[64,5120]{1,0:T(8,128)(2,1)S(1)}, u32[]{:S(2)}, u32[]{:S(2)}) collective-permute-start(bf16[64,5120]{1,0:T(8,128)(2,1)S(1)} %get-tuple-element.52), channel_id=1, source_target_pairs={{0,192},{1,7},{2,194},{3,5},{4,196},{5,3},{6,198},{7,1},{8,200},{9... | collective-permute-start | bytes 1966088 | tf_op jit(solution)/shard_map/scatter/ppermute | solution.py:31
  99.8 6.9 %collective-permute-start.12 = (bf16[16,5120]{1,0:T(8,128)(2,1)S(1)}, bf16[16,5120]{1,0:T(8,128)(2,1)S(1)}, u32[]{:S(2)}, u32[]{:S(2)}) collective-permute-start(bf16[16,5120]{1,0:T(8,128)(2,1)S(1)} %get-tuple-element.58), channel_id=1, source_target_pairs={{0,4},{1,129},{2,6},{3,131},{4,0},{5,133},{6,2},{7,135},{8,12},{9,... | collective-permute-start | bytes 491528 | tf_op jit(solution)/shard_map/scatter/ppermute | solution.py:31
  101.2 5.5 %collective-permute-start.13 = (bf16[16,5120]{1,0:T(8,128)(2,1)S(1)}, bf16[16,5120]{1,0:T(8,128)(2,1)S(1)}, u32[]{:S(2)}, u32[]{:S(2)}) collective-permute-start(bf16[16,5120]{1,0:T(8,128)(2,1)S(1)} %get-tuple-element.57), channel_id=1, source_target_pairs={{0,2},{1,65},{2,0},{3,67},{4,6},{5,69},{6,4},{7,71},{8,10},{9,73},... | collective-permute-start | bytes 491528 | tf_op jit(solution)/shard_map/scatter/ppermute | solution.py:31
  101.7 6.8 %collective-permute-start.14 = (bf16[16,5120]{1,0:T(8,128)(2,1)S(1)}, bf16[16,5120]{1,0:T(8,128)(2,1)S(1)}, u32[]{:S(2)}, u32[]{:S(2)}) collective-permute-start(bf16[16,5120]{1,0:T(8,128)(2,1)S(1)} %get-tuple-element.56), channel_id=1, source_target_pairs={{0,6},{1,193},{2,4},{3,195},{4,2},{5,197},{6,0},{7,199},{8,14},{9,... | collective-permute-start | bytes 491528 | tf_op jit(solution)/shard_map/scatter/ppermute | solution.py:31

commit v6 on v5

--- a/solution.py
+++ b/solution.py
@@ -148,7 +148,7 @@
             out_ref[at] = jnp.where(here == second, second_amount, value)
             return carry
 
-        lax.fori_loop(0, 2 * entries // step, one, 0, unroll=2)
+        lax.fori_loop(0, 2 * entries // step, one, 0, unroll=37)
         return jnp.min(place)
 
     lax.while_loop(
@@ -317,18 +317,18 @@
     first_spots = [first_place ^ step for step in range(SIDE)]
     second_spots = [second_place ^ step for step in range(SIDE)]
     firsts = jnp.stack([device * entries, (device + 1 - 2 * core) * entries])
-    other_weight = lax.ppermute(head_weight, "core", SWAP)
 
     with jax.named_scope("pack"):
         hidden_states, first_spots, second_spots, firsts = lax.optimization_barrier(
             (hidden_states, first_spots, second_spots, firsts)
         )
         packed = pack(hidden_states, teacher_ids, teacher_probs, row_weight, size_z)
+        packed, own_weight = lax.optimization_barrier((packed, head_weight))
+        other_weight = lax.ppermute(own_weight, "core", SWAP)
 
     with jax.named_scope("gather"):
         across_z = lax.all_to_all(packed, "z", 0, 0, tiled=True).reshape(group, -1)
         gathered, _ = gather_blocks(across_z, sizes, 0, first_spots)
-        gathered, other_weight = lax.optimization_barrier((gathered, other_weight))
         weights = jnp.concatenate([head_weight, other_weight], axis=0)
         gathered, weights = gather_blocks(gathered, sizes, 1, second_spots, weights)
 

time: 123 us -> 123 us (level)
  transfers between devices with their start and end apart: 15 -> 15, of which waited for: 10 -> 11; matrix products, arithmetic and copies ran while one was open for 7% -> 7% of each run, Pallas kernels for 9% -> 8%
where the time goes in v6:
time: 123 us; the launch traced here: 121 us
  blocking collectives  49.6 us (40%)
  waiting for transfers between devices  27.7 us (23%)
  starting transfers between devices  17.1 us (14%)
  Pallas kernels  16.6 us (13%)
  other arithmetic  8.29 us (7%)
    ppermute x12, waiting for transfers between devices, partner(): return lax.ppermute(block, AXES, pairs)  27.7 us
    all_to_all x1, blocking collectives, per_device(): across_z = lax.all_to_all(packed, 'z', 0, 0, tiled=True).reshape(group, -1)  19.2 us
    all_to_all x1, blocking collectives, spread(): return lax.all_to_all(copies, axes, 0, 0, tiled=True)  18.2 us
    ppermute x12, starting transfers between devices, partner(): return lax.ppermute(block, AXES, pairs)  17.1 us
    all_to_all x1, blocking collectives, per_device(): pieces = lax.all_to_all(summed, 'z', 0, 0, tiled=True)  12.2 us
    concatenate x1, other arithmetic, per_device(): weights = jnp.concatenate([head_weight, other_weight], axis=0)  6.89 us
    pallas_call x1, Pallas kernels, product(): pl.pallas_call(product_kernel, out_shape=jax.ShapeDtypeStruct((entries, w...  5.83 us
    pallas_call x1, Pallas kernels, gradients(): pl.pallas_call(grad_kernel, out_shape=(jax.ShapeDtypeStruct((rows, width)...  3.91 us
  transfers between devices with their start and end apart: 15, of which 11 were waited for; matrix products, arithmetic and copies ran while one was open for 7% of the time, Pallas kernels for 8%

profile of v6, /device:TPU:24, one launch (start us, length us, event | category | flops | bytes accessed | tf_op | source)
XLA Modules:
  0.0 121.1 jit_solution(10722526883292458471)
XLA Ops:
  0.7 1.6 %pack.1 = bf16[8,2,5504]{2,1,0:T(2,128)(2,1)} custom-call(f32[2]{0:T(128)} %weight_ref.1, bf16[2,5120]{1,0:T(2,128)(2,1)} %hidden_ref, s32[2,64]{1,0:T(2,128)} %ids_ref.1, f32[2,64]{1,0:T(2,128)} %probs_ref.1), custom_call_target="tpu_custom_call" | custom-call | tf_op jit(solution)/shard_map/pack/pack/pallas_call | solution.py:107
  2.3 19.2 %all_to_all.15 = bf16[8,2,5504]{2,1,0:T(2,128)(2,1)S(1)} all-to-all(bf16[8,2,5504]{2,1,0:T(2,128)(2,1)} %pack.1), channel_id=1, replica_groups=mesh['y'=4,'z'=8,'x'=4,'core'=2] {'z'}, dimensions={0} | all-to-all | bytes 352256 | tf_op jit(solution)/shard_map/gather/all_to_all | solution.py:330
  21.5 3.1 %collective-permute-start = (bf16[16,5504]{1,0:T(8,128)(2,1)S(1)}, bf16[16,5504]{1,0:T(8,128)(2,1)S(1)}, u32[]{:S(2)}, u32[]{:S(2)}) collective-permute-start(bf16[16,5504]{1,0:T(8,128)(2,1)S(1)} %reshape.29), channel_id=1, source_target_pairs={{0,4},{1,129},{2,6},{3,131},{4,0},{5,133},{6,2},{7,135},{8,12},{9,... | collective-permute-start | bytes 528392 | tf_op jit(solution)/shard_map/gather/ppermute | solution.py:31
  25.9 2.6 %collective-permute-done = bf16[16,5504]{1,0:T(8,128)(2,1)S(1)} collective-permute-done((bf16[16,5504]{1,0:T(8,128)(2,1)S(1)}, bf16[16,5504]{1,0:T(8,128)(2,1)S(1)}, u32[]{:S(2)}, u32[]{:S(2)}) %collective-permute-start) | collective-permute-done | bytes 176160 | tf_op jit(solution)/shard_map/gather/ppermute | solution.py:31
  28.6 2.0 %collective-permute-done.1 = bf16[16,5504]{1,0:T(8,128)(2,1)S(1)} collective-permute-done((bf16[16,5504]{1,0:T(8,128)(2,1)S(1)}, bf16[16,5504]{1,0:T(8,128)(2,1)S(1)}, u32[]{:S(2)}, u32[]{:S(2)}) %collective-permute-start.1) | collective-permute-done | bytes 176160 | tf_op jit(solution)/shard_map/gather/ppermute | solution.py:31
  30.6 1.3 %collective-permute-done.2 = bf16[16,5504]{1,0:T(8,128)(2,1)S(1)} collective-permute-done((bf16[16,5504]{1,0:T(8,128)(2,1)S(1)}, bf16[16,5504]{1,0:T(8,128)(2,1)S(1)}, u32[]{:S(2)}, u32[]{:S(2)}) %collective-permute-start.2) | collective-permute-done | bytes 176160 | tf_op jit(solution)/shard_map/gather/ppermute | solution.py:31
  33.2 2.9 %collective-permute-start.6 = (bf16[64,5504]{1,0:T(8,128)(2,1)S(1)}, bf16[64,5504]{1,0:T(8,128)(2,1)S(1)}, u32[]{:S(2)}, u32[]{:S(2)}) collective-permute-start(bf16[64,5504]{1,0:T(8,128)(2,1)S(1)} %bitcast.46), channel_id=1, source_target_pairs={{0,192},{1,7},{2,194},{3,5},{4,196},{5,3},{6,198},{7,1},{8,200},{9... | collective-permute-start | bytes 2113544 | tf_op jit(solution)/shard_map/gather/ppermute | solution.py:31
  36.1 6.9 %pad_maximum_fusion.weights_ref = bf16[1184,5120]{1,0:T(8,128)(2,1)S(1)} fusion(bf16[592,5120]{1,0:T(8,128)(2,1)} %collective-permute-done.3, bf16[592,5120]{1,0:T(8,128)(2,1)} %param.6), kind=kLoop, calls=%fused_computation | loop fusion | flops 24248320 | bytes 24248320 | tf_op jit(solution)/shard_map/gather/concatenate | solution.py:332
  43.3 1.4 %collective-permute-done.4 = bf16[64,5504]{1,0:T(8,128)(2,1)S(1)} collective-permute-done((bf16[64,5504]{1,0:T(8,128)(2,1)S(1)}, bf16[64,5504]{1,0:T(8,128)(2,1)S(1)}, u32[]{:S(2)}, u32[]{:S(2)}) %collective-permute-start.4) | collective-permute-done | bytes 704544 | tf_op jit(solution)/shard_map/gather/ppermute | solution.py:31
  44.8 5.0 %collective-permute-done.5 = bf16[64,5504]{1,0:T(8,128)(2,1)S(1)} collective-permute-done((bf16[64,5504]{1,0:T(8,128)(2,1)S(1)}, bf16[64,5504]{1,0:T(8,128)(2,1)S(1)}, u32[]{:S(2)}, u32[]{:S(2)}) %collective-permute-start.5) | collective-permute-done | bytes 704544 | tf_op jit(solution)/shard_map/gather/ppermute | solution.py:31
  49.8 2.3 %collective-permute-done.6 = bf16[64,5504]{1,0:T(8,128)(2,1)S(1)} collective-permute-done((bf16[64,5504]{1,0:T(8,128)(2,1)S(1)}, bf16[64,5504]{1,0:T(8,128)(2,1)S(1)}, u32[]{:S(2)}, u32[]{:S(2)}) %collective-permute-start.6) | collective-permute-done | bytes 704544 | tf_op jit(solution)/shard_map/gather/ppermute | solution.py:31
  52.2 1.6 %target.1.target_ref = f32[1184,256]{1,0:T(8,128)S(1)} custom-call(s32[2]{0:T(128)S(1)} %pad_add_fusion.first_ref, bf16[256,5504]{1,0:T(8,128)(2,1)S(1)} %bitcast.37, bf16[256,5504]{1,0:T(8,128)(2,1)S(1)} %bitcast.38), custom_call_target="tpu_custom_call" | custom-call | flops 10000000 | bytes 4000000 | tf_op jit(solution)/shard_map/target/target/pallas_call | solution.py:162
  53.9 3.6 %exponents.1 = (f32[1184,256]{1,0:T(8,128)S(1)}, f32[4,128]{1,0:T(4,128)S(1)}) custom-call(bf16[256,5504]{1,0:T(8,128)(2,1)S(1)} %bitcast.39, bf16[1184,5120]{1,0:T(8,128)(2,1)S(1)} %pad_maximum_fusion.weights_ref), custom_call_target="tpu_custom_call" | custom-call | flops 3103784960 | bytes 12124160 | tf_op jit(solution)/shard_map/logits/exponents/pallas_call | solution.py:206
  57.6 18.2 %all_to_all.16.stats_ref = f32[128,4,128]{2,1,0:T(4,128)S(1)} all-to-all(f32[128,4,128]{2,1,0:T(4,128)S(1)} %broadcast_in_dim.42), channel_id=1, replica_groups=mesh['y'=4,'z'=8,'x'=4,'core'=2] {'y','z','x'}, dimensions={0} | all-to-all | bytes 524288 | tf_op jit(solution)/shard_map/stats/all_to_all | solution.py:20
  75.8 3.9 %gradients.1 = (bf16[256,5120]{1,0:T(8,128)(2,1)S(1)}, bf16[592,256]{1,0:T(8,128)(2,1)S(1)}, bf16[592,256]{1,0:T(8,128)(2,1)S(1)}) custom-call(f32[128,4,128]{2,1,0:T(4,128)S(1)} %all_to_all.16.stats_ref, f32[4,128]{1,0:T(4,128)S(1)} %get-tuple-element.42.local_ref, bf16[256,5504]{1,0:T(8,128)(2,1)S(1)} %bitcast.41, ...), custom_call_target="tpu_custom_call" | custom-call | flops 3103784960 | bytes 12124160 | tf_op jit(solution)/shard_map/grads/gradients/pallas_call | solution.py:259
  79.9 2.3 %collective-permute-start.9 = (bf16[64,5120]{1,0:T(8,128)(2,1)S(1)}, bf16[64,5120]{1,0:T(8,128)(2,1)S(1)}, u32[]{:S(2)}, u32[]{:S(2)}) collective-permute-start(bf16[64,5120]{1,0:T(8,128)(2,1)S(1)} %get-tuple-element.54), channel_id=1, source_target_pairs={{0,128},{1,5},{2,130},{3,7},{4,132},{5,1},{6,134},{7,3},{8,136},{9... | collective-permute-start | bytes 1966088 | tf_op jit(solution)/shard_map/scatter/ppermute | solution.py:31
  84.4 5.8 %product.1 = bf16[592,5120]{1,0:T(8,128)(2,1)} custom-call(bf16[592,256]{1,0:T(8,128)(2,1)S(1)} %get-tuple-element.47.own_grad_ref, bf16[592,256]{1,0:T(8,128)(2,1)S(1)} %collective-permute-done.7.other_grad_ref, bf16[256,5504]{1,0:T(8,128)(2,1)S(1)} %bitcast.42, bf16[256,5504]{1,0:T(8,128)(2,1)S(1)} %collective-permute-done.8.other_ref), custom_call_target="tpu_custom_call" | custom-call | flops 3103784960 | bytes 11304960 | tf_op jit(solution)/shard_map/grad_weight/product/pallas_call | solution.py:289
  90.3 1.9 %collective-permute-done.9 = bf16[64,5120]{1,0:T(8,128)(2,1)S(1)} collective-permute-done((bf16[64,5120]{1,0:T(8,128)(2,1)S(1)}, bf16[64,5120]{1,0:T(8,128)(2,1)S(1)}, u32[]{:S(2)}, u32[]{:S(2)}) %collective-permute-start.9) | collective-permute-done | bytes 655392 | tf_op jit(solution)/shard_map/scatter/ppermute | solution.py:31
  92.3 6.8 %collective-permute-done.10 = bf16[64,5120]{1,0:T(8,128)(2,1)S(1)} collective-permute-done((bf16[64,5120]{1,0:T(8,128)(2,1)S(1)}, bf16[64,5120]{1,0:T(8,128)(2,1)S(1)}, u32[]{:S(2)}, u32[]{:S(2)}) %collective-permute-start.10) | collective-permute-done | bytes 655392 | tf_op jit(solution)/shard_map/scatter/ppermute | solution.py:31
  99.4 1.5 %collective-permute-start.12 = (bf16[16,5120]{1,0:T(8,128)(2,1)S(1)}, bf16[16,5120]{1,0:T(8,128)(2,1)S(1)}, u32[]{:S(2)}, u32[]{:S(2)}) collective-permute-start(bf16[16,5120]{1,0:T(8,128)(2,1)S(1)} %get-tuple-element.58), channel_id=1, source_target_pairs={{0,4},{1,129},{2,6},{3,131},{4,0},{5,133},{6,2},{7,135},{8,12},{9,... | collective-permute-start | bytes 491528 | tf_op jit(solution)/shard_map/scatter/ppermute | solution.py:31
  101.5 2.1 %collective-permute-start.14 = (bf16[16,5120]{1,0:T(8,128)(2,1)S(1)}, bf16[16,5120]{1,0:T(8,128)(2,1)S(1)}, u32[]{:S(2)}, u32[]{:S(2)}) collective-permute-start(bf16[16,5120]{1,0:T(8,128)(2,1)S(1)} %get-tuple-element.56), channel_id=1, source_target_pairs={{0,6},{1,193},{2,4},{3,195},{4,2},{5,197},{6,0},{7,199},{8,14},{9,... | collective-permute-start | bytes 491528 | tf_op jit(solution)/shard_map/scatter/ppermute | solution.py:31
  103.6 2.7 %collective-permute-done.12 = bf16[16,5120]{1,0:T(8,128)(2,1)S(1)} collective-permute-done((bf16[16,5120]{1,0:T(8,128)(2,1)S(1)}, bf16[16,5120]{1,0:T(8,128)(2,1)S(1)}, u32[]{:S(2)}, u32[]{:S(2)}) %collective-permute-start.12) | collective-permute-done | bytes 163872 | tf_op jit(solution)/shard_map/scatter/ppermute | solution.py:31
  106.5 1.5 %collective-permute-done.14 = bf16[16,5120]{1,0:T(8,128)(2,1)S(1)} collective-permute-done((bf16[16,5120]{1,0:T(8,128)(2,1)S(1)}, bf16[16,5120]{1,0:T(8,128)(2,1)S(1)}, u32[]{:S(2)}, u32[]{:S(2)}) %collective-permute-start.14) | collective-permute-done | bytes 163872 | tf_op jit(solution)/shard_map/scatter/ppermute | solution.py:31
  108.2 12.2 %all_to_all.17 = bf16[8,2,5120]{2,1,0:T(2,128)(2,1)S(1)} all-to-all(bf16[8,2,5120]{2,1,0:T(2,128)(2,1)S(1)} %reshape.34), channel_id=1, replica_groups=mesh['y'=4,'z'=8,'x'=4,'core'=2] {'z'}, dimensions={0} | all-to-all | bytes 327680 | tf_op jit(solution)/shard_map/scatter/all_to_all | solution.py:365
  (40 shorter events, 7.7 us)
Async XLA Ops:
  2.3 33.8 %collective-permute-start.3 = (bf16[592,5120]{1,0:T(8,128)(2,1)}, bf16[592,5120]{1,0:T(8,128)(2,1)}, u32[]{:S(2)}, u32[]{:S(2)}) collective-permute-start(bf16[592,5120]{1,0:T(8,128)(2,1)} %param.6), channel_id=1, source_target_pairs={{0,1},{1,0},{2,3},{3,2},{4,5},{5,4},{6,7},{7,6},{8,9},{9,8},{10,11... | collective-permute-start | bytes 18186248 | tf_op jit(solution)/shard_map/pack/ppermute | solution.py:327
  21.5 7.0 %collective-permute-start = (bf16[16,5504]{1,0:T(8,128)(2,1)S(1)}, bf16[16,5504]{1,0:T(8,128)(2,1)S(1)}, u32[]{:S(2)}, u32[]{:S(2)}) collective-permute-start(bf16[16,5504]{1,0:T(8,128)(2,1)S(1)} %reshape.29), channel_id=1, source_target_pairs={{0,4},{1,129},{2,6},{3,131},{4,0},{5,133},{6,2},{7,135},{8,12},{9,... | collective-permute-start | bytes 528392 | tf_op jit(solution)/shard_map/gather/ppermute | solution.py:31
  24.6 5.9 %collective-permute-start.1 = (bf16[16,5504]{1,0:T(8,128)(2,1)S(1)}, bf16[16,5504]{1,0:T(8,128)(2,1)S(1)}, u32[]{:S(2)}, u32[]{:S(2)}) collective-permute-start(bf16[16,5504]{1,0:T(8,128)(2,1)S(1)} %reshape.29), channel_id=1, source_target_pairs={{0,2},{1,65},{2,0},{3,67},{4,6},{5,69},{6,4},{7,71},{8,10},{9,73},... | collective-permute-start | bytes 528392 | tf_op jit(solution)/shard_map/gather/ppermute | solution.py:31
  25.2 6.7 %collective-permute-start.2 = (bf16[16,5504]{1,0:T(8,128)(2,1)S(1)}, bf16[16,5504]{1,0:T(8,128)(2,1)S(1)}, u32[]{:S(2)}, u32[]{:S(2)}) collective-permute-start(bf16[16,5504]{1,0:T(8,128)(2,1)S(1)} %reshape.29), channel_id=1, source_target_pairs={{0,6},{1,193},{2,4},{3,195},{4,2},{5,197},{6,0},{7,199},{8,14},{9,... | collective-permute-start | bytes 528392 | tf_op jit(solution)/shard_map/gather/ppermute | solution.py:31
  31.9 12.8 %collective-permute-start.4 = (bf16[64,5504]{1,0:T(8,128)(2,1)S(1)}, bf16[64,5504]{1,0:T(8,128)(2,1)S(1)}, u32[]{:S(2)}, u32[]{:S(2)}) collective-permute-start(bf16[64,5504]{1,0:T(8,128)(2,1)S(1)} %bitcast.44), channel_id=1, source_target_pairs={{0,128},{1,5},{2,130},{3,7},{4,132},{5,1},{6,134},{7,3},{8,136},{9... | collective-permute-start | bytes 2113544 | tf_op jit(solution)/shard_map/gather/ppermute | solution.py:31
  33.2 16.5 %collective-permute-start.5 = (bf16[64,5504]{1,0:T(8,128)(2,1)S(1)}, bf16[64,5504]{1,0:T(8,128)(2,1)S(1)}, u32[]{:S(2)}, u32[]{:S(2)}) collective-permute-start(bf16[64,5504]{1,0:T(8,128)(2,1)S(1)} %bitcast.45), channel_id=1, source_target_pairs={{0,64},{1,3},{2,66},{3,1},{4,68},{5,7},{6,70},{7,5},{8,72},{9,11},... | collective-permute-start | bytes 2113544 | tf_op jit(solution)/shard_map/gather/ppermute | solution.py:31
  33.2 18.9 %collective-permute-start.6 = (bf16[64,5504]{1,0:T(8,128)(2,1)S(1)}, bf16[64,5504]{1,0:T(8,128)(2,1)S(1)}, u32[]{:S(2)}, u32[]{:S(2)}) collective-permute-start(bf16[64,5504]{1,0:T(8,128)(2,1)S(1)} %bitcast.46), channel_id=1, source_target_pairs={{0,192},{1,7},{2,194},{3,5},{4,196},{5,3},{6,198},{7,1},{8,200},{9... | collective-permute-start | bytes 2113544 | tf_op jit(solution)/shard_map/gather/ppermute | solution.py:31
  75.8 8.6 %collective-permute-start.8 = (bf16[256,5504]{1,0:T(8,128)(2,1)S(1)}, bf16[256,5504]{1,0:T(8,128)(2,1)S(1)}, u32[]{:S(2)}, u32[]{:S(2)}) collective-permute-start(bf16[256,5504]{1,0:T(8,128)(2,1)S(1)} %bitcast.40), channel_id=1, source_target_pairs={{0,1},{1,0},{2,3},{3,2},{4,5},{5,4},{6,7},{7,6},{8,9},{9,8},{10,11... | collective-permute-start | bytes 8454152 | tf_op jit(solution)/shard_map/stats/ppermute | solution.py:346
  79.9 12.3 %collective-permute-start.9 = (bf16[64,5120]{1,0:T(8,128)(2,1)S(1)}, bf16[64,5120]{1,0:T(8,128)(2,1)S(1)}, u32[]{:S(2)}, u32[]{:S(2)}) collective-permute-start(bf16[64,5120]{1,0:T(8,128)(2,1)S(1)} %get-tuple-element.54), channel_id=1, source_target_pairs={{0,128},{1,5},{2,130},{3,7},{4,132},{5,1},{6,134},{7,3},{8,136},{9... | collective-permute-start | bytes 1966088 | tf_op jit(solution)/shard_map/scatter/ppermute | solution.py:31
  82.3 2.1 %collective-permute-start.7 = (bf16[592,256]{1,0:T(8,128)(2,1)S(1)}, bf16[592,256]{1,0:T(8,128)(2,1)S(1)}, u32[]{:S(2)}, u32[]{:S(2)}) collective-permute-start(bf16[592,256]{1,0:T(8,128)(2,1)S(1)} %get-tuple-element.48), channel_id=1, source_target_pairs={{0,1},{1,0},{2,3},{3,2},{4,5},{5,4},{6,7},{7,6},{8,9},{9,8},{10,11... | collective-permute-start | bytes 909320 | tf_op jit(solution)/shard_map/grad_weight/ppermute | solution.py:357
  82.3 16.8 %collective-permute-start.10 = (bf16[64,5120]{1,0:T(8,128)(2,1)S(1)}, bf16[64,5120]{1,0:T(8,128)(2,1)S(1)}, u32[]{:S(2)}, u32[]{:S(2)}) collective-permute-start(bf16[64,5120]{1,0:T(8,128)(2,1)S(1)} %get-tuple-element.53), channel_id=1, source_target_pairs={{0,64},{1,3},{2,66},{3,1},{4,68},{5,7},{6,70},{7,5},{8,72},{9,11},... | collective-permute-start | bytes 1966088 | tf_op jit(solution)/shard_map/scatter/ppermute | solution.py:31
  83.4 15.7 %collective-permute-start.11 = (bf16[64,5120]{1,0:T(8,128)(2,1)S(1)}, bf16[64,5120]{1,0:T(8,128)(2,1)S(1)}, u32[]{:S(2)}, u32[]{:S(2)}) collective-permute-start(bf16[64,5120]{1,0:T(8,128)(2,1)S(1)} %get-tuple-element.52), channel_id=1, source_target_pairs={{0,192},{1,7},{2,194},{3,5},{4,196},{5,3},{6,198},{7,1},{8,200},{9... | collective-permute-start | bytes 1966088 | tf_op jit(solution)/shard_map/scatter/ppermute | solution.py:31
  99.4 6.9 %collective-permute-start.12 = (bf16[16,5120]{1,0:T(8,128)(2,1)S(1)}, bf16[16,5120]{1,0:T(8,128)(2,1)S(1)}, u32[]{:S(2)}, u32[]{:S(2)}) collective-permute-start(bf16[16,5120]{1,0:T(8,128)(2,1)S(1)} %get-tuple-element.58), channel_id=1, source_target_pairs={{0,4},{1,129},{2,6},{3,131},{4,0},{5,133},{6,2},{7,135},{8,12},{9,... | collective-permute-start | bytes 491528 | tf_op jit(solution)/shard_map/scatter/ppermute | solution.py:31
  100.9 5.6 %collective-permute-start.13 = (bf16[16,5120]{1,0:T(8,128)(2,1)S(1)}, bf16[16,5120]{1,0:T(8,128)(2,1)S(1)}, u32[]{:S(2)}, u32[]{:S(2)}) collective-permute-start(bf16[16,5120]{1,0:T(8,128)(2,1)S(1)} %get-tuple-element.57), channel_id=1, source_target_pairs={{0,2},{1,65},{2,0},{3,67},{4,6},{5,69},{6,4},{7,71},{8,10},{9,73},... | collective-permute-start | bytes 491528 | tf_op jit(solution)/shard_map/scatter/ppermute | solution.py:31
  101.5 6.6 %collective-permute-start.14 = (bf16[16,5120]{1,0:T(8,128)(2,1)S(1)}, bf16[16,5120]{1,0:T(8,128)(2,1)S(1)}, u32[]{:S(2)}, u32[]{:S(2)}) collective-permute-start(bf16[16,5120]{1,0:T(8,128)(2,1)S(1)} %get-tuple-element.56), channel_id=1, source_target_pairs={{0,6},{1,193},{2,4},{3,195},{4,2},{5,197},{6,0},{7,199},{8,14},{9,... | collective-permute-start | bytes 491528 | tf_op jit(solution)/shard_map/scatter/ppermute | solution.py:31
